TPU v7x, 32 devices: a whole 2x2x4 slice. The times are simulated.
32 devices in a mesh: half: 2 (over core), dp: 4 (over z), row: 4 (over y, x).
Axes of the slice: x: 2, y: 2, z: 4, core: 2. Of those that a mesh axis runs over, the one named last changes fastest.
Arguments:
- features: bfloat16 [128, 4, 4, 1536], P(('half', 'dp'), None, None, 'row'), may hold values from -20 to 20
- noise: float32 [128, 20], P(('half', 'dp')), may hold values from -3 to 3
- labels: int32 [128], P(('half', 'dp')), may hold values from 0 to 999
- counted: int32 [128], P(('half', 'dp')), may hold values from 0 to 1, as said below
- disc_first: bfloat16 [27, 96], replicated, may hold values from -1.25 to 1.25
- disc_second: bfloat16 [864, 96], replicated, may hold values from -0.21875 to 0.21875
- disc_skip: bfloat16 [3, 96], replicated, may hold values from -3.5 to 3.5
- disc_head: float32 [96], replicated, may hold values from -0.15625 to 0.15625
- disc_table: float32 [1000, 96], replicated, may hold values from -0.15625 to 0.15625
- conv_first: float32 [13824, 768], P(('half', 'dp'), 'row'), may hold values from -0.0546875 to 0.0546875
- conv_second: float32 [6912, 768], P(('half', 'dp'), 'row'), may hold values from -0.078125 to 0.078125
- conv_skip: float32 [1536, 768], P(('half', 'dp'), 'row'), may hold values from -0.15625 to 0.15625
- momentum_first: float32 [13824, 768], P(('half', 'dp'), 'row')
- momentum_second: float32 [6912, 768], P(('half', 'dp'), 'row')
- momentum_skip: float32 [1536, 768], P(('half', 'dp'), 'row')
- class_table: float32 [1000, 128], replicated, may hold values from -1.2 to 1.2
- table_mean: float32 [1000, 128], replicated
- table_square: float32 [1000, 128], replicated
- norm_first: float32 [148, 2, 1536], P(None, None, 'row'), may hold values from -0.5 to 0.5
- first_mean: float32 [148, 2, 1536], P(None, None, 'row')
- first_square: float32 [148, 2, 1536], P(None, None, 'row')
- norm_second: float32 [148, 2, 768], P(None, None, 'row'), may hold values from -0.5 to 0.5
- second_mean: float32 [148, 2, 768], P(None, None, 'row')
- second_square: float32 [148, 2, 768], P(None, None, 'row')
- colour_conv: float32 [9, 768, 3], P(None, 'row'), may hold values from -0.078125 to 0.078125
- colour_mean: float32 [9, 768, 3], P(None, 'row')
- colour_square: float32 [9, 768, 3], P(None, 'row')
Outputs:
- loss_sum: float32 [], replicated
- fake_count: float32 [], replicated
- conv_first_new: float32 [13824, 768], P(('half', 'dp'), 'row')
- conv_second_new: float32 [6912, 768], P(('half', 'dp'), 'row')
- conv_skip_new: float32 [1536, 768], P(('half', 'dp'), 'row')
- momentum_first_new: float32 [13824, 768], P(('half', 'dp'), 'row')
- momentum_second_new: float32 [6912, 768], P(('half', 'dp'), 'row')
- momentum_skip_new: float32 [1536, 768], P(('half', 'dp'), 'row')
- class_table_new: float32 [1000, 128], replicated
- table_mean_new: float32 [1000, 128], replicated
- table_square_new: float32 [1000, 128], replicated
- norm_first_new: float32 [148, 2, 1536], P(None, None, 'row')
- first_mean_new: float32 [148, 2, 1536], P(None, None, 'row')
- first_square_new: float32 [148, 2, 1536], P(None, None, 'row')
- norm_second_new: float32 [148, 2, 768], P(None, None, 'row')
- second_mean_new: float32 [148, 2, 768], P(None, None, 'row')
- second_square_new: float32 [148, 2, 768], P(None, None, 'row')
- colour_conv_new: float32 [9, 768, 3], P(None, 'row')
- colour_mean_new: float32 [9, 768, 3], P(None, 'row')
- colour_square_new: float32 [9, 768, 3], P(None, 'row')
Inputs may be any that keep to these rules, and one draw needn't show every extreme that they name: `counted`: every image whose index is a multiple of 16 counts.
All inputs are finite; a program needn't handle non-finite values.
Results may differ from a plain program's by a relative error of at most 0.0085.
Values may be sent and summed in bfloat16 or wider, within the bound.
No kernel may reach another device: no remote copies, remote signals or barrier semaphores. Data moves between devices by JAX's collectives and lax.ppermute only.
A program may use at most 256 MiB of HBM per device.

v0:
```python
import math

import jax
import jax.numpy as jnp
from jax import lax
from jax.sharding import PartitionSpec as P

EMB = 128
NCLS = 1000
MICRO = 2
NS_ITERS = 5
STEP = 10


highest = lax.Precision.HIGHEST
BN_EPS = 1e-05
NEWTON_EPSILON = 1e-07
NS_COEF = (3.4445, -4.775, 2.0315)
MOMENTUM = 0.9
MUON_RATE = 0.03
DECAY = 0.01
BETA_ONE = 0.9
BETA_TWO = 0.95
ADAM_EPS = 1e-08
ADAM_RATE = 0.05
COLOUR_RATE = 0.01


def shortened(shard):

    def short(part):
        return part.astype(jnp.bfloat16) if part.dtype == jnp.float32 else part

    return jax.tree.map(short, shard)


def silu_slope(values):
    sigmoid_value = jax.nn.sigmoid(values)
    return sigmoid_value * (1.0 + values * (1.0 - sigmoid_value))


def patches_of(values):
    padded = jnp.pad(values, ((0, 0), (1, 1), (1, 1), (0, 0)))
    rows_in, cols_in = (values.shape[1], values.shape[2])
    return jnp.concatenate(
        [
            padded[:, row_shift : row_shift + rows_in, col_shift : col_shift + cols_in, :]
            for row_shift in range(3)
            for col_shift in range(3)
        ],
        axis=-1,
    )


def unpatch(patch_grad):
    channels = patch_grad.shape[-1] // 9
    rows_in, cols_in = (patch_grad.shape[1], patch_grad.shape[2])
    padded = jnp.zeros((patch_grad.shape[0], rows_in + 2, cols_in + 2, channels), jnp.float32)
    for tap_index in range(9):
        row_shift, col_shift = divmod(tap_index, 3)
        padded = padded.at[
            :, row_shift : row_shift + rows_in, col_shift : col_shift + cols_in, :
        ].add(patch_grad[..., tap_index * channels : (tap_index + 1) * channels])
    return padded[:, 1:-1, 1:-1, :]


def upsample(values):
    return jnp.repeat(jnp.repeat(values, 2, axis=1), 2, axis=2)


def pool_sum(values):
    shaped = values.reshape(
        values.shape[0], values.shape[1] // 2, 2, values.shape[2] // 2, 2, values.shape[3]
    )
    return jnp.sum(shaped, axis=(2, 4))


def matmul(left, right):
    return lax.dot_general(
        left, right, (((left.ndim - 1,), (0,)), ((), ())), preferred_element_type=jnp.float32
    )


def matmul_back(gradient, weight):
    return lax.dot_general(
        gradient,
        weight,
        (((gradient.ndim - 1,), (1,)), ((), ())),
        preferred_element_type=jnp.float32,
    )


def weight_grad(inputs, gradient):
    leading = tuple(range(inputs.ndim - 1))
    return lax.dot_general(
        inputs, gradient, ((leading, leading), ((), ())), preferred_element_type=jnp.float32
    )


def batch_stats(first_sum, second_sum):
    return lax.psum((first_sum, second_sum), ("half", "dp"))


def norm_forward(values, count_all):
    totals = batch_stats(jnp.sum(values, axis=(0, 1, 2)), jnp.sum(values * values, axis=(0, 1, 2)))
    centre = totals[0] / count_all
    spread = lax.rsqrt(totals[1] / count_all - centre * centre + BN_EPS)
    return ((values - centre) * spread, spread)


def norm_backward(grad_normed, normed, spread, count_all):
    totals = batch_stats(
        jnp.sum(grad_normed, axis=(0, 1, 2)), jnp.sum(grad_normed * normed, axis=(0, 1, 2))
    )
    return spread * (grad_normed - totals[0] / count_all - normed * (totals[1] / count_all))


def modulate(normed, mods):
    return normed * (1.0 + mods[:, 0])[:, None, None, :] + mods[:, 1][:, None, None, :]


def mods_backward(grad_pre, normed, mods):
    gains = jnp.sum(grad_pre * normed, axis=(1, 2))
    shifts = jnp.sum(grad_pre, axis=(1, 2))
    return (jnp.stack([gains, shifts], axis=1), grad_pre * (1.0 + mods[:, 0])[:, None, None, :])


def forward(inputs, conds, onehot, generator, discriminator, count_low):
    weight_one, weight_two, weight_skip, colour_flat, norm_first, norm_second = generator
    disc_first, disc_second, disc_skip, disc_head, disc_table = discriminator
    mods_one = jnp.einsum("bk,kgc->bgc", conds, norm_first, precision=highest)
    mods_two = jnp.einsum("bk,kgc->bgc", conds, norm_second, precision=highest)
    normed_one, spread_one = norm_forward(inputs.astype(jnp.float32), count_low)
    pre_one = modulate(normed_one, mods_one)
    acted_one = jax.nn.silu(pre_one).astype(jnp.bfloat16)
    full_one, full_inputs = (
        lax.all_gather(acted_one, "row", axis=3, tiled=True),
        lax.all_gather(inputs, "row", axis=3, tiled=True),
    )
    patch_one = patches_of(upsample(full_one))
    hidden = matmul(patch_one, weight_one)
    normed_two, spread_two = norm_forward(hidden, 4.0 * count_low)
    pre_two = modulate(normed_two, mods_two)
    acted_two = jax.nn.silu(pre_two).astype(jnp.bfloat16)
    full_two = lax.all_gather(acted_two, "row", axis=3, tiled=True)
    patch_two = patches_of(full_two)
    lifted = upsample(full_inputs)
    summed = matmul(patch_two, weight_two) + matmul(lifted, weight_skip)
    active = jax.nn.silu(summed).astype(jnp.bfloat16)
    patch_three = patches_of(active)
    picture_pre = lax.psum(matmul(patch_three, colour_flat), "row")
    shade = jnp.tanh(picture_pre)
    picture = shade.astype(jnp.bfloat16)
    front_pre = matmul(patches_of(picture), disc_first)
    front = jax.nn.silu(front_pre).astype(jnp.bfloat16)
    merged = 0.25 * pool_sum(matmul(patches_of(front), disc_second))
    merged = merged + jnp.dot(
        0.25 * pool_sum(picture.astype(jnp.float32)),
        disc_skip.astype(jnp.float32),
        precision=highest,
    )
    feature = jnp.sum(jax.nn.silu(merged), axis=(1, 2))
    class_disc = jnp.dot(onehot, disc_table, precision=highest)
    score = jnp.dot(feature, disc_head, precision=highest) + jnp.sum(feature * class_disc, axis=1)
    stored = (
        mods_one,
        mods_two,
        normed_one,
        pre_one,
        patch_one,
        normed_two,
        spread_two,
        pre_two,
        patch_two,
        lifted,
        summed,
        patch_three,
        shade,
        picture,
        front_pre,
        front,
        merged,
        class_disc,
    )
    return (stored, score)


def backward(stored, counted, conds, generator, discriminator, count_low):
    weight_one, weight_two, weight_skip, colour_flat, norm_first, norm_second = generator
    disc_first, disc_second, disc_skip, disc_head, disc_table = discriminator
    (
        mods_one,
        mods_two,
        normed_one,
        pre_one,
        patch_one,
        normed_two,
        spread_two,
        pre_two,
        patch_two,
        lifted,
        summed,
        patch_three,
        shade,
        picture,
        front_pre,
        front,
        merged,
        class_disc,
    ) = stored
    grad_score = -counted.astype(jnp.float32)
    grad_feature = grad_score[:, None] * (disc_head[None, :] + class_disc)
    grad_merged = (grad_feature[:, None, None, :] * silu_slope(merged)).astype(jnp.bfloat16)
    grad_pool = upsample(grad_merged) * jnp.bfloat16(0.25)
    grad_front = unpatch(matmul_back(grad_pool, disc_second))
    grad_front_pre = (grad_front * silu_slope(front_pre)).astype(jnp.bfloat16)
    grad_picture = unpatch(matmul_back(grad_front_pre, disc_first))
    grad_picture = grad_picture + 0.25 * upsample(matmul_back(grad_merged, disc_skip))
    grad_pre = (grad_picture * (1.0 - shade * shade)).astype(jnp.bfloat16)
    grad_colour = weight_grad(patch_three, grad_pre)
    grad_active = unpatch(matmul_back(grad_pre, colour_flat))
    grad_summed = (grad_active * silu_slope(summed)).astype(jnp.bfloat16)
    grad_two = weight_grad(patch_two, grad_summed)
    grad_skip = weight_grad(lifted, grad_summed)
    grad_full_two = unpatch(matmul_back(grad_summed, weight_two))
    grad_acted_two = lax.psum_scatter(
        grad_full_two.astype(jnp.bfloat16), "row", scatter_dimension=3, tiled=True
    ).astype(jnp.float32)
    grad_pre_two = grad_acted_two * silu_slope(pre_two)
    grad_mods_two, grad_normed_two = mods_backward(grad_pre_two, normed_two, mods_two)
    grad_hidden = norm_backward(grad_normed_two, normed_two, spread_two, 4.0 * count_low).astype(
        jnp.bfloat16
    )
    grad_one = weight_grad(patch_one, grad_hidden)
    grad_full_one = pool_sum(unpatch(matmul_back(grad_hidden, weight_one)))
    grad_acted_one = lax.psum_scatter(
        grad_full_one.astype(jnp.bfloat16), "row", scatter_dimension=3, tiled=True
    ).astype(jnp.float32)
    grad_pre_one = grad_acted_one * silu_slope(pre_one)
    grad_mods_one, unused_grad = mods_backward(grad_pre_one, normed_one, mods_one)
    grad_norm_one = jnp.einsum("bk,bgc->kgc", conds, grad_mods_one, precision=highest)
    grad_norm_two = jnp.einsum("bk,bgc->kgc", conds, grad_mods_two, precision=highest)
    grad_cond = jnp.einsum("bgc,kgc->bk", grad_mods_one, norm_first, precision=highest)
    grad_cond = grad_cond + jnp.einsum("bgc,kgc->bk", grad_mods_two, norm_second, precision=highest)
    return (
        grad_one,
        grad_two,
        grad_skip,
        grad_colour,
        grad_norm_one,
        grad_norm_two,
        grad_cond[:, :EMB],
    )


def gather_columns(first, second, third):
    return (
        lax.all_gather(shortened(first), "row", axis=1, tiled=True).astype(first.dtype),
        lax.all_gather(shortened(second), "row", axis=1, tiled=True).astype(second.dtype),
        lax.all_gather(shortened(third), "row", axis=1, tiled=True).astype(third.dtype),
    )


def gram_total(complete_blocks):
    gram_blocks = tuple(
        (
            jnp.einsum("kc,kd->cd", update_matrix, update_matrix, precision=highest)
            for update_matrix in complete_blocks
        )
    )
    shares = (
        lax.psum_scatter(gram_blocks[0], ("half", "dp"), scatter_dimension=0, tiled=True),
        lax.psum_scatter(gram_blocks[1], ("half", "dp"), scatter_dimension=0, tiled=True),
        lax.psum_scatter(gram_blocks[2], ("half", "dp"), scatter_dimension=0, tiled=True),
    )
    return (
        lax.all_gather(shares[0].astype(jnp.bfloat16), ("half", "dp"), axis=0, tiled=True).astype(
            jnp.float32
        ),
        lax.all_gather(shares[1].astype(jnp.bfloat16), ("half", "dp"), axis=0, tiled=True).astype(
            jnp.float32
        ),
        lax.all_gather(shares[2].astype(jnp.bfloat16), ("half", "dp"), axis=0, tiled=True).astype(
            jnp.float32
        ),
    )


def polynomial(gram_product):
    identity = jnp.eye(gram_product.shape[0], dtype=jnp.float32)
    return (
        NS_COEF[0] * identity
        + NS_COEF[1] * gram_product
        + NS_COEF[2] * jnp.dot(gram_product, gram_product, precision=highest)
    )


def orthogonal(first, second, third):
    own_width = first.shape[1]
    offset = lax.axis_index("row") * own_width
    owned_blocks = (first, second, third)
    complete_blocks = gather_columns(first, second, third)
    gram_blocks = gram_total(complete_blocks)
    norm_scales = tuple(
        (lax.rsqrt(jnp.trace(gram_product) + NEWTON_EPSILON) for gram_product in gram_blocks)
    )
    complete_blocks = tuple(
        (
            update_matrix * norm_scale
            for update_matrix, norm_scale in zip(complete_blocks, norm_scales)
        )
    )
    owned_blocks = tuple(
        (update_matrix * norm_scale for update_matrix, norm_scale in zip(owned_blocks, norm_scales))
    )
    gram_blocks = tuple(
        (
            gram_product * norm_scale * norm_scale
            for gram_product, norm_scale in zip(gram_blocks, norm_scales)
        )
    )
    for iteration in range(NS_ITERS):
        if iteration > 0:
            complete_blocks = gather_columns(owned_blocks[0], owned_blocks[1], owned_blocks[2])
            gram_blocks = gram_total(complete_blocks)
        mappings = tuple((polynomial(gram_product) for gram_product in gram_blocks))
        owned_blocks = tuple(
            (
                jnp.dot(
                    update_matrix,
                    lax.dynamic_slice_in_dim(mapping, offset, own_width, 1),
                    precision=highest,
                )
                for update_matrix, mapping in zip(complete_blocks, mappings)
            )
        )
    return owned_blocks


def adam_update(weight, gradient, mean_old, square_old, rate):
    mean_new = BETA_ONE * mean_old + (1.0 - BETA_ONE) * gradient
    square_new = BETA_TWO * square_old + (1.0 - BETA_TWO) * gradient * gradient
    ratio = (
        mean_new
        / (1.0 - BETA_ONE**STEP)
        / (jnp.sqrt(square_new / (1.0 - BETA_TWO**STEP)) + ADAM_EPS)
    )
    return (weight - rate * (ratio + DECAY * weight), mean_new, square_new)


def per_device(
    features,
    noise,
    labels,
    counted,
    disc_first,
    disc_second,
    disc_skip,
    disc_head,
    disc_table,
    conv_first,
    conv_second,
    conv_skip,
    momentum_first,
    momentum_second,
    momentum_skip,
    class_table,
    table_mean,
    table_square,
    norm_first,
    first_mean,
    first_square,
    norm_second,
    second_mean,
    second_square,
    colour_conv,
    colour_mean,
    colour_square,
):
    groups = lax.axis_size("half") * lax.axis_size("dp")
    weight_one, weight_two, weight_skip = (
        lax.all_gather(conv_first.astype(jnp.bfloat16), ("half", "dp"), axis=0, tiled=True),
        lax.all_gather(conv_second.astype(jnp.bfloat16), ("half", "dp"), axis=0, tiled=True),
        lax.all_gather(conv_skip.astype(jnp.bfloat16), ("half", "dp"), axis=0, tiled=True),
    )
    colour_flat = colour_conv.reshape(-1, 3).astype(jnp.bfloat16)
    generator = (weight_one, weight_two, weight_skip, colour_flat, norm_first, norm_second)
    discriminator = (disc_first, disc_second, disc_skip, disc_head, disc_table)
    onehot_all = (labels[:, None] == jnp.arange(NCLS)[None, :]).astype(jnp.float32)
    conds_all = jnp.concatenate(
        [jnp.dot(onehot_all, class_table, precision=highest), noise], axis=1
    )
    micro_rows = features.shape[0] // MICRO
    count_low = float(micro_rows * 16 * groups)
    sums = None
    cond_parts = []
    loss_part = jnp.zeros((), jnp.float32)
    for micro_index in range(MICRO):
        rows_span = slice(micro_index * micro_rows, (micro_index + 1) * micro_rows)
        stored, score = forward(
            features[rows_span],
            conds_all[rows_span],
            onehot_all[rows_span],
            generator,
            discriminator,
            count_low,
        )
        loss_part = loss_part - jnp.sum(counted[rows_span].astype(jnp.float32) * score)
        grads = backward(
            stored, counted[rows_span], conds_all[rows_span], generator, discriminator, count_low
        )
        cond_parts.append(grads[6])
        sums = (
            grads[:6]
            if sums is None
            else tuple((older + newer for older, newer in zip(sums, grads[:6])))
        )
    cond_back = lax.psum(jnp.concatenate(cond_parts, axis=0), "row")
    grad_table = jnp.einsum("bn,bk->nk", onehot_all, cond_back, precision=highest)
    count_part = jnp.sum(counted).astype(jnp.float32)
    g_norm_one, g_norm_two, g_colour, g_table, loss_sum, fake_count = lax.psum(
        (sums[4], sums[5], sums[3].reshape(colour_conv.shape), grad_table, loss_part, count_part),
        ("half", "dp"),
    )
    inverse = 1.0 / fake_count
    muon_grads = (
        lax.psum_scatter(sums[0], ("half", "dp"), scatter_dimension=0, tiled=True),
        lax.psum_scatter(sums[1], ("half", "dp"), scatter_dimension=0, tiled=True),
        lax.psum_scatter(sums[2], ("half", "dp"), scatter_dimension=0, tiled=True),
    )
    masters = (conv_first, conv_second, conv_skip)
    moments_new = tuple(
        (
            MOMENTUM * moment + gradient * inverse
            for moment, gradient in zip(
                (momentum_first, momentum_second, momentum_skip), muon_grads
            )
        )
    )
    directions = orthogonal(moments_new[0], moments_new[1], moments_new[2])
    weights_new = []
    for master, direction in zip(masters, directions):
        factor = 0.2 * math.sqrt(
            max(master.shape[0] * groups, master.shape[1] * lax.axis_size("row"))
        )
        weights_new.append(master - MUON_RATE * (factor * direction + DECAY * master))
    table_new = adam_update(class_table, g_table * inverse, table_mean, table_square, ADAM_RATE)
    first_new = adam_update(norm_first, g_norm_one * inverse, first_mean, first_square, ADAM_RATE)
    second_new = adam_update(
        norm_second, g_norm_two * inverse, second_mean, second_square, ADAM_RATE
    )
    colour_new = adam_update(
        colour_conv, g_colour * inverse, colour_mean, colour_square, COLOUR_RATE
    )
    return (
        loss_sum,
        fake_count,
        weights_new[0],
        weights_new[1],
        weights_new[2],
        moments_new[0],
        moments_new[1],
        moments_new[2],
        table_new[0],
        table_new[1],
        table_new[2],
        first_new[0],
        first_new[1],
        first_new[2],
        second_new[0],
        second_new[1],
        second_new[2],
        colour_new[0],
        colour_new[1],
        colour_new[2],
    )


def solution(mesh):
    placed = (
        P(("half", "dp"), None, None, "row"),
        P(("half", "dp"), None),
        P(("half", "dp")),
        P(("half", "dp")),
        P(),
        P(),
        P(),
        P(),
        P(),
        P(("half", "dp"), "row"),
        P(("half", "dp"), "row"),
        P(("half", "dp"), "row"),
        P(("half", "dp"), "row"),
        P(("half", "dp"), "row"),
        P(("half", "dp"), "row"),
        P(),
        P(),
        P(),
        P(None, None, "row"),
        P(None, None, "row"),
        P(None, None, "row"),
        P(None, None, "row"),
        P(None, None, "row"),
        P(None, None, "row"),
        P(None, "row", None),
        P(None, "row", None),
        P(None, "row", None),
    )
    return jax.shard_map(
        per_device,
        mesh=mesh,
        in_specs=placed,
        out_specs=(
            P(),
            P(),
            P(("half", "dp"), "row"),
            P(("half", "dp"), "row"),
            P(("half", "dp"), "row"),
            P(("half", "dp"), "row"),
            P(("half", "dp"), "row"),
            P(("half", "dp"), "row"),
            P(),
            P(),
            P(),
            P(None, None, "row"),
            P(None, None, "row"),
            P(None, None, "row"),
            P(None, None, "row"),
            P(None, None, "row"),
            P(None, None, "row"),
            P(None, "row", None),
            P(None, "row", None),
            P(None, "row", None),
        ),
        check_vma=False,
    )
```

profile of v0, /device:TPU:0, one launch (start us, length us, event | category | flops | bytes accessed | tf_op | source)
XLA Modules:
  0.0 3663.2 jit_solution(6207366849698638542)
XLA Ops:
  71.1 35.7 all_gather.122
  173.3 109.1 %all_gather.119 = bf16[8,8,8,768]{2,1,0,3:T(8,128)(2,1)} all-gather(bf16[8,8,8,192]{2,1,0,3:T(8,128)(2,1)S(1)} %copy.234), channel_id=1, replica_groups=mesh['half'=2,'dp'=4,'row'=4] {'row'}, dimensions={3}, use_global_device_ids=true | all-gather | bytes 983040 | tf_op jit(solution)/shard_map/all_gather | solution.py:145
  549.1 19.4 reshape.3501
  568.5 23.0 reduce-scatter.67.cloned.1.call-done
  643.9 21.2 scatter-add.421
  671.9 21.2 scatter-add.424
  702.9 19.7 scatter-add.426
  727.4 19.7 scatter-add.429
  756.9 19.4 scatter-add.431
  781.1 19.6 scatter-add.434
  827.4 24.3 reshape.3511
  960.2 107.2 %all_gather.124 = bf16[8,8,8,768]{2,1,0,3:T(8,128)(2,1)} all-gather(bf16[8,8,8,192]{2,1,0,3:T(8,128)(2,1)S(1)} %copy.253), channel_id=1, replica_groups=mesh['half'=2,'dp'=4,'row'=4] {'row'}, dimensions={3}, use_global_device_ids=true | all-gather | bytes 983040 | tf_op jit(solution)/shard_map/all_gather | solution.py:145
  1389.7 37.7 %all-reduce.20 = (f32[]{:T(128)}, f32[]{:T(128)}, f32[192]{0:T(256)S(1)}, f32[192]{0:T(256)S(1)}, f32[9,192,3]{1,0,2:T(8,128)}) all-reduce(f32[]{:T(128)S(6)} %sub.142, f32[]{:T(128)S(6)} %convert_element_type.322, f32[192]{0:T(256)S(1)} %get-tuple-element.1183, ...), channel_id=1, replica_groups=mesh['half'=2,'dp'=4,'row'=4] {'half','dp'}, use_global_device_ids=true, to_apply=%region_28.29 | all-reduce | flops 5570 | bytes 44560 | tf_op jit(solution)/shard_map/psum | solution.py:421
  1468.8 54.5 %reduce-scatter.73.cloned.1.call-done = f32[864,192]{1,0:T(8,128)} async-done(((f32[6912,192]{1,0:T(8,128)}), f32[864,192]{1,0:T(8,128)}) %reduce-scatter.73.cloned.1.call-update) | async-done | bytes 663568
  1525.9 275.6 %reduce-scatter.71.cloned.1.call-done = f32[1728,192]{1,0:T(8,128)} async-done(((f32[13824,192]{1,0:T(8,128)}), f32[1728,192]{1,0:T(8,128)}) %reduce-scatter.71.cloned.1.call-update) | async-done | bytes 1327120
  1806.4 28.1 all-gather.50.cloned.1.call-done
  1839.4 38.3 %all-gather.30.cloned.1.call-done = bf16[1728,768]{0,1:T(8,128)(2,1)} async-done(((bf16[1728,192]{0,1:T(8,128)(2,1)}), bf16[1728,768]{0,1:T(8,128)(2,1)}) %all-gather.30.cloned.1.call-update) | async-done | bytes 2654224 | tf_op jit(solution)/shard_map/all_gather | solution.py:258
  1884.1 49.8 %reduce-scatter.47.cloned.1.call-done = f32[96,768]{1,0:T(8,128)} async-done(((f32[768,768]{1,0:T(8,128)}), f32[96,768]{1,0:T(8,128)}) %reduce-scatter.47.cloned.1.call-update) | async-done | bytes 294928 | tf_op jit(solution)/shard_map/reduce_scatter | solution.py:273
  1935.7 53.8 %reduce-scatter.37.cloned.1.call-done = f32[96,768]{1,0:T(8,128)} async-done(((f32[768,768]{1,0:T(8,128)}), f32[96,768]{1,0:T(8,128)}) %reduce-scatter.37.cloned.1.call-update) | async-done | bytes 294928 | tf_op jit(solution)/shard_map/reduce_scatter | solution.py:272
  1991.6 21.8 all-gather.52.cloned.1.call-done
  2074.2 38.2 %all-gather.34.cloned.1.call-done = bf16[1728,768]{0,1:T(8,128)(2,1)} async-done(((bf16[1728,192]{0,1:T(8,128)(2,1)}), bf16[1728,768]{0,1:T(8,128)(2,1)}) %all-gather.34.cloned.1.call-update) | async-done | bytes 2654224 | tf_op jit(solution)/shard_map/all_gather | solution.py:258
  2119.8 34.3 reduce-scatter.75.cloned.1.call-done
  2167.2 42.4 %reduce-scatter.49.cloned.1.call-done = f32[96,768]{1,0:T(8,128)} async-done(((f32[768,768]{1,0:T(8,128)}), f32[96,768]{1,0:T(8,128)}) %reduce-scatter.49.cloned.1.call-update) | async-done | bytes 294928 | tf_op jit(solution)/shard_map/reduce_scatter | solution.py:273
  2211.3 53.7 %reduce-scatter.39.cloned.1.call-done = f32[96,768]{1,0:T(8,128)} async-done(((f32[768,768]{1,0:T(8,128)}), f32[96,768]{1,0:T(8,128)}) %reduce-scatter.39.cloned.1.call-update) | async-done | bytes 294928 | tf_op jit(solution)/shard_map/reduce_scatter | solution.py:272
  2266.7 53.8 %reduce-scatter.57.cloned.1.call-done = f32[96,768]{1,0:T(8,128)} async-done(((f32[768,768]{1,0:T(8,128)}), f32[96,768]{1,0:T(8,128)}) %reduce-scatter.57.cloned.1.call-update) | async-done | bytes 294928 | tf_op jit(solution)/shard_map/reduce_scatter | solution.py:274
  2322.2 22.1 all-gather.56.cloned.1.call-done
  2430.1 38.2 %all-gather.38.cloned.1.call-done = bf16[1728,768]{0,1:T(8,128)(2,1)} async-done(((bf16[1728,192]{0,1:T(8,128)(2,1)}), bf16[1728,768]{0,1:T(8,128)(2,1)}) %all-gather.38.cloned.1.call-update) | async-done | bytes 2654224 | tf_op jit(solution)/shard_map/all_gather | solution.py:258
  2474.7 50.0 %reduce-scatter.59.cloned.1.call-done = f32[96,768]{1,0:T(8,128)} async-done(((f32[768,768]{1,0:T(8,128)}), f32[96,768]{1,0:T(8,128)}) %reduce-scatter.59.cloned.1.call-update) | async-done | bytes 294928 | tf_op jit(solution)/shard_map/reduce_scatter | solution.py:274
  2526.4 53.6 %reduce-scatter.51.cloned.1.call-done = f32[96,768]{1,0:T(8,128)} async-done(((f32[768,768]{1,0:T(8,128)}), f32[96,768]{1,0:T(8,128)}) %reduce-scatter.51.cloned.1.call-update) | async-done | bytes 294928 | tf_op jit(solution)/shard_map/reduce_scatter | solution.py:273
  2581.8 53.6 %reduce-scatter.41.cloned.1.call-done = f32[96,768]{1,0:T(8,128)} async-done(((f32[768,768]{1,0:T(8,128)}), f32[96,768]{1,0:T(8,128)}) %reduce-scatter.41.cloned.1.call-update) | async-done | bytes 294928 | tf_op jit(solution)/shard_map/reduce_scatter | solution.py:272
  2637.6 21.8 all-gather.72.cloned.1.call-done
  2716.1 48.6 %reduce-scatter.61.cloned.1.call-done = f32[96,768]{1,0:T(8,128)} async-done(((f32[768,768]{1,0:T(8,128)}), f32[96,768]{1,0:T(8,128)}) %reduce-scatter.61.cloned.1.call-update) | async-done | bytes 294928 | tf_op jit(solution)/shard_map/reduce_scatter | solution.py:274
  2766.4 29.2 all-gather.62.cloned.1.call-done
  2800.3 38.4 %all-gather.42.cloned.1.call-done = bf16[1728,768]{0,1:T(8,128)(2,1)} async-done(((bf16[1728,192]{0,1:T(8,128)(2,1)}), bf16[1728,768]{0,1:T(8,128)(2,1)}) %all-gather.42.cloned.1.call-update) | async-done | bytes 2654224 | tf_op jit(solution)/shard_map/all_gather | solution.py:258
  2880.0 39.6 %reduce-scatter.53.cloned.1.call-done = f32[96,768]{1,0:T(8,128)} async-done(((f32[768,768]{1,0:T(8,128)}), f32[96,768]{1,0:T(8,128)}) %reduce-scatter.53.cloned.1.call-update) | async-done | bytes 294928 | tf_op jit(solution)/shard_map/reduce_scatter | solution.py:273
  2921.4 53.6 %reduce-scatter.43.cloned.1.call-done = f32[96,768]{1,0:T(8,128)} async-done(((f32[768,768]{1,0:T(8,128)}), f32[96,768]{1,0:T(8,128)}) %reduce-scatter.43.cloned.1.call-update) | async-done | bytes 294928 | tf_op jit(solution)/shard_map/reduce_scatter | solution.py:272
  2976.7 53.6 %reduce-scatter.63.cloned.1.call-done = f32[96,768]{1,0:T(8,128)} async-done(((f32[768,768]{1,0:T(8,128)}), f32[96,768]{1,0:T(8,128)}) %reduce-scatter.63.cloned.1.call-update) | async-done | bytes 294928 | tf_op jit(solution)/shard_map/reduce_scatter | solution.py:274
  3032.1 22.3 all-gather.64.cloned.1.call-done
  3086.9 22.4 scatter-add.436
  3118.0 22.4 scatter-add.439
  3160.2 21.4 scatter-add.441
  3187.9 20.8 scatter-add.444
  3220.3 20.5 scatter-add.446
  3247.2 20.5 scatter-add.449
  3298.0 24.3 reshape.3513
  3404.7 53.7 %reduce-scatter.55.cloned.1.call-done = f32[96,768]{1,0:T(8,128)} async-done(((f32[768,768]{1,0:T(8,128)}), f32[96,768]{1,0:T(8,128)}) %reduce-scatter.55.cloned.1.call-update) | async-done | bytes 294928 | tf_op jit(solution)/shard_map/reduce_scatter | solution.py:273
  3463.1 50.6 %reduce-scatter.45.cloned.1.call-done = f32[96,768]{1,0:T(8,128)} async-done(((f32[768,768]{1,0:T(8,128)}), f32[96,768]{1,0:T(8,128)}) %reduce-scatter.45.cloned.1.call-update) | async-done | bytes 294928 | tf_op jit(solution)/shard_map/reduce_scatter | solution.py:272
  3515.3 60.6 %all-reduce.29.cloned.1.call-done = (f32[1000,128]{1,0:T(8,128)}, f32[148,2,384]{2,0,1:T(8,128)}, f32[148,2,192]{2,0,1:T(8,128)}) async-done(((f32[1000,128]{1,0:T(8,128)}, f32[148,2,384]{2,0,1:T(8,128)}, f32[148,2,192]{2,0,1:T(8,128)}), (f32[1000,128]{1,0:T(8,128)}, f32[148,2,384]{2,0,1:T(8,128)}, f32[148,2,192]{2,0,1:T(8,128)})) %all-reduce.29.cloned.1.call-update) | async-done | bytes 1194000 | tf_op jit(solution)/shard_map/psum | solution.py:421
  (888 shorter events, 1577.1 us)
Async XLA Ops:
  7.3 112.5 %all-gather.82.cloned.1.call-start = ((), (), s32[]{:S(2)}) async-start(), calls=%async_computation.63 | async-start | bytes 3096576 | tf_op jit(solution)/shard_map/all_gather | solution.py:383
  9.3 117.3 %all-gather.80.cloned.1.call-start = ((), (), s32[]{:S(2)}) async-start(), calls=%async_computation.62 | async-start | bytes 6193152 | tf_op jit(solution)/shard_map/all_gather | solution.py:382
  11.6 579.9 %reduce-scatter.67.cloned.1.call-start = ((), (), s32[]{:S(2)}) async-start(), calls=%async_computation.64 | async-start | bytes 983040
  568.4 305.2 %reduce-scatter.77.cloned.1.call-start = ((), (), s32[]{:S(2)}) async-start(), calls=%async_computation.69 | async-start | bytes 491520
  851.7 527.9 %reduce-scatter.69.cloned.1.call-start = ((), (), s32[]{:S(2)}) async-start(), calls=%async_computation.65 | async-start | bytes 983040
  1353.0 170.3 %reduce-scatter.73.cloned.1.call-start = ((), (), s32[]{:S(2)}) async-start(), calls=%async_computation.67 | async-start | bytes 7962624
  1372.5 429.0 %reduce-scatter.71.cloned.1.call-start = ((), (), s32[]{:S(2)}) async-start(), calls=%async_computation.66 | async-start | bytes 15925248
  1468.0 366.6 %all-gather.50.cloned.1.call-start = ((), (), s32[]{:S(2)}) async-start(), calls=%async_computation.37 | async-start | bytes 1720320 | tf_op jit(solution)/shard_map/all_gather | solution.py:259
  1525.9 351.8 %all-gather.30.cloned.1.call-start = ((), (), s32[]{:S(2)}) async-start(), calls=%async_computation.22 | async-start | bytes 3440640 | tf_op jit(solution)/shard_map/all_gather | solution.py:258
  1806.4 127.6 %reduce-scatter.47.cloned.1.call-start = ((), (), s32[]{:S(2)}) async-start(), calls=%async_computation.38 | async-start | bytes 2654208 | tf_op jit(solution)/shard_map/reduce_scatter | solution.py:273
  1839.3 150.1 %reduce-scatter.37.cloned.1.call-start = ((), (), s32[]{:S(2)}) async-start(), calls=%async_computation.23 | async-start | bytes 2654208 | tf_op jit(solution)/shard_map/reduce_scatter | solution.py:272
  1884.1 129.2 %all-gather.52.cloned.1.call-start = ((), (), s32[]{:S(2)}) async-start(), calls=%async_computation.39 | async-start | bytes 1327104 | tf_op jit(solution)/shard_map/all_gather | solution.py:280
  1935.6 102.3 %all-gather.32.cloned.1.call-start = ((), (), s32[]{:S(2)}) async-start(), calls=%async_computation.24 | async-start | bytes 1327104 | tf_op jit(solution)/shard_map/all_gather | solution.py:277
  2029.2 83.2 %all-gather.34.cloned.1.call-start = ((), (), s32[]{:S(2)}) async-start(), calls=%async_computation.25 | async-start | bytes 3440640 | tf_op jit(solution)/shard_map/all_gather | solution.py:258
  2056.3 97.7 %reduce-scatter.75.cloned.1.call-start = ((), (), s32[]{:S(2)}) async-start(), calls=%async_computation.68 | async-start | bytes 1769472
  2063.1 146.5 %reduce-scatter.49.cloned.1.call-start = ((), (), s32[]{:S(2)}) async-start(), calls=%async_computation.41 | async-start | bytes 2654208 | tf_op jit(solution)/shard_map/reduce_scatter | solution.py:273
  2074.1 190.9 %reduce-scatter.39.cloned.1.call-start = ((), (), s32[]{:S(2)}) async-start(), calls=%async_computation.26 | async-start | bytes 2654208 | tf_op jit(solution)/shard_map/reduce_scatter | solution.py:272
  2118.7 201.8 %reduce-scatter.57.cloned.1.call-start = ((), (), s32[]{:S(2)}) async-start(), calls=%async_computation.52 | async-start | bytes 2654208 | tf_op jit(solution)/shard_map/reduce_scatter | solution.py:274
  2167.2 177.2 %all-gather.56.cloned.1.call-start = ((), (), s32[]{:S(2)}) async-start(), calls=%async_computation.42 | async-start | bytes 1327104 | tf_op jit(solution)/shard_map/all_gather | solution.py:280
  2211.3 157.7 %all-gather.36.cloned.1.call-start = ((), (), s32[]{:S(2)}) async-start(), calls=%async_computation.27 | async-start | bytes 1327104 | tf_op jit(solution)/shard_map/all_gather | solution.py:277
  2266.7 126.9 %all-gather.70.cloned.1.call-start = ((), (), s32[]{:S(2)}) async-start(), calls=%async_computation.53 | async-start | bytes 1327104 | tf_op jit(solution)/shard_map/all_gather | solution.py:283
  2322.2 103.1 %all-gather.58.cloned.1.call-start = ((), (), s32[]{:S(2)}) async-start(), calls=%async_computation.43 | async-start | bytes 1720320 | tf_op jit(solution)/shard_map/all_gather | solution.py:259
  2350.9 117.4 %all-gather.38.cloned.1.call-start = ((), (), s32[]{:S(2)}) async-start(), calls=%async_computation.28 | async-start | bytes 3440640 | tf_op jit(solution)/shard_map/all_gather | solution.py:258
  2376.6 148.1 %reduce-scatter.59.cloned.1.call-start = ((), (), s32[]{:S(2)}) async-start(), calls=%async_computation.54 | async-start | bytes 2654208 | tf_op jit(solution)/shard_map/reduce_scatter | solution.py:274
  2418.2 161.9 %reduce-scatter.51.cloned.1.call-start = ((), (), s32[]{:S(2)}) async-start(), calls=%async_computation.44 | async-start | bytes 2654208 | tf_op jit(solution)/shard_map/reduce_scatter | solution.py:273
  2430.0 205.4 %reduce-scatter.41.cloned.1.call-start = ((), (), s32[]{:S(2)}) async-start(), calls=%async_computation.29 | async-start | bytes 2654208 | tf_op jit(solution)/shard_map/reduce_scatter | solution.py:272
  2474.7 184.7 %all-gather.72.cloned.1.call-start = ((), (), s32[]{:S(2)}) async-start(), calls=%async_computation.55 | async-start | bytes 1327104 | tf_op jit(solution)/shard_map/all_gather | solution.py:283
  2526.3 157.7 %all-gather.60.cloned.1.call-start = ((), (), s32[]{:S(2)}) async-start(), calls=%async_computation.45 | async-start | bytes 1327104 | tf_op jit(solution)/shard_map/all_gather | solution.py:280
  2581.7 126.8 %all-gather.40.cloned.1.call-start = ((), (), s32[]{:S(2)}) async-start(), calls=%async_computation.30 | async-start | bytes 1327104 | tf_op jit(solution)/shard_map/all_gather | solution.py:277
  2637.1 127.6 %reduce-scatter.61.cloned.1.call-start = ((), (), s32[]{:S(2)}) async-start(), calls=%async_computation.56 | async-start | bytes 2654208 | tf_op jit(solution)/shard_map/reduce_scatter | solution.py:274
  2675.8 119.8 %all-gather.62.cloned.1.call-start = ((), (), s32[]{:S(2)}) async-start(), calls=%async_computation.46 | async-start | bytes 1720320 | tf_op jit(solution)/shard_map/all_gather | solution.py:259
  2690.6 148.1 %all-gather.42.cloned.1.call-start = ((), (), s32[]{:S(2)}) async-start(), calls=%async_computation.31 | async-start | bytes 3440640 | tf_op jit(solution)/shard_map/all_gather | solution.py:258
  2716.0 147.5 %all-gather.74.cloned.1.call-start = ((), (), s32[]{:S(2)}) async-start(), calls=%async_computation.57 | async-start | bytes 1327104 | tf_op jit(solution)/shard_map/all_gather | solution.py:283
  2766.3 153.3 %reduce-scatter.53.cloned.1.call-start = ((), (), s32[]{:S(2)}) async-start(), calls=%async_computation.47 | async-start | bytes 2654208 | tf_op jit(solution)/shard_map/reduce_scatter | solution.py:273
  2800.2 174.8 %reduce-scatter.43.cloned.1.call-start = ((), (), s32[]{:S(2)}) async-start(), calls=%async_computation.32 | async-start | bytes 2654208 | tf_op jit(solution)/shard_map/reduce_scatter | solution.py:272
  2845.1 185.3 %reduce-scatter.63.cloned.1.call-start = ((), (), s32[]{:S(2)}) async-start(), calls=%async_computation.58 | async-start | bytes 2654208 | tf_op jit(solution)/shard_map/reduce_scatter | solution.py:274
  2880.0 174.4 %all-gather.64.cloned.1.call-start = ((), (), s32[]{:S(2)}) async-start(), calls=%async_computation.48 | async-start | bytes 1327104 | tf_op jit(solution)/shard_map/all_gather | solution.py:280
  2921.3 219.1 %all-gather.44.cloned.1.call-start = ((), (), s32[]{:S(2)}) async-start(), calls=%async_computation.33 | async-start | bytes 1327104 | tf_op jit(solution)/shard_map/all_gather | solution.py:277
  2976.7 345.9 %all-gather.76.cloned.1.call-start = ((), (), s32[]{:S(2)}) async-start(), calls=%async_computation.59 | async-start | bytes 1327104 | tf_op jit(solution)/shard_map/all_gather | solution.py:283
  3032.0 307.6 %all-gather.66.cloned.1.call-start = ((), (), s32[]{:S(2)}) async-start(), calls=%async_computation.49 | async-start | bytes 1720320 | tf_op jit(solution)/shard_map/all_gather | solution.py:259
  3060.9 283.6 %all-gather.46.cloned.1.call-start = ((), (), s32[]{:S(2)}) async-start(), calls=%async_computation.34 | async-start | bytes 3440640 | tf_op jit(solution)/shard_map/all_gather | solution.py:258
  3148.0 208.8 %reduce-scatter.79.cloned.1.call-start = ((), (), s32[]{:S(2)}) async-start(), calls=%async_computation.70 | async-start | bytes 491520
  3339.5 118.8 %reduce-scatter.55.cloned.1.call-start = ((), (), s32[]{:S(2)}) async-start(), calls=%async_computation.50 | async-start | bytes 2654208 | tf_op jit(solution)/shard_map/reduce_scatter | solution.py:273
  3344.4 169.3 %reduce-scatter.45.cloned.1.call-start = ((), (), s32[]{:S(2)}) async-start(), calls=%async_computation.35 | async-start | bytes 2654208 | tf_op jit(solution)/shard_map/reduce_scatter | solution.py:272
  3351.0 224.9 %all-reduce.29.cloned.1.call-start = ((), (), s32[]{:S(2)}) async-start(), calls=%async_computation.71 | async-start | bytes 2580480 | tf_op jit(solution)/shard_map/psum | solution.py:421
  3385.6 214.3 %all-gather.78.cloned.1.call-start = ((), (), s32[]{:S(2)}) async-start(), calls=%async_computation.61 | async-start | bytes 1327104 | tf_op jit(solution)/shard_map/all_gather | solution.py:283
  3404.6 219.8 %all-gather.68.cloned.1.call-start = ((), (), s32[]{:S(2)}) async-start(), calls=%async_computation.51 | async-start | bytes 1327104 | tf_op jit(solution)/shard_map/all_gather | solution.py:280
  3460.0 188.5 %all-gather.48.cloned.1.call-start = ((), (), s32[]{:S(2)}) async-start(), calls=%async_computation.36 | async-start | bytes 1327104 | tf_op jit(solution)/shard_map/all_gather | solution.py:277
  (138 other events, 2380.5 us)
Sparse Core Ops, SparseCore 0:
  10.3 38.0 all-gather.81
  50.5 71.4 all-gather.79
  568.6 22.8 reduce-scatter.66
  1353.1 23.1 reduce-scatter.68
  1378.5 144.8 reduce-scatter.72
  1525.6 275.8 reduce-scatter.70
  1804.0 30.5 all-gather.49
  1837.0 40.7 all-gather.29
  1879.9 54.0 reduce-scatter.46
  1936.3 53.1 reduce-scatter.36
  1991.5 21.7 all-gather.51
  2015.5 22.4 all-gather.31
  2040.2 29.1 all-gather.53
  2071.6 40.7 all-gather.33
  2114.5 39.4 reduce-scatter.74
  2156.2 53.3 reduce-scatter.48
  2211.8 53.1 reduce-scatter.38
  2267.3 53.1 reduce-scatter.56
  2322.5 21.7 all-gather.55
  2346.5 22.4 all-gather.35
  2371.2 22.4 all-gather.69
  2396.0 29.1 all-gather.57
  2427.6 40.7 all-gather.37
  2470.6 54.0 reduce-scatter.58
  2526.9 53.1 reduce-scatter.50
  2582.2 53.1 reduce-scatter.40
  2661.6 22.4 all-gather.59
  2686.0 22.4 all-gather.39
  2710.8 53.7 reduce-scatter.60
  2767.1 28.4 all-gather.61
  2797.9 40.7 all-gather.41
  2840.8 22.6 all-gather.73
  2865.8 53.7 reduce-scatter.52
  2921.8 53.1 reduce-scatter.42
  2977.2 53.1 reduce-scatter.62
  3032.5 21.7 all-gather.63
  3056.4 22.4 all-gather.43
  3081.0 22.4 all-gather.75
  3105.9 29.1 all-gather.65
  3148.1 40.0 all-gather.45
  3322.5 24.0 reduce-scatter.78
  3348.9 54.0 reduce-scatter.64
  3405.1 53.1 reduce-scatter.54
  3460.5 53.1 reduce-scatter.44
  3516.7 59.1 all-reduce.28
  3578.0 21.9 all-gather.77
  3602.0 22.4 all-gather.67
  3626.0 22.4 all-gather.47
  (2 shorter events, 43.4 us)
where the time goes:
time: 3680 us; the launch traced here: 3660 us
  waiting for transfers between devices  1630 us (44%)
  local copies, waits for them, and re-layouts  926 us (25%)
  blocking collectives  515 us (14%)
  matrix products  308 us (8%)
  other arithmetic  257 us (7%)
    scatter-add x74, local copies, waits for them, and re-layouts, unpatch(): padded = padded.at[:, row_shift:row_shift + rows_in, col_shift:col_shift...  517 us
    unnamed x57, waiting for transfers between devices  392 us
    unnamed x339, local copies, waits for them, and re-layouts  292 us
    reduce_scatter x5, waiting for transfers between devices, gram_total(): lax.psum_scatter(gram_blocks[0], ('half', 'dp'), scatter_dimension=0, til...  265 us
    reduce_scatter x5, waiting for transfers between devices, gram_total(): lax.psum_scatter(gram_blocks[1], ('half', 'dp'), scatter_dimension=0, til...  239 us
    reduce_scatter x5, waiting for transfers between devices, gram_total(): lax.psum_scatter(gram_blocks[2], ('half', 'dp'), scatter_dimension=0, til...  223 us
    all_gather x2, blocking collectives, forward(): full_two = lax.all_gather(acted_two, 'row', axis=3, tiled=True)  216 us
    all_gather x5, waiting for transfers between devices, gather_columns(): lax.all_gather(shortened(first), 'row', axis=1, tiled=True)  153 us
  transfers between devices with their start and end apart: 50, of which 42 were waited for; matrix products, arithmetic and copies ran while one was open for 17% of the time, Pallas kernels for 0%

commit v1 on v0

v1 whole, which is shorter than its diff:
```python
import functools
import math

import jax
import jax.numpy as jnp
from jax import lax
from jax.experimental import pallas as pl
from jax.experimental.pallas import tpu as pltpu
from jax.sharding import PartitionSpec as P

EMB = 128
NCLS = 1000
MICRO = 2
NS_ITERS = 5
STEP = 10

highest = lax.Precision.HIGHEST
high = lax.Precision.HIGH
bf16 = jnp.bfloat16
f32 = jnp.float32
BN_EPS = 1e-05
NEWTON_EPSILON = 1e-07
NS_COEF = (3.4445, -4.775, 2.0315)
MOMENTUM = 0.9
MUON_RATE = 0.03
DECAY = 0.01
BETA_ONE = 0.9
BETA_TWO = 0.95
ADAM_EPS = 1e-08
ADAM_RATE = 0.05
COLOUR_RATE = 0.01
PAD = 8
VMEM_BYTES = 48 * 1024 * 1024


def kernel_params():
    return pltpu.CompilerParams(vmem_limit_bytes=VMEM_BYTES)


def whole(shape):
    return pl.BlockSpec(shape, lambda t, r: (0,) * len(shape))


def silu_slope(values):
    sigmoid_value = jax.nn.sigmoid(values)
    return sigmoid_value * (1.0 + values * (1.0 - sigmoid_value))


def contract_last(left, right):
    return lax.dot_general(left, right, (((1,), (1,)), ((), ())), preferred_element_type=f32)


def times(left, right):
    return jnp.dot(left, right, preferred_element_type=f32)


def axis_swap(value, axis, k):
    n = lax.axis_size(axis)
    return lax.ppermute(value, axis, [(i, i ^ k) for i in range(n)])


def axis_shift(value, axis, k):
    n = lax.axis_size(axis)
    return lax.ppermute(value, axis, [(i, (i + k) % n) for i in range(n)])


def row_gather(value):
    return [value] + [axis_swap(value, "row", k) for k in range(1, lax.axis_size("row"))]


def row_sum(value):
    return sum(row_gather(value))


def row_scatter(pieces):
    arrived = [axis_swap(pieces[k], "row", k) for k in range(1, len(pieces))]
    total = pieces[0].astype(f32)
    for piece in arrived:
        total = total + piece.astype(f32)
    return total


def group_sum(value):
    value = value + axis_swap(value, "half", 1)
    return sum([value] + [axis_shift(value, "dp", k) for k in range(1, lax.axis_size("dp"))])


def group_pile(value):
    parts = [value] + [axis_shift(value, "dp", k) for k in range(1, lax.axis_size("dp"))]
    return jnp.concatenate(parts + [axis_swap(part, "half", 1) for part in parts], axis=0)


def group_gather(value):
    n = lax.axis_size("dp")
    h, z = lax.axis_index("half"), lax.axis_index("dp")
    rows = value.shape[0]
    full = jnp.zeros((2 * n * rows,) + value.shape[1:], value.dtype)
    for k in range(n):
        part = value if k == 0 else axis_shift(value, "dp", k)
        other = axis_swap(part, "half", 1)
        place = lax.rem(z + n - k, n)
        full = lax.dynamic_update_slice_in_dim(full, part, (h * n + place) * rows, 0)
        full = lax.dynamic_update_slice_in_dim(full, other, ((1 - h) * n + place) * rows, 0)
    return full


def group_scatter(value):
    n = lax.axis_size("dp")
    h, z = lax.axis_index("half"), lax.axis_index("dp")
    halves = value.reshape((2, n, value.shape[0] // (2 * n)) + value.shape[1:])
    kept = lax.dynamic_index_in_dim(halves, h, 0, keepdims=False)
    sent = lax.dynamic_index_in_dim(halves, 1 - h, 0, keepdims=False)
    kept = kept.astype(f32) + axis_swap(sent, "half", 1).astype(f32)
    wire = kept.astype(value.dtype)
    total = lax.dynamic_index_in_dim(kept, z, 0, keepdims=False)
    for k in range(1, n):
        block = lax.dynamic_index_in_dim(wire, lax.rem(z + k, n), 0, keepdims=False)
        total = total + axis_shift(block, "dp", k).astype(f32)
    return total


def raise_two(values):
    h, w, n, c = values.shape
    wide = jnp.stack([values, values], axis=2).reshape(h, 2 * w, n, c)
    return jnp.stack([wide, wide], axis=1).reshape(2 * h, 2 * w, n, c)


def sum_two(values):
    h, w, n, c = values.shape
    shaped = values.reshape(h // 2, 2, w // 2, 2, n, c)
    return (shaped[:, 0, :, 0] + shaped[:, 0, :, 1]) + (shaped[:, 1, :, 0] + shaped[:, 1, :, 1])


def owned_rows(row_ref, k, size):
    return pl.ds(pl.multiple_of(lax.bitwise_xor(row_ref[0], k) * size, size), size)


def flat(values):
    return values.reshape(-1, values.shape[-1])


def conv_one_kernel(row_ref, *refs):
    blocks, (w_ref, out_ref, sums_ref, acc_ref) = refs[:-4], refs[-4:]
    h2, w2, n, c = out_ref.shape
    t = pl.program_id(0)
    dy, dx = lax.div(t, 3), lax.rem(t, 3)

    @pl.when(t == 0)
    def _():
        acc_ref[...] = jnp.zeros_like(acc_ref)

    product = sum(
        times(x_ref[...], w_ref[0, owned_rows(row_ref, k, x_ref.shape[1]), :])
        for k, x_ref in enumerate(blocks)
    )
    raised = raise_two(product.reshape(h2 // 2, w2 // 2, n, c))
    acc_ref[pl.ds(2 - dy, h2), pl.ds(2 - dx, w2)] += raised

    @pl.when(t == 8)
    def _():
        hidden = acc_ref[1 : h2 + 1, 1 : w2 + 1]
        out_ref[...] = hidden
        shaped = hidden.reshape(h2 * w2, n, c)
        first, second = jnp.sum(shaped, axis=0), jnp.sum(shaped * shaped, axis=0)
        m = n // MICRO
        for i in range(MICRO):
            sums_ref[i : i + 1, :] = jnp.sum(first[i * m : (i + 1) * m], axis=0, keepdims=True)
            sums_ref[MICRO + i : MICRO + i + 1, :] = jnp.sum(
                second[i * m : (i + 1) * m], axis=0, keepdims=True
            )


def conv_one(row, blocks, weight, pixels):
    h, w, n = pixels
    c = weight.shape[-1]
    return pl.pallas_call(
        conv_one_kernel,
        out_shape=(
            jax.ShapeDtypeStruct((2 * h, 2 * w, n, c), f32),
            jax.ShapeDtypeStruct((2 * MICRO, c), f32),
        ),
        grid_spec=pltpu.PrefetchScalarGridSpec(
            num_scalar_prefetch=1,
            grid=(9,),
            in_specs=[whole(b.shape) for b in blocks]
            + [pl.BlockSpec((1,) + weight.shape[1:], lambda t, r: (t, 0, 0))],
            out_specs=(whole((2 * h, 2 * w, n, c)), whole((2 * MICRO, c))),
            scratch_shapes=[pltpu.VMEM((2 * h + 2, 2 * w + 2, n, c), f32)],
        ),
        compiler_params=kernel_params(),
        name="conv_one",
    )(row, *blocks, weight)


def conv_two_kernel(count, row_ref, *refs):
    blocks, raws = refs[:count], refs[count : 2 * count]
    w_ref, skip_ref, colour_ref, sum_ref, act_ref, pic_ref, pad_ref, apad_ref = refs[2 * count :]
    h2, w2, n, c = sum_ref.shape
    t = pl.program_id(0)
    dy, dx = lax.div(t, 3), lax.rem(t, 3)

    @pl.when(t == 0)
    def _():
        pad_ref[...] = jnp.zeros_like(pad_ref)
        for k in range(count):
            pad_ref[k, 1 : h2 + 1, 1 : w2 + 1] = blocks[k][...]
        skipped = sum(
            times(x_ref[...], skip_ref[owned_rows(row_ref, k, x_ref.shape[1]), :])
            for k, x_ref in enumerate(raws)
        )
        sum_ref[...] = raise_two(skipped.reshape(h2 // 2, w2 // 2, n, c))

    product = sum(
        times(
            flat(pad_ref[k, pl.ds(dy, h2), pl.ds(dx, w2)]), w_ref[0, owned_rows(row_ref, k, c), :]
        )
        for k in range(count)
    )
    sum_ref[...] += product.reshape(sum_ref.shape)

    @pl.when(t == 8)
    def _():
        active = jax.nn.silu(sum_ref[...]).astype(bf16)
        act_ref[...] = active
        apad_ref[...] = jnp.zeros_like(apad_ref)
        apad_ref[1 : h2 + 1, 1 : w2 + 1] = active
        picture = jnp.zeros(pic_ref.shape, f32)
        for tap in range(9):
            y, x = divmod(tap, 3)
            picture = picture + contract_last(
                colour_ref[tap], flat(apad_ref[y : y + h2, x : x + w2])
            )
        pic_ref[...] = picture


def conv_two(row, blocks, raws, weight, skip, colour):
    h2, w2, n, c = blocks[0].shape
    return pl.pallas_call(
        functools.partial(conv_two_kernel, len(blocks)),
        out_shape=(
            jax.ShapeDtypeStruct((h2, w2, n, c), f32),
            jax.ShapeDtypeStruct((h2, w2, n, c), bf16),
            jax.ShapeDtypeStruct((PAD, h2 * w2 * n), f32),
        ),
        grid_spec=pltpu.PrefetchScalarGridSpec(
            num_scalar_prefetch=1,
            grid=(9,),
            in_specs=[whole(b.shape) for b in blocks + raws]
            + [
                pl.BlockSpec((1,) + weight.shape[1:], lambda t, r: (t, 0, 0)),
                whole(skip.shape),
                whole(colour.shape),
            ],
            out_specs=(whole((h2, w2, n, c)), whole((h2, w2, n, c)), whole((PAD, h2 * w2 * n))),
            scratch_shapes=[
                pltpu.VMEM((len(blocks), h2 + 2, w2 + 2, n, c), bf16),
                pltpu.VMEM((h2 + 2, w2 + 2, n, c), bf16),
            ],
        ),
        compiler_params=kernel_params(),
        name="conv_two",
    )(row, *blocks, *raws, weight, skip, colour)


def critic_kernel(
    dims, pic_ref, first_ref, second_ref, skip_ref, head_ref, count_ref, out_ref, loss_ref, small_ref, pad_ref
):
    h2, w2, n = dims
    h, w = h2 // 2, w2 // 2
    c = second_ref.shape[-1]
    taps = [divmod(tap, 3) for tap in range(9)]
    shade = jnp.tanh(jnp.transpose(pic_ref[...]))
    picture = shade.astype(bf16).reshape(h2, w2, n, PAD)
    small_ref[...] = jnp.zeros_like(small_ref)
    small_ref[1 : h2 + 1, 1 : w2 + 1] = picture
    pad_ref[...] = jnp.zeros_like(pad_ref)
    front_pre = sum(
        times(flat(small_ref[y : y + h2, x : x + w2]), first_ref[3 * y + x]) for y, x in taps
    )
    pad_ref[1 : h2 + 1, 1 : w2 + 1] = jax.nn.silu(front_pre).astype(bf16).reshape(h2, w2, n, c)
    merged = sum(times(flat(pad_ref[y : y + h2, x : x + w2]), second_ref[3 * y + x]) for y, x in taps)
    merged = 0.25 * flat(sum_two(merged.reshape(h2, w2, n, c)))
    small = 0.25 * flat(sum_two(picture.astype(f32)))
    skip = skip_ref[...].astype(f32)
    for i in range(3):
        merged = merged + small[:, i : i + 1] * skip[i : i + 1, :]
    feature = jnp.sum(jax.nn.silu(merged).reshape(h * w, n, c), axis=0)
    weights = head_ref[...] * count_ref[...]
    loss_ref[...] = jnp.broadcast_to(-jnp.sum(feature * weights, keepdims=True), loss_ref.shape)
    grad_merged = (silu_slope(merged).reshape(h * w, n, c) * -weights[None]).astype(bf16)
    grad_merged = grad_merged.reshape(h, w, n, c)
    grad_pool = raise_two(grad_merged) * jnp.bfloat16(0.25)
    pad_ref[1 : h2 + 1, 1 : w2 + 1] = grad_pool
    grad_front = sum(
        contract_last(flat(pad_ref[2 - y : 2 - y + h2, 2 - x : 2 - x + w2]), second_ref[3 * y + x])
        for y, x in taps
    )
    grad_front_pre = (grad_front * silu_slope(front_pre)).astype(bf16)
    pad_ref[1 : h2 + 1, 1 : w2 + 1] = grad_front_pre.reshape(h2, w2, n, c)
    grad_picture = sum(
        contract_last(flat(pad_ref[2 - y : 2 - y + h2, 2 - x : 2 - x + w2]), first_ref[3 * y + x])
        for y, x in taps
    )
    grad_skip = contract_last(flat(grad_merged), skip_ref[...]).reshape(h, w, n, PAD)
    grad_picture = grad_picture + 0.25 * flat(raise_two(grad_skip))
    grad_pre = (grad_picture * (1.0 - shade * shade)).astype(bf16)
    small_ref[1 : h2 + 1, 1 : w2 + 1] = grad_pre.reshape(h2, w2, n, PAD)
    out_ref[...] = jnp.concatenate(
        [flat(small_ref[2 - y : 2 - y + h2, 2 - x : 2 - x + w2]) for y, x in taps]
        + [jnp.zeros((h2 * w2 * n, 128 - 9 * PAD), bf16)],
        axis=1,
    )


def critic(picture, disc_first, disc_second, disc_skip, head, counted, dims):
    h2, w2, n = dims
    c = disc_second.shape[-1]
    return pl.pallas_call(
        functools.partial(critic_kernel, dims),
        out_shape=(
            jax.ShapeDtypeStruct((h2 * w2 * n, 128), bf16),
            jax.ShapeDtypeStruct((8, 128), f32),
        ),
        scratch_shapes=[
            pltpu.VMEM((h2 + 2, w2 + 2, n, PAD), bf16),
            pltpu.VMEM((h2 + 2, w2 + 2, n, c), bf16),
        ],
        compiler_params=kernel_params(),
        name="critic",
    )(picture, disc_first, disc_second, disc_skip, head, counted)


def back_two_kernel(count, row_ref, g_ref, sum_ref, act_ref, colour_ref, w_ref, *refs):
    gpad_ref, gcol_ref = refs[0], refs[1]
    outs, acc_ref = refs[2:-1], refs[-1]
    h2, w2, n, c = sum_ref.shape
    t = pl.program_id(0)
    dy, dx = lax.div(t, 3), lax.rem(t, 3)

    @pl.when(t == 0)
    def _():
        grad_active = times(g_ref[...], colour_ref[...]).reshape(h2, w2, n, c)
        gpad_ref[...] = jnp.zeros_like(gpad_ref)
        gpad_ref[1 : h2 + 1, 1 : w2 + 1] = (grad_active * silu_slope(sum_ref[...])).astype(bf16)
        gcol_ref[...] = lax.dot_general(
            g_ref[...], flat(act_ref[...]), (((0,), (0,)), ((), ())), preferred_element_type=f32
        )
        acc_ref[...] = jnp.zeros_like(acc_ref)

    shifted = flat(gpad_ref[pl.ds(2 - dy, h2), pl.ds(2 - dx, w2)])
    for k in range(count):
        acc_ref[k] += contract_last(shifted, w_ref[0, owned_rows(row_ref, k, c), :])

    @pl.when(t == 8)
    def _():
        for k in range(count):
            outs[k][...] = acc_ref[k].astype(bf16)


def back_two(row, grads, summed, active, colour, weight, count):
    h2, w2, n, c = summed.shape
    rows = h2 * w2 * n
    return pl.pallas_call(
        functools.partial(back_two_kernel, count),
        out_shape=(
            jax.ShapeDtypeStruct((h2 + 2, w2 + 2, n, c), bf16),
            jax.ShapeDtypeStruct((128, c), f32),
        )
        + tuple(jax.ShapeDtypeStruct((rows, c), bf16) for _ in range(count)),
        grid_spec=pltpu.PrefetchScalarGridSpec(
            num_scalar_prefetch=1,
            grid=(9,),
            in_specs=[
                whole(grads.shape),
                whole(summed.shape),
                whole(active.shape),
                whole(colour.shape),
                pl.BlockSpec((1,) + weight.shape[1:], lambda t, r: (t, 0, 0)),
            ],
            out_specs=(whole((h2 + 2, w2 + 2, n, c)), whole((128, c)))
            + tuple(whole((rows, c)) for _ in range(count)),
            scratch_shapes=[pltpu.VMEM((count, rows, c), f32)],
        ),
        compiler_params=kernel_params(),
        name="back_two",
    )(row, grads, summed, active, colour, weight)


def weight_two_kernel(count, row_ref, gpad_ref, *refs):
    blocks, raws, (out_ref, skip_ref) = refs[:count], refs[count : 2 * count], refs[2 * count :]
    h2, w2, n, c = (gpad_ref.shape[0] - 2, gpad_ref.shape[1] - 2) + gpad_ref.shape[2:]
    t = pl.program_id(0)
    dy, dx = lax.div(t, 3), lax.rem(t, 3)
    shifted = flat(gpad_ref[pl.ds(2 - dy, h2), pl.ds(2 - dx, w2)])
    for k in range(count):
        out_ref[0, owned_rows(row_ref, k, c), :] = times(blocks[k][...], shifted).astype(bf16)

    @pl.when(t == 8)
    def _():
        phases = gpad_ref[1 : h2 + 1, 1 : w2 + 1].reshape(h2 // 2, 2, w2 // 2, 2, n, c)
        for k in range(count):
            size = raws[k].shape[0]
            skip_ref[owned_rows(row_ref, k, size), :] = sum(
                times(raws[k][...], flat(phases[:, a, :, b])) for a in range(2) for b in range(2)
            ).astype(bf16)


def weight_two(row, gpad, blocks, raws):
    c = gpad.shape[-1]
    count = len(blocks)
    tall, wide = count * blocks[0].shape[0], count * raws[0].shape[0]
    return pl.pallas_call(
        functools.partial(weight_two_kernel, count),
        out_shape=(
            jax.ShapeDtypeStruct((9, tall, c), bf16),
            jax.ShapeDtypeStruct((wide, c), bf16),
        ),
        grid_spec=pltpu.PrefetchScalarGridSpec(
            num_scalar_prefetch=1,
            grid=(9,),
            in_specs=[whole(gpad.shape)] + [whole(b.shape) for b in blocks + raws],
            out_specs=(pl.BlockSpec((1, tall, c), lambda t, r: (t, 0, 0)), whole((wide, c))),
        ),
        compiler_params=kernel_params(),
        name="weight_two",
    )(row, gpad, *blocks, *raws)


def back_one_kernel(count, row_ref, g_ref, w_ref, *refs):
    blocks, out_ref, outs = refs[:count], refs[count], refs[count + 1 : 2 * count + 1]
    pad_ref, acc_ref = refs[2 * count + 1 :]
    h2, w2, n, c = g_ref.shape
    size = blocks[0].shape[0]
    t = pl.program_id(0)
    dy, dx = lax.div(t, 3), lax.rem(t, 3)

    @pl.when(t == 0)
    def _():
        pad_ref[...] = jnp.zeros_like(pad_ref)
        pad_ref[1 : h2 + 1, 1 : w2 + 1] = g_ref[...]
        acc_ref[...] = jnp.zeros_like(acc_ref)

    shifted = pad_ref[pl.ds(2 - dy, h2), pl.ds(2 - dx, w2)].astype(f32)
    pooled = flat(sum_two(shifted)).astype(bf16)
    for k in range(count):
        rows = owned_rows(row_ref, k, size)
        acc_ref[k] += contract_last(pooled, w_ref[0, rows, :])
        out_ref[0, rows, :] = times(blocks[k][...], pooled).astype(bf16)

    @pl.when(t == 8)
    def _():
        for k in range(count):
            outs[k][...] = acc_ref[k].astype(bf16)


def back_one(row, grads, weight, blocks):
    h2, w2, n, c = grads.shape
    count = len(blocks)
    size, rows = blocks[0].shape
    return pl.pallas_call(
        functools.partial(back_one_kernel, count),
        out_shape=(jax.ShapeDtypeStruct((9, count * size, c), bf16),)
        + tuple(jax.ShapeDtypeStruct((rows, size), bf16) for _ in range(count)),
        grid_spec=pltpu.PrefetchScalarGridSpec(
            num_scalar_prefetch=1,
            grid=(9,),
            in_specs=[
                whole(grads.shape),
                pl.BlockSpec((1,) + weight.shape[1:], lambda t, r: (t, 0, 0)),
            ]
            + [whole(b.shape) for b in blocks],
            out_specs=(pl.BlockSpec((1, count * size, c), lambda t, r: (t, 0, 0)),)
            + tuple(whole((rows, size)) for _ in range(count)),
            scratch_shapes=[
                pltpu.VMEM((h2 + 2, w2 + 2, n, c), bf16),
                pltpu.VMEM((count, rows, size), f32),
            ],
        ),
        compiler_params=kernel_params(),
        name="back_one",
    )(row, grads, weight, *blocks)


def in_order(pieces, axis_name):
    piled = jnp.stack(pieces, axis=0)
    r = lax.axis_index(axis_name)
    return jnp.concatenate(
        [
            lax.dynamic_index_in_dim(piled, lax.bitwise_xor(r, j), 0, keepdims=False)
            for j in range(len(pieces))
        ],
        axis=0,
    )


def gram_share(owned, pieces):
    blocks = [
        lax.dot_general(piece, owned, (((0,), (0,)), ((), ())), preferred_element_type=f32)
        for piece in pieces
    ]
    return in_order(blocks, "row")


def gram_whole(panel):
    n = lax.axis_size("dp")
    h, z = lax.axis_index("half"), lax.axis_index("dp")
    total = group_sum_wide(panel)
    pieces = row_gather(total)
    piled = jnp.stack(pieces, axis=0)
    r = lax.axis_index("row")
    return jnp.concatenate(
        [
            lax.dynamic_index_in_dim(piled, lax.bitwise_xor(r, j), 0, keepdims=False)
            for j in range(len(pieces))
        ],
        axis=1,
    )


def group_sum_wide(value):
    return group_gather(group_scatter(value))


def mul(left, right):
    return jnp.dot(left, right, precision=high, preferred_element_type=f32)


def newton_columns(gram, own):
    scale = lax.rsqrt(jnp.trace(gram) + NEWTON_EPSILON)
    current = gram * (scale * scale)
    identity = jnp.eye(gram.shape[0], dtype=f32)
    maps = []
    for iteration in range(NS_ITERS):
        square = mul(current, current)
        mapping = NS_COEF[0] * identity + NS_COEF[1] * current + NS_COEF[2] * square
        maps.append(mapping)
        if iteration < NS_ITERS - 1:
            current = mul(mapping, mul(current, mapping))
    start = lax.axis_index("row") * own
    columns = lax.dynamic_slice_in_dim(maps[-1], start, own, 1)
    for mapping in maps[-2::-1]:
        columns = mul(mapping, columns)
    return columns * scale


def muon(master, moment, gradient, groups):
    moment_new = MOMENTUM * moment + gradient
    owned = moment_new.astype(bf16)
    pieces = row_gather(owned)
    own = owned.shape[1]
    gram = gram_whole(gram_share(owned, pieces))
    columns = newton_columns(gram, own).astype(bf16)
    r = lax.axis_index("row")
    direction = sum(
        times(
            piece,
            lax.dynamic_slice_in_dim(columns, lax.bitwise_xor(r, k) * own, own, 0),
        )
        for k, piece in enumerate(pieces)
    )
    factor = 0.2 * math.sqrt(max(master.shape[0] * groups, own * len(pieces)))
    return master - MUON_RATE * (factor * direction + DECAY * master), moment_new


def adam_update(weight, gradient, mean_old, square_old, rate):
    mean_new = BETA_ONE * mean_old + (1.0 - BETA_ONE) * gradient
    square_new = BETA_TWO * square_old + (1.0 - BETA_TWO) * gradient * gradient
    ratio = (
        mean_new
        / (1.0 - BETA_ONE**STEP)
        / (jnp.sqrt(square_new / (1.0 - BETA_TWO**STEP)) + ADAM_EPS)
    )
    return (weight - rate * (ratio + DECAY * weight), mean_new, square_new)


def moments_of(totals, count):
    centre = totals[:MICRO] / count
    return centre, lax.rsqrt(totals[MICRO:] / count - centre * centre + BN_EPS)


def per_image(values, n):
    return jnp.repeat(values, n // MICRO, axis=0)


def per_micro(values):
    return jnp.sum(values.reshape(MICRO, -1, values.shape[-1]), axis=1)


def per_device(
    features,
    noise,
    labels,
    counted,
    disc_first,
    disc_second,
    disc_skip,
    disc_head,
    disc_table,
    conv_first,
    conv_second,
    conv_skip,
    momentum_first,
    momentum_second,
    momentum_skip,
    class_table,
    table_mean,
    table_square,
    norm_first,
    first_mean,
    first_square,
    norm_second,
    second_mean,
    second_square,
    colour_conv,
    colour_mean,
    colour_square,
):
    groups = lax.axis_size("half") * lax.axis_size("dp")
    ranks = lax.axis_size("row")
    row = lax.axis_index("row").astype(jnp.int32).reshape(1)
    n, h, w, c_in = features.shape
    c_out = conv_first.shape[1]
    count_low = float(n // MICRO * h * w * groups)
    count_high = 4.0 * count_low

    inputs = jnp.transpose(features, (1, 2, 0, 3))
    raw = inputs.astype(f32)
    sums_low = jnp.concatenate(
        [per_micro(jnp.sum(raw, axis=(0, 1))), per_micro(jnp.sum(raw * raw, axis=(0, 1)))], axis=0
    )
    totals_low = group_sum(sums_low)
    weight_one = group_gather(conv_first.astype(bf16)).reshape(9, ranks * c_in, c_out)

    onehot = (labels[:, None] == jnp.arange(NCLS)[None, :]).astype(f32)
    conds = jnp.concatenate([jnp.dot(onehot, class_table, precision=highest), noise], axis=1)
    class_disc = jnp.dot(onehot, disc_table, precision=highest)
    mods_one = jnp.einsum("bk,kgc->bgc", conds, norm_first, precision=highest)
    mods_two = jnp.einsum("bk,kgc->bgc", conds, norm_second, precision=highest)

    centre_one, spread_one = moments_of(totals_low, count_low)
    centre_one, spread_one = per_image(centre_one, n), per_image(spread_one, n)
    gain_one, gain_two = 1.0 + mods_one[:, 0], 1.0 + mods_two[:, 0]
    normed_one = (raw - centre_one) * spread_one
    pre_one = normed_one * gain_one + mods_one[:, 1]
    acted_one = flat(jax.nn.silu(pre_one).astype(bf16))
    ones = row_gather(acted_one)
    raws = row_gather(flat(inputs))

    hidden, sums_high = conv_one(row, ones, weight_one, (h, w, n))
    held_second, held_skip, _ = lax.optimization_barrier(
        (conv_second.astype(bf16), conv_skip.astype(bf16), weight_one[0, 0, 0])
    )
    weight_skip = group_gather(held_skip)
    weight_two = group_gather(held_second).reshape(9, ranks * c_out, c_out)
    totals_high = group_sum(sums_high)
    centre_two, spread_two = moments_of(totals_high, count_high)
    centre_two, spread_two = per_image(centre_two, n), per_image(spread_two, n)
    normed_two = (hidden - centre_two) * spread_two
    pre_two = normed_two * gain_two + mods_two[:, 1]
    acted_two = jax.nn.silu(pre_two).astype(bf16)
    twos = row_gather(acted_two)

    colour = jnp.pad(
        jnp.transpose(colour_conv, (0, 2, 1)).astype(bf16), ((0, 0), (0, PAD - 3), (0, 0))
    )
    summed, active, picture = conv_two(row, twos, raws, weight_two, weight_skip, colour)
    picture = row_sum(picture)

    first_taps = jnp.pad(disc_first.reshape(9, 3, -1), ((0, 0), (0, PAD - 3), (0, 0)))
    second_taps = disc_second.reshape(9, -1, disc_second.shape[-1])
    skip_taps = jnp.pad(disc_skip, ((0, PAD - 3), (0, 0)))
    mark = counted.astype(f32)[:, None]
    grads, loss_part = critic(
        picture,
        first_taps,
        second_taps,
        skip_taps,
        disc_head[None, :] + class_disc,
        mark,
        (2 * h, 2 * w, n),
    )
    colour_rows = jnp.pad(colour.reshape(9 * PAD, c_out), ((0, 128 - 9 * PAD), (0, 0)))
    backs = back_two(row, grads, summed, active, colour_rows, weight_two, ranks)
    gpad, grad_colour, pieces = backs[0], backs[1], backs[2:]
    grad_two, grad_skip = weight_two_grads(row, gpad, twos, raws)
    grad_acted_two = row_scatter(list(pieces)).reshape(hidden.shape)

    grad_pre_two = grad_acted_two * silu_slope(pre_two)
    gains_two = jnp.sum(grad_pre_two * normed_two, axis=(0, 1))
    shifts_two = jnp.sum(grad_pre_two, axis=(0, 1))
    back_sums = group_sum(
        jnp.concatenate([per_micro(gain_two * shifts_two), per_micro(gain_two * gains_two)], axis=0)
    )
    mean_g = per_image(back_sums[:MICRO] / count_high, n)
    mean_gy = per_image(back_sums[MICRO:] / count_high, n)
    grad_hidden = (spread_two * (grad_pre_two * gain_two - mean_g - normed_two * mean_gy)).astype(
        bf16
    )
    ones_turned = [jnp.transpose(one) for one in ones]
    backs = back_one(row, grad_hidden, weight_one, ones_turned)
    grad_one, pieces = flat(backs[0]), backs[1:]
    grad_acted_one = row_scatter(list(pieces)).reshape(raw.shape)
    grad_pre_one = grad_acted_one * silu_slope(pre_one)
    gains_one = jnp.sum(grad_pre_one * normed_one, axis=(0, 1))
    shifts_one = jnp.sum(grad_pre_one, axis=(0, 1))
    grad_mods_one = jnp.stack([gains_one, shifts_one], axis=1)
    grad_mods_two = jnp.stack([gains_two, shifts_two], axis=1)

    grad_cond = jnp.einsum("bgc,kgc->bk", grad_mods_one, norm_first[:EMB], precision=highest)
    grad_cond = grad_cond + jnp.einsum(
        "bgc,kgc->bk", grad_mods_two, norm_second[:EMB], precision=highest
    )
    grad_cond = row_sum(grad_cond)

    count_part = jnp.sum(counted).astype(f32)
    small = jnp.concatenate(
        [
            grad_colour[: 9 * PAD],
            jnp.broadcast_to(loss_part[:1, :1], (1, c_out)),
            jnp.broadcast_to(count_part, (1, c_out)),
        ],
        axis=0,
    )
    small = group_sum(small)
    loss_sum, fake_count = small[9 * PAD, 0], small[9 * PAD + 1, 0]
    inverse = 1.0 / fake_count
    g_colour = jnp.transpose(small[: 9 * PAD].reshape(9, PAD, c_out)[:, :3], (0, 2, 1))

    known = group_pile(jnp.concatenate([conds, labels.astype(f32)[:, None]], axis=1))
    found = group_pile(
        jnp.concatenate(
            [grad_mods_one.reshape(n, -1), grad_mods_two.reshape(n, -1), grad_cond], axis=1
        )
    )
    conds_all, labels_all = known[:, :-1], known[:, -1].astype(jnp.int32)
    onehot_all = (labels_all[:, None] == jnp.arange(NCLS)[None, :]).astype(f32)
    cut_one, cut_two = 2 * c_in, 2 * c_in + 2 * c_out
    g_norm = lax.dot_general(
        conds_all,
        found[:, :cut_two],
        (((0,), (0,)), ((), ())),
        precision=highest,
        preferred_element_type=f32,
    )
    g_norm_one = g_norm[:, :cut_one].reshape(norm_first.shape)
    g_norm_two = g_norm[:, cut_one:].reshape(norm_second.shape)
    g_table = lax.dot_general(
        onehot_all,
        found[:, cut_two:],
        (((0,), (0,)), ((), ())),
        precision=highest,
        preferred_element_type=f32,
    )

    shares = [group_scatter(flat(g)) for g in (grad_one, grad_two, grad_skip)]
    muons = [
        muon(master, moment, share * inverse, groups)
        for master, moment, share in zip(
            (conv_first, conv_second, conv_skip),
            (momentum_first, momentum_second, momentum_skip),
            shares,
        )
    ]
    table_new = adam_update(class_table, g_table * inverse, table_mean, table_square, ADAM_RATE)
    first_new = adam_update(norm_first, g_norm_one * inverse, first_mean, first_square, ADAM_RATE)
    second_new = adam_update(
        norm_second, g_norm_two * inverse, second_mean, second_square, ADAM_RATE
    )
    colour_new = adam_update(
        colour_conv, g_colour * inverse, colour_mean, colour_square, COLOUR_RATE
    )
    return (
        (loss_sum, fake_count)
        + tuple(m[0] for m in muons)
        + tuple(m[1] for m in muons)
        + table_new
        + first_new
        + second_new
        + colour_new
    )


def weight_two_grads(row, gpad, twos, raws):
    turned = [jnp.transpose(flat(two)) for two in twos]
    return weight_two(row, gpad, turned, [jnp.transpose(one) for one in raws])


def solution(mesh):
    group = ("half", "dp")
    placed = (
        (P(group, None, None, "row"), P(group, None), P(group), P(group))
        + (P(),) * 5
        + (P(group, "row"),) * 6
        + (P(),) * 3
        + (P(None, None, "row"),) * 6
        + (P(None, "row", None),) * 3
    )
    return jax.shard_map(
        per_device,
        mesh=mesh,
        in_specs=placed,
        out_specs=(P(), P())
        + (P(group, "row"),) * 6
        + (P(),) * 3
        + (P(None, None, "row"),) * 6
        + (P(None, "row", None),) * 3,
        check_vma=False,
    )
```

time: 3680 us -> 861 us (0.23)
  waiting for transfers between devices: 1630 us -> 199 us
  local copies, waits for them, and re-layouts: 926 us -> 183 us
  blocking collectives: 515 us -> 0 us
  other arithmetic: 257 us -> 54.2 us
  starting transfers between devices: 4.12 us -> 153 us
  matrix products: 308 us -> 201 us
  Pallas kernels: 0 us -> 55.7 us
    reduce_scatter x15 -> x0, waiting for transfers between devices: 728 us -> none  [the longest x5 265 us: gram_total(): lax.psum_scatter(gram_blocks[0], ('half', 'dp'), scatter_dimension=0, til...]
    scatter-add x74 -> x0, local copies, waits for them, and re-layouts: 517 us -> none  [unpatch(): padded = padded.at[:, row_shift:row_shift + rows_in, col_shift:col_shift...]
    all_gather x27 -> x0, waiting for transfers between devices: 450 us -> none  [the longest x5 153 us: gather_columns(): lax.all_gather(shortened(first), 'row', axis=1, tiled=True)]
    unnamed x57 -> x0, waiting for transfers between devices: 392 us -> none
    all_gather x12 -> x0, blocking collectives: 351 us -> none  [the longest x2 216 us: forward(): full_two = lax.all_gather(acted_two, 'row', axis=3, tiled=True)]
    unnamed x339 -> x300, local copies, waits for them, and re-layouts: 292 us -> 24.5 us
    ppermute x0 -> x135, waiting for transfers between devices: none -> 199 us  [the longest x81 106 us: axis_swap(): return lax.ppermute(value, axis, [(i, i ^ k) for i in range(n)])]
    psum x9 -> x0, blocking collectives: 163 us -> none  [the longest x5 81.6 us: batch_stats(): return lax.psum((first_sum, second_sum), ('half', 'dp'))]
  transfers between devices with their start and end apart: 50 -> 135, of which waited for: 42 -> 51; matrix products, arithmetic and copies ran while one was open for 17% -> 39% of each run, Pallas kernels for 0% -> 3%
where the time goes in v1:
time: 861 us; the launch traced here: 854 us
  matrix products  201 us (23%)
  waiting for transfers between devices  199 us (23%)
  local copies, waits for them, and re-layouts  183 us (21%)
  starting transfers between devices  153 us (18%)
  Pallas kernels  55.7 us (6%)
  other arithmetic  54.2 us (6%)
    dot_general x51, matrix products, mul(): return jnp.dot(left, right, precision=high, preferred_element_type=f32)  179 us
    ppermute x81, waiting for transfers between devices, axis_swap(): return lax.ppermute(value, axis, [(i, i ^ k) for i in range(n)])  106 us
    ppermute x54, starting transfers between devices, axis_shift(): return lax.ppermute(value, axis, [(i, (i + k) % n) for i in range(n)])  99.8 us
    ppermute x54, waiting for transfers between devices, axis_shift(): return lax.ppermute(value, axis, [(i, (i + k) % n) for i in range(n)])  93.8 us
    ppermute x81, starting transfers between devices, axis_swap(): return lax.ppermute(value, axis, [(i, i ^ k) for i in range(n)])  53.6 us
    dynamic_update_slice x24, local copies, waits for them, and re-layouts, group_gather(): lax.dynamic_update_slice_in_dim(full, other, ((1 - h) * n + place) * rows...  31.8 us
    dynamic_update_slice x24, local copies, waits for them, and re-layouts, group_gather(): lax.dynamic_update_slice_in_dim(full, part, (h * n + place) * rows, 0)  30.9 us
    unnamed x300, local copies, waits for them, and re-layouts  24.5 us
  transfers between devices with their start and end apart: 135, of which 51 were waited for; matrix products, arithmetic and copies ran while one was open for 39% of the time, Pallas kernels for 3%

profile of v1, /device:TPU:0, one launch (start us, length us, event | category | flops | bytes accessed | tf_op | source)
XLA Modules:
  0.0 854.2 jit_solution(3960032501266599721)
XLA Ops:
  51.4 5.0 collective-permute-done.34
  71.6 3.9 collective-permute-start.12
  75.6 4.2 collective-permute-done.8
  84.8 31.2 %collective-permute-done.25 = bf16[864,192]{0,1:T(8,128)(2,1)} collective-permute-done((bf16[864,192]{0,1:T(8,128)(2,1)}, bf16[864,192]{0,1:T(8,128)(2,1)}, u32[]{:S(2)}, u32[]{:S(2)}) %collective-permute-start.25) | collective-permute-done | bytes 331808 | tf_op jit(solution)/shard_map/ppermute | solution.py:64
  116.0 12.9 %collective-permute-start.27 = (bf16[864,192]{0,1:T(8,128)(2,1)}, bf16[864,192]{0,1:T(8,128)(2,1)}, u32[]{:S(2)}, u32[]{:S(2)}) collective-permute-start(bf16[864,192]{0,1:T(8,128)(2,1)} %copy-done.89), channel_id=1, source_target_pairs={{0,8},{4,12},{8,0},{12,4},{1,9},{5,13},{9,1},{13,5},{2,10},{6,14},... | collective-permute-start | bytes 995336 | tf_op jit(solution)/shard_map/ppermute | solution.py:64
  160.6 8.3 conv_one.1
  200.2 9.6 %collective-permute-done.19.refs_2_ = bf16[8,8,16,192]{3,2,1,0:T(8,128)(2,1)S(1)} collective-permute-done((bf16[8,8,16,192]{3,2,1,0:T(8,128)(2,1)S(1)}, bf16[8,8,16,192]{3,2,1,0:T(8,128)(2,1)S(1)}, u32[]{:S(2)}, u32[]{:S(2)}) %collective-permute-start.19) | collective-permute-done | bytes 393248 | tf_op jit(solution)/shard_map/ppermute | solution.py:59
  209.9 11.7 %conv_two.1 = (f32[8,8,16,192]{3,2,1,0:T(8,128)S(1)}, bf16[8,8,16,192]{3,2,1,0:T(8,128)(2,1)S(1)}, f32[8,1024]{1,0:T(8,128)}) custom-call(s32[1]{0:T(128)} %bitcast.row_ref, bf16[8,8,16,192]{3,2,1,0:T(8,128)(2,1)S(1)} %multiply_convert_fusion.1.refs_0_, bf16[8,8,16,192]{3,2,1,0:T(8,128)(2,1)S(1)} %collective-permute-done.18.refs_1_, ...), custom_call_target="tpu_custom_call" | custom-call | tf_op jit(solution)/shard_map/conv_two/pallas_call | solution.py:238
  231.6 5.7 critic.1
  239.6 10.7 %back_two.1 = (bf16[10,10,16,192]{3,2,1,0:T(8,128)(2,1)S(1)}, f32[128,192]{1,0:T(8,128)S(1)}, bf16[1024,192]{1,0:T(8,128)(2,1)S(1)}, bf16[1024,192]{1,0:T(8,128)...) custom-call(s32[1]{0:T(128)} %bitcast.row_ref, bf16[1024,128]{1,0:T(8,128)(2,1)S(1)} %get-tuple-element.47.g_ref, ...), custom_call_target="tpu_custom_call" | custom-call | tf_op jit(solution)/shard_map/back_two/pallas_call | solution.py:363
  254.5 7.8 weight_two.1
  262.3 4.1 constant_dynamic-slice_fusion.16
  283.3 9.4 %collective-permute-start.95 = (bf16[192,192]{1,0:T(8,128)(2,1)S(1)}, bf16[192,192]{1,0:T(8,128)(2,1)S(1)}, u32[]{:S(2)}, u32[]{:S(2)}) collective-permute-start(bf16[192,192]{1,0:T(8,128)(2,1)S(1)} %get-tuple-element.140), channel_id=1, source_target_pairs={{0,4},{4,8},{8,12},{12,0},{1,5},{5,9},{9,13},{13,1},{2,6},{6,10},{... | collective-permute-start | bytes 221192 | tf_op jit(solution)/shard_map/ppermute | solution.py:64
  294.2 4.0 collective-permute-done.95
  315.1 11.4 %back_one.1 = (bf16[9,1536,192]{2,1,0:T(8,128)(2,1)}, bf16[256,384]{1,0:T(8,128)(2,1)S(1)}, bf16[256,384]{1,0:T(8,128)(2,1)S(1)}, bf16[256,384]{1,0:T(8,128)(2,1)S(1)}, bf16[256,384]{1,0:T(8,128)(2,1)S(1)}) custom-call(s32[1]{0:T(128)} %bitcast.row_ref, bf16[8,8,16,192]{3,2,1,0:T(8,128)(2,1)S(1)} %multiply_convert_fusion.g_ref, ...), custom_call_target="tpu_custom_call" | custom-call | tf_op jit(solution)/shard_map/back_one/pallas_call | solution.py:460
  326.5 6.4 constant_dynamic-slice_fusion.26
  332.9 4.7 copy.416
  337.7 4.7 copy.466
  381.1 5.6 collective-permute-done.103
  428.5 11.2 %collective-permute-done.113 = f32[768,192]{0,1:T(8,128)S(1)} collective-permute-done((f32[768,192]{0,1:T(8,128)S(1)}, f32[768,192]{0,1:T(8,128)S(1)}, u32[]{:S(2)}, u32[]{:S(2)}) %collective-permute-start.113) | collective-permute-done | bytes 589856 | tf_op jit(solution)/shard_map/ppermute | solution.py:59
  446.2 3.7 fusion.14
  479.3 3.6 fusion.52
  483.0 3.6 fusion.50
  486.7 7.2 fusion.481
  496.1 5.0 fusion.48
  511.7 5.7 collective-permute-done.79
  517.7 5.9 collective-permute-done.78
  537.5 6.8 collective-permute-done.82
  575.1 4.8 convert_add_fusion
  581.3 4.0 collective-permute-start.55
  585.3 3.6 collective-permute-done.93
  590.9 9.7 %collective-permute-done.92 = f32[768,192]{0,1:T(8,128)S(1)} collective-permute-done((f32[768,192]{0,1:T(8,128)}, f32[768,192]{0,1:T(8,128)S(1)}, u32[]{:S(2)}, u32[]{:S(2)}) %collective-permute-start.92) | collective-permute-done | bytes 589856 | tf_op jit(solution)/shard_map/ppermute | solution.py:59
  607.3 5.6 fusion.9
  646.1 3.6 fusion.56
  649.7 7.4 fusion.476
  657.1 3.5 fusion.463
  667.2 6.3 fusion.54
  673.9 6.1 collective-permute-done.58
  681.5 12.2 %collective-permute-done.57 = bf16[1728,192]{0,1:T(8,128)(2,1)S(1)} collective-permute-done((bf16[1728,192]{0,1:T(8,128)(2,1)S(1)}, bf16[1728,192]{0,1:T(8,128)(2,1)S(1)}, u32[]{:S(2)}, u32[]{:S(2)}) %collective-permute-start.57) | collective-permute-done | bytes 663584 | tf_op jit(solution)/shard_map/ppermute | solution.py:59
  707.9 4.2 collective-permute-start.62
  715.3 5.9 collective-permute-done.61
  756.0 10.0 %collective-permute-done.72 = f32[768,192]{0,1:T(8,128)S(1)} collective-permute-done((f32[768,192]{0,1:T(8,128)}, f32[768,192]{0,1:T(8,128)S(1)}, u32[]{:S(2)}, u32[]{:S(2)}) %collective-permute-start.72) | collective-permute-done | bytes 589856 | tf_op jit(solution)/shard_map/ppermute | solution.py:59
  766.1 11.6 %collective-permute-done.71 = f32[768,192]{0,1:T(8,128)S(1)} collective-permute-done((f32[768,192]{0,1:T(8,128)}, f32[768,192]{0,1:T(8,128)S(1)}, u32[]{:S(2)}, u32[]{:S(2)}) %collective-permute-start.71) | collective-permute-done | bytes 589856 | tf_op jit(solution)/shard_map/ppermute | solution.py:59
  786.8 5.6 fusion.5
  808.7 3.6 fusion.469
  825.5 3.6 fusion.74
  829.2 7.3 fusion.471
  839.6 5.5 fusion.72
  (841 shorter events, 508.4 us)
Async XLA Ops:
  3.7 44.8 %collective-permute-start.31 = (bf16[192,192]{1,0:T(8,128)(2,1)}, bf16[192,192]{1,0:T(8,128)(2,1)}, u32[]{:S(2)}, u32[]{:S(2)}) collective-permute-start(bf16[192,192]{1,0:T(8,128)(2,1)} %convert_element_type.163), channel_id=1, source_target_pairs={{0,16},{16,0},{1,17},{17,1},{2,18},{18,2},{3,19},{19,3},{4,20},{20... | collective-permute-start | bytes 221192 | tf_op jit(solution)/shard_map/ppermute | solution.py:59
  4.2 47.2 %collective-permute-start.32 = (bf16[192,192]{1,0:T(8,128)(2,1)}, bf16[192,192]{1,0:T(8,128)(2,1)}, u32[]{:S(2)}, u32[]{:S(2)}) collective-permute-start(bf16[192,192]{1,0:T(8,128)(2,1)} %convert_element_type.163), channel_id=1, source_target_pairs={{0,4},{4,8},{8,12},{12,0},{1,5},{5,9},{9,13},{13,1},{2,6},{6,10},{... | collective-permute-start | bytes 221192 | tf_op jit(solution)/shard_map/ppermute | solution.py:64
  10.2 26.6 %collective-permute-start.115 = (f32[16,149]{1,0:T(8,128)}, f32[16,149]{1,0:T(8,128)}, u32[]{:S(2)}, u32[]{:S(2)}) collective-permute-start(f32[16,149]{1,0:T(8,128)} %get-tuple-element.85), channel_id=1, source_target_pairs={{0,4},{4,8},{8,12},{12,0},{1,5},{5,9},{9,13},{13,1},{2,6},{6,10},{... | collective-permute-start | bytes 28616 | tf_op jit(solution)/shard_map/ppermute | solution.py:64
  11.8 26.1 %collective-permute-start.116 = (f32[16,149]{1,0:T(8,128)}, f32[16,149]{1,0:T(8,128)}, u32[]{:S(2)}, u32[]{:S(2)}) collective-permute-start(f32[16,149]{1,0:T(8,128)} %get-tuple-element.85), channel_id=1, source_target_pairs={{0,8},{4,12},{8,0},{12,4},{1,9},{5,13},{9,1},{13,5},{2,10},{6,14},... | collective-permute-start | bytes 28616 | tf_op jit(solution)/shard_map/ppermute | solution.py:64
  14.5 18.7 %collective-permute-start = (f32[4,384]{1,0:T(4,128)}, f32[4,384]{1,0:T(4,128)}, u32[]{:S(2)}, u32[]{:S(2)}) collective-permute-start(f32[4,384]{1,0:T(4,128)} %pad_maximum_fusion.17), channel_id=1, source_target_pairs={{0,16},{16,0},{1,17},{17,1},{2,18},{18,2},{3,19},{19,3},{4,20},{20... | collective-permute-start | bytes 18440 | tf_op jit(solution)/shard_map/ppermute | solution.py:59
  42.4 18.6 %collective-permute-start.21 = (bf16[256,384]{0,1:T(8,128)(2,1)S(1)}, bf16[256,384]{0,1:T(8,128)(2,1)S(1)}, u32[]{:S(2)}, u32[]{:S(2)}) collective-permute-start(bf16[256,384]{0,1:T(8,128)(2,1)S(1)} %copy.398), channel_id=1, source_target_pairs={{0,1},{1,0},{2,3},{3,2},{4,5},{5,4},{6,7},{7,6},{8,9},{9,8},{10,11... | collective-permute-start | bytes 589832 | tf_op jit(solution)/shard_map/ppermute | solution.py:59
  46.0 15.9 %collective-permute-start.22 = (bf16[256,384]{0,1:T(8,128)(2,1)S(1)}, bf16[256,384]{0,1:T(8,128)(2,1)S(1)}, u32[]{:S(2)}, u32[]{:S(2)}) collective-permute-start(bf16[256,384]{0,1:T(8,128)(2,1)S(1)} %copy.398), channel_id=1, source_target_pairs={{0,2},{1,3},{2,0},{3,1},{4,6},{5,7},{6,4},{7,5},{8,10},{9,11},{10,... | collective-permute-start | bytes 589832 | tf_op jit(solution)/shard_map/ppermute | solution.py:59
  59.3 20.5 %collective-permute-start.8 = (bf16[1728,192]{0,1:T(8,128)(2,1)}, bf16[1728,192]{0,1:T(8,128)(2,1)}, u32[]{:S(2)}, u32[]{:S(2)}) collective-permute-start(bf16[1728,192]{0,1:T(8,128)(2,1)} %convert_element_type.160), channel_id=1, source_target_pairs={{0,4},{4,8},{8,12},{12,0},{1,5},{5,9},{9,13},{13,1},{2,6},{6,10},{... | collective-permute-start | bytes 1990664 | tf_op jit(solution)/shard_map/ppermute | solution.py:64
  67.5 67.5 %collective-permute-start.7 = (bf16[1728,192]{0,1:T(8,128)(2,1)}, bf16[1728,192]{0,1:T(8,128)(2,1)}, u32[]{:S(2)}, u32[]{:S(2)}) collective-permute-start(bf16[1728,192]{0,1:T(8,128)(2,1)} %convert_element_type.160), channel_id=1, source_target_pairs={{0,16},{16,0},{1,17},{17,1},{2,18},{18,2},{3,19},{19,3},{4,20},{20... | collective-permute-start | bytes 1990664 | tf_op jit(solution)/shard_map/ppermute | solution.py:59
  68.1 69.9 %collective-permute-start.10 = (bf16[1728,192]{0,1:T(8,128)(2,1)}, bf16[1728,192]{0,1:T(8,128)(2,1)}, u32[]{:S(2)}, u32[]{:S(2)}) collective-permute-start(bf16[1728,192]{0,1:T(8,128)(2,1)} %convert_element_type.160), channel_id=1, source_target_pairs={{0,8},{4,12},{8,0},{12,4},{1,9},{5,13},{9,1},{13,5},{2,10},{6,14},... | collective-permute-start | bytes 1990664 | tf_op jit(solution)/shard_map/ppermute | solution.py:64
  71.6 67.8 %collective-permute-start.12 = (bf16[1728,192]{0,1:T(8,128)(2,1)}, bf16[1728,192]{0,1:T(8,128)(2,1)}, u32[]{:S(2)}, u32[]{:S(2)}) collective-permute-start(bf16[1728,192]{0,1:T(8,128)(2,1)} %convert_element_type.160), channel_id=1, source_target_pairs={{0,12},{4,0},{8,4},{12,8},{1,13},{5,1},{9,5},{13,9},{2,14},{6,2},{... | collective-permute-start | bytes 1990664 | tf_op jit(solution)/shard_map/ppermute | solution.py:64
  75.5 40.4 %collective-permute-start.25 = (bf16[864,192]{0,1:T(8,128)(2,1)}, bf16[864,192]{0,1:T(8,128)(2,1)}, u32[]{:S(2)}, u32[]{:S(2)}) collective-permute-start(bf16[864,192]{0,1:T(8,128)(2,1)} %copy-done.89), channel_id=1, source_target_pairs={{0,4},{4,8},{8,12},{12,0},{1,5},{5,9},{9,13},{13,1},{2,6},{6,10},{... | collective-permute-start | bytes 995336 | tf_op jit(solution)/shard_map/ppermute | solution.py:64
  79.8 66.9 %collective-permute-start.9 = (bf16[1728,192]{0,1:T(8,128)(2,1)}, bf16[1728,192]{0,1:T(8,128)(2,1)}, u32[]{:S(2)}, u32[]{:S(2)}) collective-permute-start(bf16[1728,192]{0,1:T(8,128)(2,1)} %collective-permute-done.8), channel_id=1, source_target_pairs={{0,16},{16,0},{1,17},{17,1},{2,18},{18,2},{3,19},{19,3},{4,20},{20... | collective-permute-start | bytes 1990664 | tf_op jit(solution)/shard_map/ppermute | solution.py:59
  116.0 54.3 %collective-permute-start.27 = (bf16[864,192]{0,1:T(8,128)(2,1)}, bf16[864,192]{0,1:T(8,128)(2,1)}, u32[]{:S(2)}, u32[]{:S(2)}) collective-permute-start(bf16[864,192]{0,1:T(8,128)(2,1)} %copy-done.89), channel_id=1, source_target_pairs={{0,8},{4,12},{8,0},{12,4},{1,9},{5,13},{9,1},{13,5},{2,10},{6,14},... | collective-permute-start | bytes 995336 | tf_op jit(solution)/shard_map/ppermute | solution.py:64
  135.0 37.3 %collective-permute-start.29 = (bf16[864,192]{0,1:T(8,128)(2,1)}, bf16[864,192]{0,1:T(8,128)(2,1)}, u32[]{:S(2)}, u32[]{:S(2)}) collective-permute-start(bf16[864,192]{0,1:T(8,128)(2,1)} %copy-done.89), channel_id=1, source_target_pairs={{0,12},{4,0},{8,4},{12,8},{1,13},{5,1},{9,5},{13,9},{2,14},{6,2},{... | collective-permute-start | bytes 995336 | tf_op jit(solution)/shard_map/ppermute | solution.py:64
  138.0 36.6 %collective-permute-start.26 = (bf16[864,192]{0,1:T(8,128)(2,1)}, bf16[864,192]{0,1:T(8,128)(2,1)}, u32[]{:S(2)}, u32[]{:S(2)}) collective-permute-start(bf16[864,192]{0,1:T(8,128)(2,1)} %collective-permute-done.25), channel_id=1, source_target_pairs={{0,16},{16,0},{1,17},{17,1},{2,18},{18,2},{3,19},{19,3},{4,20},{20... | collective-permute-start | bytes 995336 | tf_op jit(solution)/shard_map/ppermute | solution.py:59
  172.2 17.5 %collective-permute-start.28 = (bf16[864,192]{0,1:T(8,128)(2,1)}, bf16[864,192]{0,1:T(8,128)(2,1)}, u32[]{:S(2)}, u32[]{:S(2)}) collective-permute-start(bf16[864,192]{0,1:T(8,128)(2,1)} %collective-permute-done.27), channel_id=1, source_target_pairs={{0,16},{16,0},{1,17},{17,1},{2,18},{18,2},{3,19},{19,3},{4,20},{20... | collective-permute-start | bytes 995336 | tf_op jit(solution)/shard_map/ppermute | solution.py:59
  174.2 17.4 %collective-permute-start.30 = (bf16[864,192]{0,1:T(8,128)(2,1)}, bf16[864,192]{0,1:T(8,128)(2,1)}, u32[]{:S(2)}, u32[]{:S(2)}) collective-permute-start(bf16[864,192]{0,1:T(8,128)(2,1)} %collective-permute-done.29), channel_id=1, source_target_pairs={{0,16},{16,0},{1,17},{17,1},{2,18},{18,2},{3,19},{19,3},{4,20},{20... | collective-permute-start | bytes 995336 | tf_op jit(solution)/shard_map/ppermute | solution.py:59
  185.3 14.9 %collective-permute-start.18 = (bf16[8,8,16,192]{3,2,1,0:T(8,128)(2,1)S(1)}, bf16[8,8,16,192]{3,2,1,0:T(8,128)(2,1)S(1)}, u32[]{:S(2)}, u32[]{:S(2)}) collective-permute-start(bf16[8,8,16,192]{3,2,1,0:T(8,128)(2,1)S(1)} %multiply_convert_fusion.1.refs_0_), channel_id=1, source_target_pairs={{0,1},{1,0},{2,3},{3,2},{4,5},{5,4},{6,7},{7,6},{8,9},{9,8},{10,11... | collective-permute-start | bytes 1179656 | tf_op jit(solution)/shard_map/ppermute | solution.py:59
  186.6 23.2 %collective-permute-start.19 = (bf16[8,8,16,192]{3,2,1,0:T(8,128)(2,1)S(1)}, bf16[8,8,16,192]{3,2,1,0:T(8,128)(2,1)S(1)}, u32[]{:S(2)}, u32[]{:S(2)}) collective-permute-start(bf16[8,8,16,192]{3,2,1,0:T(8,128)(2,1)S(1)} %multiply_convert_fusion.1.refs_0_), channel_id=1, source_target_pairs={{0,2},{1,3},{2,0},{3,1},{4,6},{5,7},{6,4},{7,5},{8,10},{9,11},{10,... | collective-permute-start | bytes 1179656 | tf_op jit(solution)/shard_map/ppermute | solution.py:59
  187.5 22.3 %collective-permute-start.20 = (bf16[8,8,16,192]{3,2,1,0:T(8,128)(2,1)S(1)}, bf16[8,8,16,192]{3,2,1,0:T(8,128)(2,1)}, u32[]{:S(2)}, u32[]{:S(2)}) collective-permute-start(bf16[8,8,16,192]{3,2,1,0:T(8,128)(2,1)S(1)} %multiply_convert_fusion.1.refs_0_), channel_id=1, source_target_pairs={{0,3},{1,2},{2,1},{3,0},{4,7},{5,6},{6,5},{7,4},{8,11},{9,10},{10,... | collective-permute-start | bytes 1179656 | tf_op jit(solution)/shard_map/ppermute | solution.py:59
  251.8 49.6 %collective-permute-start.47 = (bf16[1024,192]{1,0:T(8,128)(2,1)}, bf16[1024,192]{1,0:T(8,128)(2,1)}, u32[]{:S(2)}, u32[]{:S(2)}) collective-permute-start(bf16[1024,192]{1,0:T(8,128)(2,1)} %get-tuple-element.55), channel_id=1, source_target_pairs={{0,3},{1,2},{2,1},{3,0},{4,7},{5,6},{6,5},{7,4},{8,11},{9,10},{10,... | collective-permute-start | bytes 1179656 | tf_op jit(solution)/shard_map/ppermute | solution.py:59
  253.4 48.0 %collective-permute-start.46 = (bf16[1024,192]{1,0:T(8,128)(2,1)}, bf16[1024,192]{1,0:T(8,128)(2,1)}, u32[]{:S(2)}, u32[]{:S(2)}) collective-permute-start(bf16[1024,192]{1,0:T(8,128)(2,1)} %get-tuple-element.54), channel_id=1, source_target_pairs={{0,2},{1,3},{2,0},{3,1},{4,6},{5,7},{6,4},{7,5},{8,10},{9,11},{10,... | collective-permute-start | bytes 1179656 | tf_op jit(solution)/shard_map/ppermute | solution.py:59
  274.0 27.3 %collective-permute-start.45 = (bf16[1024,192]{1,0:T(8,128)(2,1)S(1)}, bf16[1024,192]{1,0:T(8,128)(2,1)}, u32[]{:S(2)}, u32[]{:S(2)}) collective-permute-start(bf16[1024,192]{1,0:T(8,128)(2,1)S(1)} %copy-done.31), channel_id=1, source_target_pairs={{0,1},{1,0},{2,3},{3,2},{4,5},{5,4},{6,7},{7,6},{8,9},{9,8},{10,11... | collective-permute-start | bytes 1179656 | tf_op jit(solution)/shard_map/ppermute | solution.py:59
  294.2 123.1 %collective-permute-start.73 = (bf16[4,864,192]{1,2,0:T(8,128)(2,1)}, bf16[4,864,192]{1,2,0:T(8,128)(2,1)}, u32[]{:S(2)}, u32[]{:S(2)}) collective-permute-start(bf16[4,864,192]{1,2,0:T(8,128)(2,1)} %bitcast.470), channel_id=1, source_target_pairs={{0,16},{16,0},{1,17},{17,1},{2,18},{18,2},{3,19},{19,3},{4,20},{20... | collective-permute-start | bytes 3981320 | tf_op jit(solution)/shard_map/ppermute | solution.py:59
  300.0 43.9 %collective-permute-start.100 = (bf16[192,192]{1,0:T(8,128)(2,1)S(1)}, bf16[192,192]{1,0:T(8,128)(2,1)S(1)}, u32[]{:S(2)}, u32[]{:S(2)}) collective-permute-start(bf16[192,192]{1,0:T(8,128)(2,1)S(1)} %get-tuple-element.86), channel_id=1, source_target_pairs={{0,3},{1,2},{2,1},{3,0},{4,7},{5,6},{6,5},{7,4},{8,11},{9,10},{10,... | collective-permute-start | bytes 221192 | tf_op jit(solution)/shard_map/ppermute | solution.py:59
  309.7 35.3 %collective-permute-start.99 = (bf16[192,192]{1,0:T(8,128)(2,1)S(1)}, bf16[192,192]{1,0:T(8,128)(2,1)S(1)}, u32[]{:S(2)}, u32[]{:S(2)}) collective-permute-start(bf16[192,192]{1,0:T(8,128)(2,1)S(1)} %get-tuple-element.86), channel_id=1, source_target_pairs={{0,2},{1,3},{2,0},{3,1},{4,6},{5,7},{6,4},{7,5},{8,10},{9,11},{10,... | collective-permute-start | bytes 221192 | tf_op jit(solution)/shard_map/ppermute | solution.py:59
  312.5 33.9 %collective-permute-start.98 = (bf16[192,192]{1,0:T(8,128)(2,1)S(1)}, bf16[192,192]{1,0:T(8,128)(2,1)S(1)}, u32[]{:S(2)}, u32[]{:S(2)}) collective-permute-start(bf16[192,192]{1,0:T(8,128)(2,1)S(1)} %get-tuple-element.86), channel_id=1, source_target_pairs={{0,1},{1,0},{2,3},{3,2},{4,5},{5,4},{6,7},{7,6},{8,9},{9,8},{10,11... | collective-permute-start | bytes 221192 | tf_op jit(solution)/shard_map/ppermute | solution.py:59
  403.0 172.1 %collective-permute-start.52 = (bf16[4,1728,192]{1,2,0:T(8,128)(2,1)}, bf16[4,1728,192]{1,2,0:T(8,128)(2,1)}, u32[]{:S(2)}, u32[]{:S(2)}) collective-permute-start(bf16[4,1728,192]{1,2,0:T(8,128)(2,1)} %bitcast.466), channel_id=1, source_target_pairs={{0,16},{16,0},{1,17},{17,1},{2,18},{18,2},{3,19},{19,3},{4,20},{20... | collective-permute-start | bytes 7962632 | tf_op jit(solution)/shard_map/ppermute | solution.py:59
  410.5 17.1 %collective-permute-start.114 = (f32[768,192]{0,1:T(8,128)S(1)}, f32[768,192]{0,1:T(8,128)S(1)}, u32[]{:S(2)}, u32[]{:S(2)}) collective-permute-start(f32[768,192]{0,1:T(8,128)S(1)} %dynamic_update_slice.191), channel_id=1, source_target_pairs={{0,3},{1,2},{2,1},{3,0},{4,7},{5,6},{6,5},{7,4},{8,11},{9,10},{10,... | collective-permute-start | bytes 1769480 | tf_op jit(solution)/shard_map/ppermute | solution.py:59
  411.9 27.8 %collective-permute-start.113 = (f32[768,192]{0,1:T(8,128)S(1)}, f32[768,192]{0,1:T(8,128)S(1)}, u32[]{:S(2)}, u32[]{:S(2)}) collective-permute-start(f32[768,192]{0,1:T(8,128)S(1)} %dynamic_update_slice.191), channel_id=1, source_target_pairs={{0,2},{1,3},{2,0},{3,1},{4,6},{5,7},{6,4},{7,5},{8,10},{9,11},{10,... | collective-permute-start | bytes 1769480 | tf_op jit(solution)/shard_map/ppermute | solution.py:59
  412.8 28.6 %collective-permute-start.112 = (f32[768,192]{0,1:T(8,128)S(1)}, f32[768,192]{0,1:T(8,128)S(1)}, u32[]{:S(2)}, u32[]{:S(2)}) collective-permute-start(f32[768,192]{0,1:T(8,128)S(1)} %dynamic_update_slice.191), channel_id=1, source_target_pairs={{0,1},{1,0},{2,3},{3,2},{4,5},{5,4},{6,7},{7,6},{8,9},{9,8},{10,11... | collective-permute-start | bytes 1769480 | tf_op jit(solution)/shard_map/ppermute | solution.py:59
  421.5 81.4 %collective-permute-start.76 = (bf16[864,192]{0,1:T(8,128)(2,1)}, bf16[864,192]{0,1:T(8,128)(2,1)}, u32[]{:S(2)}, u32[]{:S(2)}) collective-permute-start(bf16[864,192]{0,1:T(8,128)(2,1)} %get-tuple-element.119), channel_id=1, source_target_pairs={{0,12},{4,0},{8,4},{12,8},{1,13},{5,1},{9,5},{13,9},{2,14},{6,2},{... | collective-permute-start | bytes 995336 | tf_op jit(solution)/shard_map/ppermute | solution.py:64
  427.6 75.3 %collective-permute-start.75 = (bf16[864,192]{0,1:T(8,128)(2,1)}, bf16[864,192]{0,1:T(8,128)(2,1)}, u32[]{:S(2)}, u32[]{:S(2)}) collective-permute-start(bf16[864,192]{0,1:T(8,128)(2,1)} %get-tuple-element.120), channel_id=1, source_target_pairs={{0,8},{4,12},{8,0},{12,4},{1,9},{5,13},{9,1},{13,5},{2,10},{6,14},... | collective-permute-start | bytes 995336 | tf_op jit(solution)/shard_map/ppermute | solution.py:64
  439.7 63.2 %collective-permute-start.74 = (bf16[864,192]{0,1:T(8,128)(2,1)}, bf16[864,192]{0,1:T(8,128)(2,1)}, u32[]{:S(2)}, u32[]{:S(2)}) collective-permute-start(bf16[864,192]{0,1:T(8,128)(2,1)} %get-tuple-element.118), channel_id=1, source_target_pairs={{0,4},{4,8},{8,12},{12,0},{1,5},{5,9},{9,13},{13,1},{2,6},{6,10},{... | collective-permute-start | bytes 995336 | tf_op jit(solution)/shard_map/ppermute | solution.py:64
  506.7 16.9 %collective-permute-start.78 = (bf16[864,192]{0,1:T(8,128)(2,1)S(1)}, bf16[864,192]{0,1:T(8,128)(2,1)S(1)}, u32[]{:S(2)}, u32[]{:S(2)}) collective-permute-start(bf16[864,192]{0,1:T(8,128)(2,1)S(1)} %get-tuple-element.90), channel_id=1, source_target_pairs={{0,2},{1,3},{2,0},{3,1},{4,6},{5,7},{6,4},{7,5},{8,10},{9,11},{10,... | collective-permute-start | bytes 995336 | tf_op jit(solution)/shard_map/ppermute | solution.py:59
  571.6 17.3 %collective-permute-start.93 = (f32[768,192]{0,1:T(8,128)}, f32[768,192]{0,1:T(8,128)S(1)}, u32[]{:S(2)}, u32[]{:S(2)}) collective-permute-start(f32[768,192]{0,1:T(8,128)} %dynamic_update_slice.183), channel_id=1, source_target_pairs={{0,3},{1,2},{2,1},{3,0},{4,7},{5,6},{6,5},{7,4},{8,11},{9,10},{10,... | collective-permute-start | bytes 1769480 | tf_op jit(solution)/shard_map/ppermute | solution.py:59
  572.8 27.8 %collective-permute-start.92 = (f32[768,192]{0,1:T(8,128)}, f32[768,192]{0,1:T(8,128)S(1)}, u32[]{:S(2)}, u32[]{:S(2)}) collective-permute-start(f32[768,192]{0,1:T(8,128)} %dynamic_update_slice.183), channel_id=1, source_target_pairs={{0,2},{1,3},{2,0},{3,1},{4,6},{5,7},{6,4},{7,5},{8,10},{9,11},{10,... | collective-permute-start | bytes 1769480 | tf_op jit(solution)/shard_map/ppermute | solution.py:59
  573.9 26.7 %collective-permute-start.91 = (f32[768,192]{0,1:T(8,128)}, f32[768,192]{0,1:T(8,128)S(1)}, u32[]{:S(2)}, u32[]{:S(2)}) collective-permute-start(f32[768,192]{0,1:T(8,128)} %dynamic_update_slice.183), channel_id=1, source_target_pairs={{0,1},{1,0},{2,3},{3,2},{4,5},{5,4},{6,7},{7,6},{8,9},{9,8},{10,11... | collective-permute-start | bytes 1769480 | tf_op jit(solution)/shard_map/ppermute | solution.py:59
  581.3 75.8 %collective-permute-start.55 = (bf16[1728,192]{0,1:T(8,128)(2,1)}, bf16[1728,192]{0,1:T(8,128)(2,1)}, u32[]{:S(2)}, u32[]{:S(2)}) collective-permute-start(bf16[1728,192]{0,1:T(8,128)(2,1)} %get-tuple-element.104), channel_id=1, source_target_pairs={{0,12},{4,0},{8,4},{12,8},{1,13},{5,1},{9,5},{13,9},{2,14},{6,2},{... | collective-permute-start | bytes 1990664 | tf_op jit(solution)/shard_map/ppermute | solution.py:64
  585.3 71.8 %collective-permute-start.54 = (bf16[1728,192]{0,1:T(8,128)(2,1)}, bf16[1728,192]{0,1:T(8,128)(2,1)}, u32[]{:S(2)}, u32[]{:S(2)}) collective-permute-start(bf16[1728,192]{0,1:T(8,128)(2,1)} %get-tuple-element.105), channel_id=1, source_target_pairs={{0,8},{4,12},{8,0},{12,4},{1,9},{5,13},{9,1},{13,5},{2,10},{6,14},... | collective-permute-start | bytes 1990664 | tf_op jit(solution)/shard_map/ppermute | solution.py:64
  588.9 68.2 %collective-permute-start.53 = (bf16[1728,192]{0,1:T(8,128)(2,1)}, bf16[1728,192]{0,1:T(8,128)(2,1)}, u32[]{:S(2)}, u32[]{:S(2)}) collective-permute-start(bf16[1728,192]{0,1:T(8,128)(2,1)} %get-tuple-element.103), channel_id=1, source_target_pairs={{0,4},{4,8},{8,12},{12,0},{1,5},{5,9},{9,13},{13,1},{2,6},{6,10},{... | collective-permute-start | bytes 1990664 | tf_op jit(solution)/shard_map/ppermute | solution.py:64
  660.6 19.3 %collective-permute-start.58 = (bf16[1728,192]{0,1:T(8,128)(2,1)S(1)}, bf16[1728,192]{0,1:T(8,128)(2,1)}, u32[]{:S(2)}, u32[]{:S(2)}) collective-permute-start(bf16[1728,192]{0,1:T(8,128)(2,1)S(1)} %get-tuple-element.92), channel_id=1, source_target_pairs={{0,3},{1,2},{2,1},{3,0},{4,7},{5,6},{6,5},{7,4},{8,11},{9,10},{10,... | collective-permute-start | bytes 1990664 | tf_op jit(solution)/shard_map/ppermute | solution.py:59
  664.9 28.7 %collective-permute-start.57 = (bf16[1728,192]{0,1:T(8,128)(2,1)S(1)}, bf16[1728,192]{0,1:T(8,128)(2,1)S(1)}, u32[]{:S(2)}, u32[]{:S(2)}) collective-permute-start(bf16[1728,192]{0,1:T(8,128)(2,1)S(1)} %get-tuple-element.92), channel_id=1, source_target_pairs={{0,2},{1,3},{2,0},{3,1},{4,6},{5,7},{6,4},{7,5},{8,10},{9,11},{10,... | collective-permute-start | bytes 1990664 | tf_op jit(solution)/shard_map/ppermute | solution.py:59
  666.0 28.0 %collective-permute-start.56 = (bf16[1728,192]{0,1:T(8,128)(2,1)S(1)}, bf16[1728,192]{0,1:T(8,128)(2,1)S(1)}, u32[]{:S(2)}, u32[]{:S(2)}) collective-permute-start(bf16[1728,192]{0,1:T(8,128)(2,1)S(1)} %get-tuple-element.92), channel_id=1, source_target_pairs={{0,1},{1,0},{2,3},{3,2},{4,5},{5,4},{6,7},{7,6},{8,9},{9,8},{10,11... | collective-permute-start | bytes 1990664 | tf_op jit(solution)/shard_map/ppermute | solution.py:59
  748.6 17.4 %collective-permute-start.72 = (f32[768,192]{0,1:T(8,128)}, f32[768,192]{0,1:T(8,128)S(1)}, u32[]{:S(2)}, u32[]{:S(2)}) collective-permute-start(f32[768,192]{0,1:T(8,128)} %dynamic_update_slice.175), channel_id=1, source_target_pairs={{0,3},{1,2},{2,1},{3,0},{4,7},{5,6},{6,5},{7,4},{8,11},{9,10},{10,... | collective-permute-start | bytes 1769480 | tf_op jit(solution)/shard_map/ppermute | solution.py:59
  749.9 27.8 %collective-permute-start.71 = (f32[768,192]{0,1:T(8,128)}, f32[768,192]{0,1:T(8,128)S(1)}, u32[]{:S(2)}, u32[]{:S(2)}) collective-permute-start(f32[768,192]{0,1:T(8,128)} %dynamic_update_slice.175), channel_id=1, source_target_pairs={{0,2},{1,3},{2,0},{3,1},{4,6},{5,7},{6,4},{7,5},{8,10},{9,11},{10,... | collective-permute-start | bytes 1769480 | tf_op jit(solution)/shard_map/ppermute | solution.py:59
  751.0 26.7 %collective-permute-start.70 = (f32[768,192]{0,1:T(8,128)}, f32[768,192]{0,1:T(8,128)S(1)}, u32[]{:S(2)}, u32[]{:S(2)}) collective-permute-start(f32[768,192]{0,1:T(8,128)} %dynamic_update_slice.175), channel_id=1, source_target_pairs={{0,1},{1,0},{2,3},{3,2},{4,5},{5,4},{6,7},{7,6},{8,9},{9,8},{10,11... | collective-permute-start | bytes 1769480 | tf_op jit(solution)/shard_map/ppermute | solution.py:59
  (228 other events, 2816.2 us)

commit v2 on v1

--- a/solution.py
+++ b/solution.py
@@ -30,11 +30,11 @@
 ADAM_RATE = 0.05
 COLOUR_RATE = 0.01
 PAD = 8
-VMEM_BYTES = 48 * 1024 * 1024
-
-
-def kernel_params():
-    return pltpu.CompilerParams(vmem_limit_bytes=VMEM_BYTES)
+MIB = 1024 * 1024
+
+
+def kernel_params(size=20):
+    return pltpu.CompilerParams(vmem_limit_bytes=size * MIB)
 
 
 def whole(shape):
@@ -72,51 +72,87 @@
     return sum(row_gather(value))
 
 
+def row_exchange(pieces):
+    return [pieces[0]] + [axis_swap(pieces[k], "row", k) for k in range(1, len(pieces))]
+
+
 def row_scatter(pieces):
-    arrived = [axis_swap(pieces[k], "row", k) for k in range(1, len(pieces))]
-    total = pieces[0].astype(f32)
-    for piece in arrived:
-        total = total + piece.astype(f32)
-    return total
+    return sum(piece.astype(f32) for piece in row_exchange(pieces))
+
+
+GROUP = ("half", "dp")
 
 
 def group_sum(value):
-    value = value + axis_swap(value, "half", 1)
-    return sum([value] + [axis_shift(value, "dp", k) for k in range(1, lax.axis_size("dp"))])
+    return lax.psum(value, GROUP)
 
 
 def group_pile(value):
-    parts = [value] + [axis_shift(value, "dp", k) for k in range(1, lax.axis_size("dp"))]
-    return jnp.concatenate(parts + [axis_swap(part, "half", 1) for part in parts], axis=0)
+    return lax.all_gather(value, GROUP, axis=0, tiled=True)
 
 
 def group_gather(value):
+    return lax.all_gather(value, GROUP, axis=0, tiled=True)
+
+
+def group_scatter(value):
+    return lax.psum_scatter(value, GROUP, scatter_dimension=0, tiled=True).astype(f32)
+
+
+def spread(value, axis):
+    n = math.prod(lax.axis_size(name) for name in axis)
+    return lax.all_to_all(jnp.broadcast_to(value[None], (n,) + value.shape), axis, 0, 0)
+
+
+def near_sum(value):
+    return jnp.sum(spread(value, GROUP), axis=0)
+
+
+def after(value, *others):
+    return lax.optimization_barrier((value,) + others)[0]
+
+
+def step_below(value, s):
     n = lax.axis_size("dp")
-    h, z = lax.axis_index("half"), lax.axis_index("dp")
-    rows = value.shape[0]
-    full = jnp.zeros((2 * n * rows,) + value.shape[1:], value.dtype)
-    for k in range(n):
-        part = value if k == 0 else axis_shift(value, "dp", k)
-        other = axis_swap(part, "half", 1)
-        place = lax.rem(z + n - k, n)
-        full = lax.dynamic_update_slice_in_dim(full, part, (h * n + place) * rows, 0)
-        full = lax.dynamic_update_slice_in_dim(full, other, ((1 - h) * n + place) * rows, 0)
-    return full
-
-
-def group_scatter(value):
+    return lax.ppermute(value, "dp", [(i, i + 1) for i in range(s - 1, n - 1)])
+
+
+def step_above(value, s):
     n = lax.axis_size("dp")
-    h, z = lax.axis_index("half"), lax.axis_index("dp")
-    halves = value.reshape((2, n, value.shape[0] // (2 * n)) + value.shape[1:])
-    kept = lax.dynamic_index_in_dim(halves, h, 0, keepdims=False)
-    sent = lax.dynamic_index_in_dim(halves, 1 - h, 0, keepdims=False)
-    kept = kept.astype(f32) + axis_swap(sent, "half", 1).astype(f32)
-    wire = kept.astype(value.dtype)
-    total = lax.dynamic_index_in_dim(kept, z, 0, keepdims=False)
+    return lax.ppermute(value, "dp", [(i, i - 1) for i in range(1, n - s + 1)])
+
+
+def straight(value):
+    return [value] + [axis_shift(value, "dp", k) for k in range(1, lax.axis_size("dp"))]
+
+
+def both_cores(pieces):
+    return pieces + [axis_swap(piece, "half", 1) for piece in pieces]
+
+
+def placed_in_order(pieces):
+    n = len(pieces)
+    turned = [pieces[0]] + pieces[:0:-1]
+    piled = jnp.stack(turned + turned[:-1], axis=0)
+    start = lax.rem(n - lax.axis_index("dp"), n)
+    return lax.dynamic_slice_in_dim(piled, start, n, 0)
+
+
+def near_halves(value):
+    h = lax.axis_index("half")
+    kept = lax.dynamic_index_in_dim(value, h, 0, keepdims=False)
+    sent = lax.dynamic_index_in_dim(value, 1 - h, 0, keepdims=False)
+    return kept.astype(f32) + axis_swap(sent, "half", 1).astype(f32)
+
+
+def near_blocks(kept, wire):
+    n = lax.axis_size("dp")
+    z = lax.axis_index("dp")
+    pieces = [lax.dynamic_index_in_dim(kept, z, 0, keepdims=False)]
     for k in range(1, n):
         block = lax.dynamic_index_in_dim(wire, lax.rem(z + k, n), 0, keepdims=False)
-        total = total + axis_shift(block, "dp", k).astype(f32)
-    return total
+        pieces.append(axis_shift(block, "dp", k))
+    return pieces
 
 
 def raise_two(values):
@@ -150,7 +186,7 @@
         acc_ref[...] = jnp.zeros_like(acc_ref)
 
     product = sum(
-        times(x_ref[...], w_ref[0, owned_rows(row_ref, k, x_ref.shape[1]), :])
+        times(x_ref[0], w_ref[0, owned_rows(row_ref, k, x_ref.shape[2]), :])
         for k, x_ref in enumerate(blocks)
     )
     raised = raise_two(product.reshape(h2 // 2, w2 // 2, n, c))
@@ -205,7 +241,7 @@
         for k in range(count):
             pad_ref[k, 1 : h2 + 1, 1 : w2 + 1] = blocks[k][...]
         skipped = sum(
-            times(x_ref[...], skip_ref[owned_rows(row_ref, k, x_ref.shape[1]), :])
+            times(x_ref[x_ref.shape[0] - 1], skip_ref[owned_rows(row_ref, k, x_ref.shape[2]), :])
             for k, x_ref in enumerate(raws)
         )
         sum_ref[...] = raise_two(skipped.reshape(h2 // 2, w2 // 2, n, c))
@@ -257,7 +293,7 @@
                 pltpu.VMEM((h2 + 2, w2 + 2, n, c), bf16),
             ],
         ),
-        compiler_params=kernel_params(),
+        compiler_params=kernel_params(28),
         name="conv_two",
     )(row, *blocks, *raws, weight, skip, colour)
 
@@ -325,7 +361,7 @@
             pltpu.VMEM((h2 + 2, w2 + 2, n, PAD), bf16),
             pltpu.VMEM((h2 + 2, w2 + 2, n, c), bf16),
         ],
-        compiler_params=kernel_params(),
+        compiler_params=kernel_params(28),
         name="critic",
     )(picture, disc_first, disc_second, disc_skip, head, counted)
 
@@ -381,7 +417,7 @@
             + tuple(whole((rows, c)) for _ in range(count)),
             scratch_shapes=[pltpu.VMEM((count, rows, c), f32)],
         ),
-        compiler_params=kernel_params(),
+        compiler_params=kernel_params(28),
         name="back_two",
     )(row, grads, summed, active, colour, weight)
 
@@ -421,7 +457,7 @@
             in_specs=[whole(gpad.shape)] + [whole(b.shape) for b in blocks + raws],
             out_specs=(pl.BlockSpec((1, tall, c), lambda t, r: (t, 0, 0)), whole((wide, c))),
         ),
-        compiler_params=kernel_params(),
+        compiler_params=kernel_params(28),
         name="weight_two",
     )(row, gpad, *blocks, *raws)
 
@@ -476,7 +512,7 @@
                 pltpu.VMEM((count, rows, size), f32),
             ],
         ),
-        compiler_params=kernel_params(),
+        compiler_params=kernel_params(28),
         name="back_one",
     )(row, grads, weight, *blocks)
 
@@ -562,6 +598,461 @@
     return master - MUON_RATE * (factor * direction + DECAY * master), moment_new
 
 
+def transposed(values):
+    return jnp.transpose(values.astype(f32)).astype(values.dtype)
+
+
+def place_kernel(count, sizes, index_ref, mine_ref, other_ref, *refs):
+    outs = refs[-len(sizes) :]
+
+    def write(values):
+        turned = jnp.transpose(values.astype(f32)).astype(bf16)
+        start = 0
+        for size, out_ref in zip(sizes, outs):
+            out_ref[...] = turned[start : start + size]
+            start += size
+
+    @pl.when(pl.program_id(0) < count)
+    def _():
+        write(mine_ref[0])
+
+    @pl.when(pl.program_id(0) >= count)
+    def _():
+        write(other_ref[0])
+
+
+def place(held, index, mine, other, sizes):
+    count, c, wide = mine.shape
+    groups = 2 * lax.axis_size("dp")
+    given = [] if held is None else list(held)
+    return pl.pallas_call(
+        functools.partial(place_kernel, count, sizes),
+        out_shape=tuple(jax.ShapeDtypeStruct((groups * size, c), bf16) for size in sizes),
+        grid_spec=pltpu.PrefetchScalarGridSpec(
+            num_scalar_prefetch=1,
+            grid=(2 * count,),
+            in_specs=[
+                pl.BlockSpec((1, c, wide), lambda t, r: (jnp.minimum(t, count - 1), 0, 0)),
+                pl.BlockSpec((1, c, wide), lambda t, r: (jnp.maximum(t - count, 0), 0, 0)),
+            ]
+            + [pl.BlockSpec(memory_space=pl.ANY) for _ in given],
+            out_specs=tuple(pl.BlockSpec((size, c), lambda t, r: (r[t], 0)) for size in sizes),
+        ),
+        input_output_aliases={3 + i: i for i in range(len(given))},
+        compiler_params=kernel_params(),
+        name="place",
+    )(jnp.stack(index).astype(jnp.int32), mine, other, *given)
+
+
+def place_cores(held, spots, mine, sizes):
+    n = lax.axis_size("dp")
+    h = lax.axis_index("half")
+    index = [h * n + spot for spot in spots] + [(1 - h) * n + spot for spot in spots]
+    return place(held, index, mine, axis_swap(mine, "half", 1), sizes)
+
+
+def weight_one_kernel(groups, where_ref, inverse_ref, *refs):
+    pieces = refs[:groups]
+    all_ref, moment_ref, out_ref, low_ref, pad_ref, pool_ref, grads, inputs_ref, sem = refs[groups:]
+    copies = [
+        pltpu.make_async_copy(piece, grads.at[g], sem.at[g]) for g, piece in enumerate(pieces)
+    ]
+    copies.append(pltpu.make_async_copy(all_ref, inputs_ref, sem.at[groups]))
+    for copy in copies:
+        copy.start()
+    h2, w2, n, c = grads.shape[1:]
+    size = h2 * w2 * n // 4
+    row, d = where_ref[0], where_ref[1] * (groups // 2) + where_ref[2]
+    owners = []
+    for side in range(2):
+        for k in range(groups // 2):
+            spot = lax.rem(where_ref[2] + groups // 2 - k, groups // 2)
+            owners.append((where_ref[1] if side == 0 else 1 - where_ref[1]) * (groups // 2) + spot)
+    pad_ref[...] = jnp.zeros_like(pad_ref)
+    for g in range(groups):
+        copies[g].wait()
+        pad_ref[1 : h2 + 1, 1 : w2 + 1] = grads[g]
+        for j in range(2):
+            dy, dx = lax.div(d + j, 3), lax.rem(d + j, 3)
+            shifted = pad_ref[pl.ds(2 - dy, h2), pl.ds(2 - dx, w2)].astype(f32)
+            pool_ref[j, g * size : (g + 1) * size, :] = flat(sum_two(shifted)).astype(bf16)
+    copies[groups].wait()
+    inverse = inverse_ref[0, 0]
+    for q in range(groups + 1):
+        i = lax.rem(d + q, groups)
+        j = lax.div(d + q, groups)
+        start = lax.bitwise_xor(row, lax.div(i, 2)) * (2 * c) + lax.rem(i, 2) * c
+        start = pl.multiple_of(start, c)
+        total = sum(
+            times(inputs_ref[owners[g], pl.ds(start, c), :], pool_ref[j, g * size : (g + 1) * size, :])
+            for g in range(groups)
+        )
+        span = slice(q * c, (q + 1) * c)
+        moment = MOMENTUM * moment_ref[:, span] + jnp.transpose(total) * inverse
+        out_ref[:, span] = moment
+        low_ref[:, span] = moment.astype(bf16)
+
+
+def weight_one_moment(where, inverse, grads, inputs, moment):
+    h2, w2, n, c = grads[0].shape
+    groups = len(grads)
+    vmem = pl.BlockSpec(memory_space=pltpu.VMEM)
+    smem = pl.BlockSpec(memory_space=pltpu.SMEM)
+    flops = 2 * moment.shape[1] * c * groups * h2 * w2 * n // 4
+    return pl.pallas_call(
+        functools.partial(weight_one_kernel, groups),
+        out_shape=(
+            jax.ShapeDtypeStruct(moment.shape, f32),
+            jax.ShapeDtypeStruct(moment.shape, bf16),
+        ),
+        in_specs=[smem, smem] + [pl.BlockSpec(memory_space=pl.ANY)] * (groups + 1) + [vmem],
+        out_specs=(vmem, vmem),
+        scratch_shapes=[
+            pltpu.VMEM((h2 + 2, w2 + 2, n, c), bf16),
+            pltpu.VMEM((2, groups * h2 * w2 * n // 4, c), bf16),
+            pltpu.VMEM((groups,) + grads[0].shape, bf16),
+            pltpu.VMEM(inputs.shape, bf16),
+            pltpu.SemaphoreType.DMA((groups + 1,)),
+        ],
+        compiler_params=kernel_params(28),
+        cost_estimate=pl.CostEstimate(flops=4 * flops, bytes_accessed=0, transcendentals=0),
+        name="weight_one",
+    )(where, inverse, *grads, inputs, moment)
+
+
+def weight_pack_kernel(count, row_ref, gpad_ref, *refs):
+    blocks, raws, (out_ref, tall_ref) = refs[:count], refs[count : 2 * count], refs[2 * count :]
+    h2, w2, n, c = (gpad_ref.shape[0] - 2, gpad_ref.shape[1] - 2) + gpad_ref.shape[2:]
+    groups = out_ref.shape[0]
+    unit = count * c // groups
+    half = unit // 2
+    t = pl.program_id(0)
+    dy, dx = lax.div(t, 3), lax.rem(t, 3)
+    shifted = flat(gpad_ref[pl.ds(2 - dy, h2), pl.ds(2 - dx, w2)])
+    for k in range(count):
+        tall_ref[owned_rows(row_ref, k, c), :] = times(blocks[k][...], shifted)
+    for i in range(groups):
+        rows = tall_ref[i * unit : (i + 1) * unit, :]
+        u = groups * t + i
+        packed = jnp.concatenate([rows[:half], rows[half:]], axis=1).astype(bf16)
+        spot = pl.multiple_of(lax.rem(u, groups + 1) * half, half)
+        out_ref[lax.div(u, groups + 1), pl.ds(spot, half), :] = packed
+
+    @pl.when(t == 8)
+    def _():
+        phases = gpad_ref[1 : h2 + 1, 1 : w2 + 1].reshape(h2 // 2, 2, w2 // 2, 2, n, c)
+        size = raws[0].shape[0]
+        each = count * size // groups
+        for k in range(count):
+            block = sum(
+                times(raws[k][...], flat(phases[:, a, :, b])) for a in range(2) for b in range(2)
+            )
+            for m in range(size // each):
+                rows = block[m * each : (m + 1) * each]
+                packed = jnp.concatenate([rows[: each // 2], rows[each // 2 :]], axis=1)
+                spot = lax.bitwise_xor(row_ref[0], k) * (size // each) + m
+                out_ref[spot, (groups + 1) * half :, :] = packed.astype(bf16)
+
+
+def weight_pack(row, gpad, blocks, raws, groups):
+    c = gpad.shape[-1]
+    count = len(blocks)
+    tall, wide = count * blocks[0].shape[0], count * raws[0].shape[0]
+    shape = (groups, (9 * tall + wide) // (2 * groups), 2 * c)
+    flops = 2 * 9 * tall * c * blocks[0].shape[1]
+    return pl.pallas_call(
+        functools.partial(weight_pack_kernel, count),
+        out_shape=jax.ShapeDtypeStruct(shape, bf16),
+        grid_spec=pltpu.PrefetchScalarGridSpec(
+            num_scalar_prefetch=1,
+            grid=(9,),
+            in_specs=[whole(gpad.shape)] + [whole(b.shape) for b in blocks + raws],
+            out_specs=whole(shape),
+            scratch_shapes=[pltpu.VMEM((tall, c), f32)],
+        ),
+        compiler_params=kernel_params(28),
+        cost_estimate=pl.CostEstimate(flops=3 * flops, bytes_accessed=0, transcendentals=0),
+        name="weight_two",
+    )(row, gpad, *blocks, *raws)
+
+
+def moments_kernel(count, inverse_ref, *refs):
+    pieces = refs[:count]
+    tall_ref, skip_ref, tall_out, skip_out, low_ref = refs[count:]
+    c, size = tall_ref.shape
+    total = pieces[0][...].astype(f32)
+    for piece in pieces[1:]:
+        total = total + piece[...].astype(f32)
+    total = total * inverse_ref[0, 0]
+    units = 9
+    half = size // (2 * units)
+    for q in range(units):
+        rows = total[q * half : (q + 1) * half]
+        rows = jnp.concatenate([rows[:, :c], rows[:, c:]], axis=0)
+        span = slice(2 * q * half, 2 * (q + 1) * half)
+        moment = MOMENTUM * tall_ref[:, span] + jnp.transpose(rows)
+        tall_out[:, span] = moment
+        low_ref[:, span] = moment.astype(bf16)
+    rows = total[units * half :]
+    rows = jnp.concatenate([rows[:, :c], rows[:, c:]], axis=0)
+    moment = MOMENTUM * skip_ref[...] + jnp.transpose(rows)
+    skip_out[...] = moment
+    low_ref[:, size:] = moment.astype(bf16)
+
+
+def moments_two(inverse, pieces, tall, skip):
+    vmem = pl.BlockSpec(memory_space=pltpu.VMEM)
+    return pl.pallas_call(
+        functools.partial(moments_kernel, len(pieces)),
+        out_shape=(
+            jax.ShapeDtypeStruct(tall.shape, f32),
+            jax.ShapeDtypeStruct(skip.shape, f32),
+            jax.ShapeDtypeStruct((tall.shape[0], tall.shape[1] + skip.shape[1]), bf16),
+        ),
+        in_specs=[pl.BlockSpec(memory_space=pltpu.SMEM)] + [vmem] * (len(pieces) + 2),
+        out_specs=(vmem, vmem, vmem),
+        compiler_params=kernel_params(),
+        name="moments",
+    )(inverse, *pieces, tall, skip)
+
+
+def gram_kernel(count, spans, row_ref, *refs):
+    pieces, out_ref, hold_ref = refs[:count], refs[count], refs[count + 1]
+    for m, (start, stop) in enumerate(spans):
+        owned = pieces[0][:, start:stop]
+        for k in range(count):
+            hold_ref[k] = contract_last(owned, pieces[k][:, start:stop])
+        out_ref[m] = jnp.concatenate(
+            [hold_ref[lax.bitwise_xor(row_ref[0], j)] for j in range(count)], axis=1
+        )
+
+
+def gram_rows(row, pieces, spans):
+    c = pieces[0].shape[0]
+    count = len(pieces)
+    vmem = pl.BlockSpec(memory_space=pltpu.VMEM)
+    return pl.pallas_call(
+        functools.partial(gram_kernel, count, spans),
+        out_shape=jax.ShapeDtypeStruct((len(spans), c, count * c), f32),
+        in_specs=[pl.BlockSpec(memory_space=pltpu.SMEM)] + [vmem] * count,
+        out_specs=vmem,
+        scratch_shapes=[pltpu.VMEM((count, c, c), f32)],
+        compiler_params=kernel_params(),
+        cost_estimate=pl.CostEstimate(
+            flops=6 * count * c * c * pieces[0].shape[1], bytes_accessed=0, transcendentals=0
+        ),
+        name="gram",
+    )(row, *pieces)
+
+
+def gram_terms(halves):
+    kept = near_halves(halves)
+    return near_blocks(kept, kept)
+
+
+def gram_total(terms):
+    return placed_in_order(straight(sum(terms)))
+
+
+def newton_kernel(count, sides, where_ref, *refs):
+    pieces = refs[: sides * count]
+    out_ref, a_ref, ah, al, ph, pl_low, th, tl = refs[sides * count :]
+    size = a_ref.shape[0]
+    own = size // count
+    block = size // 3
+    row, h = where_ref[0], where_ref[1]
+    for q in range(count):
+        for side in range(sides):
+            piece = pieces[side * count + q]
+            s = piece.shape[2]
+            half = 0 if sides == 1 else (h if side == 0 else 1 - h)
+            for p in range(piece.shape[0]):
+                start = lax.bitwise_xor(row, q) * own + half * (own // 2) + p * s
+                a_ref[pl.ds(pl.multiple_of(start, s), s), :] = piece[p, 0]
+
+    def eye(shape, offset):
+        rows = lax.broadcasted_iota(jnp.int32, shape, 0) + offset
+        return rows == lax.broadcasted_iota(jnp.int32, shape, 1)
+
+    whole_gram = a_ref[...]
+    trace = jnp.sum(jnp.where(eye(whole_gram.shape, 0), whole_gram, 0.0), keepdims=True)
+    scale = lax.rsqrt(trace + NEWTON_EPSILON)
+    a_ref[...] = whole_gram * (scale * scale)
+
+    def split(values):
+        top = values.astype(bf16)
+        return top, (values - top.astype(f32)).astype(bf16)
+
+    def three(xh, xl, yh, yl):
+        return times(xh, yh) + (times(xh, yl) + times(xl, yh))
+
+    spans = [slice(i * block, (i + 1) * block) for i in range(3)]
+
+    def symmetric(xh, xl, yh, yl, write):
+        for i in range(3):
+            for j in range(i, 3):
+                a, b = spans[i], spans[j]
+                value = three(xh[a, :], xl[a, :], yh[:, b], yl[:, b])
+                write(i, j, value)
+
+    def store(high_ref, low_ref, i, j, value):
+        top, low = split(value)
+        high_ref[spans[i], spans[j]] = top
+        low_ref[spans[i], spans[j]] = low
+        if i != j:
+            turned = jnp.transpose(value)
+            top, low = split(turned)
+            high_ref[spans[j], spans[i]] = top
+            low_ref[spans[j], spans[i]] = low
+
+    top, low = split(a_ref[...])
+    ah[...] = top
+    al[...] = low
+
+    def step(k, carry):
+        hp, lp = ph.at[k], pl_low.at[k]
+
+        def write_map(i, j, value):
+            value = NS_COEF[1] * a_ref[spans[i], spans[j]] + NS_COEF[2] * value
+            if i == j:
+                value = value + jnp.where(eye(value.shape, 0), NS_COEF[0], 0.0)
+            store(hp, lp, i, j, value)
+
+        symmetric(ah, al, ah, al, write_map)
+        symmetric(ah, al, hp, lp, functools.partial(store, th, tl))
+
+        def write_gram(i, j, value):
+            a_ref[spans[i], spans[j]] = value
+            store(ah, al, i, j, value)
+            if i != j:
+                a_ref[spans[j], spans[i]] = jnp.transpose(value)
+
+        symmetric(hp, lp, th, tl, write_gram)
+        return carry
+
+    lax.fori_loop(0, NS_ITERS - 1, step, 0)
+    mine = pl.ds(pl.multiple_of(row * own, own), own)
+    last = a_ref[mine, :]
+    columns = NS_COEF[1] * last + NS_COEF[2] * three(ah[mine, :], al[mine, :], ah[...], al[...])
+    columns = columns + jnp.where(eye(columns.shape, row * own), NS_COEF[0], 0.0)
+
+    def fold(k, columns):
+        high_part, low_part = split(columns)
+        k = NS_ITERS - 2 - k
+        return three(high_part, low_part, ph[k], pl_low[k])
+
+    columns = lax.fori_loop(0, NS_ITERS - 1, fold, columns) * scale
+    for j in range(count):
+        out_ref[0, j] = columns[:, j * own : (j + 1) * own].astype(bf16)
+
+
+def newton(where, pieces, count):
+    sides = len(pieces) // count
+    n, m, s, size = pieces[0].shape
+    own = size // count
+    square = (size, size)
+    maps = (NS_ITERS - 1,) + square
+    return pl.pallas_call(
+        functools.partial(newton_kernel, count, sides),
+        out_shape=jax.ShapeDtypeStruct((m, count, own, own), bf16),
+        grid_spec=pltpu.PrefetchScalarGridSpec(
+            num_scalar_prefetch=1,
+            grid=(m,),
+            in_specs=[pl.BlockSpec((n, 1, s, size), lambda t, r: (0, t, 0, 0)) for _ in pieces],
+            out_specs=pl.BlockSpec((1, count, own, own), lambda t, r: (t, 0, 0, 0)),
+            scratch_shapes=[
+                pltpu.VMEM(square, f32),
+                pltpu.VMEM(square, bf16),
+                pltpu.VMEM(square, bf16),
+                pltpu.VMEM(maps, bf16),
+                pltpu.VMEM(maps, bf16),
+                pltpu.VMEM(square, bf16),
+                pltpu.VMEM(square, bf16),
+            ],
+        ),
+        compiler_params=kernel_params(36),
+        cost_estimate=pl.CostEstimate(
+            flops=m * 64 * size**3, bytes_accessed=0, transcendentals=0
+        ),
+        name="newton",
+    )(where, *pieces)
+
+
+def update_kernel(count, spans, factors, row_ref, map_ref, *refs):
+    pieces, masters, outs = refs[:count], refs[count : count + len(spans)], refs[count + len(spans) :]
+    for m, (start, stop) in enumerate(spans):
+        direction = sum(
+            times(map_ref[m, lax.bitwise_xor(row_ref[0], k)], pieces[k][:, start:stop])
+            for k in range(count)
+        )
+        master = masters[m][...]
+        outs[m][...] = master - MUON_RATE * (factors[m] * direction + DECAY * master)
+
+
+def update(row, maps, pieces, masters, spans, factors):
+    count = len(pieces)
+    vmem = pl.BlockSpec(memory_space=pltpu.VMEM)
+    return pl.pallas_call(
+        functools.partial(update_kernel, count, spans, factors),
+        out_shape=tuple(jax.ShapeDtypeStruct(master.shape, f32) for master in masters),
+        in_specs=[pl.BlockSpec(memory_space=pltpu.SMEM)] + [vmem] * (1 + count + len(masters)),
+        out_specs=(vmem,) * len(masters),
+        compiler_params=kernel_params(),
+        name="update",
+    )(row, maps, *pieces, *masters)
+
+
+def back_in_kernel(count, row_ref, g_ref, w_ref, *refs):
+    outs, (pad_ref, acc_ref) = refs[:count], refs[count:]
+    h2, w2, n, c = g_ref.shape
+    size = outs[0].shape[1]
+    t = pl.program_id(0)
+    dy, dx = lax.div(t, 3), lax.rem(t, 3)
+
+    @pl.when(t == 0)
+    def _():
+        pad_ref[...] = jnp.zeros_like(pad_ref)
+        pad_ref[1 : h2 + 1, 1 : w2 + 1] = g_ref[...]
+        acc_ref[...] = jnp.zeros_like(acc_ref)
+
+    shifted = pad_ref[pl.ds(2 - dy, h2), pl.ds(2 - dx, w2)].astype(f32)
+    pooled = flat(sum_two(shifted)).astype(bf16)
+    for k in range(count):
+        acc_ref[k] += contract_last(pooled, w_ref[0, owned_rows(row_ref, k, size), :])
+
+    @pl.when(t == 8)
+    def _():
+        for k in range(count):
+            outs[k][...] = acc_ref[k].astype(bf16)
+
+
+def back_in(row, grads, weight, count):
+    h2, w2, n, c = grads.shape
+    size, rows = weight.shape[1] // count, h2 * w2 * n // 4
+    return pl.pallas_call(
+        functools.partial(back_in_kernel, count),
+        out_shape=tuple(jax.ShapeDtypeStruct((rows, size), bf16) for _ in range(count)),
+        grid_spec=pltpu.PrefetchScalarGridSpec(
+            num_scalar_prefetch=1,
+            grid=(9,),
+            in_specs=[
+                whole(grads.shape),
+                pl.BlockSpec((1,) + weight.shape[1:], lambda t, r: (t, 0, 0)),
+            ],
+            out_specs=tuple(whole((rows, size)) for _ in range(count)),
+            scratch_shapes=[
+                pltpu.VMEM((h2 + 2, w2 + 2, n, c), bf16),
+                pltpu.VMEM((count, rows, size), f32),
+            ],
+        ),
+        compiler_params=kernel_params(28),
+        cost_estimate=pl.CostEstimate(
+            flops=6 * 9 * rows * count * size * c, bytes_accessed=0, transcendentals=0
+        ),
+        name="back_one",
+    )(row, grads, weight)
+
+
 def adam_update(weight, gradient, mean_old, square_old, rate):
     mean_new = BETA_ONE * mean_old + (1.0 - BETA_ONE) * gradient
     square_new = BETA_TWO * square_old + (1.0 - BETA_TWO) * gradient * gradient
@@ -586,7 +1077,7 @@
     return jnp.sum(values.reshape(MICRO, -1, values.shape[-1]), axis=1)
 
 
-def per_device(
+def wide_device(
     features,
     noise,
     labels,
@@ -646,7 +1137,7 @@
     ones = row_gather(acted_one)
     raws = row_gather(flat(inputs))
 
-    hidden, sums_high = conv_one(row, ones, weight_one, (h, w, n))
+    hidden, sums_high = conv_one(row, [one[None] for one in ones], weight_one, (h, w, n))
     held_second, held_skip, _ = lax.optimization_barrier(
         (conv_second.astype(bf16), conv_skip.astype(bf16), weight_one[0, 0, 0])
     )
@@ -663,7 +1154,7 @@
     colour = jnp.pad(
         jnp.transpose(colour_conv, (0, 2, 1)).astype(bf16), ((0, 0), (0, PAD - 3), (0, 0))
     )
-    summed, active, picture = conv_two(row, twos, raws, weight_two, weight_skip, colour)
+    summed, active, picture = conv_two(row, twos, [one[None] for one in raws], weight_two, weight_skip, colour)
     picture = row_sum(picture)
 
     first_taps = jnp.pad(disc_first.reshape(9, 3, -1), ((0, 0), (0, PAD - 3), (0, 0)))
@@ -780,6 +1271,288 @@
     )
 
 
+def near_device(
+    features,
+    noise,
+    labels,
+    counted,
+    disc_first,
+    disc_second,
+    disc_skip,
+    disc_head,
+    disc_table,
+    conv_first,
+    conv_second,
+    conv_skip,
+    momentum_first,
+    momentum_second,
+    momentum_skip,
+    class_table,
+    table_mean,
+    table_square,
+    norm_first,
+    first_mean,
+    first_square,
+    norm_second,
+    second_mean,
+    second_square,
+    colour_conv,
+    colour_mean,
+    colour_square,
+):
+    groups = lax.axis_size("half") * lax.axis_size("dp")
+    ranks = lax.axis_size("row")
+    row = lax.axis_index("row").astype(jnp.int32).reshape(1)
+    n, h, w, c_in = features.shape
+    c_out = conv_first.shape[1]
+    count_low = float(n // MICRO * h * w * groups)
+    count_high = 4.0 * count_low
+
+    where = jnp.stack(
+        [lax.axis_index("row"), lax.axis_index("half"), lax.axis_index("dp")]
+    ).astype(jnp.int32)
+    n_dp, half, spot = lax.axis_size("dp"), lax.axis_index("half"), lax.axis_index("dp")
+    turned = conv_first.T.astype(bf16)
+    below, above = [turned, step_below(turned, 1)], [turned, step_above(turned, 1)]
+    inputs = jnp.transpose(features, (1, 2, 0, 3))
+    raw = inputs.astype(f32)
+    sums_low = jnp.concatenate(
+        [
+            per_micro(jnp.sum(raw, axis=(0, 1))),
+            per_micro(jnp.sum(raw * raw, axis=(0, 1))),
+            jnp.broadcast_to(jnp.sum(counted).astype(f32), (1, c_in)),
+        ],
+        axis=0,
+    )
+    totals_low = near_sum(sums_low)
+    below.append(step_below(below[1], 2))
+    above.append(step_above(above[1], 2))
+    fake_count = totals_low[2 * MICRO, 0]
+    inverse = 1.0 / fake_count
+
+    onehot = (labels[:, None] == jnp.arange(NCLS)[None, :]).astype(f32)
+    conds = jnp.concatenate([jnp.dot(onehot, class_table, precision=highest), noise], axis=1)
+    class_disc = jnp.dot(onehot, disc_table, precision=highest)
+    mods_one = jnp.einsum("bk,kgc->bgc", conds, norm_first, precision=highest)
+    mods_two = jnp.einsum("bk,kgc->bgc", conds, norm_second, precision=highest)
+
+    centre_one, spread_one = moments_of(totals_low[: 2 * MICRO], count_low)
+    centre_one, spread_one = per_image(centre_one, n), per_image(spread_one, n)
+    gain_one, gain_two = 1.0 + mods_one[:, 0], 1.0 + mods_two[:, 0]
+    normed_one = (raw - centre_one) * spread_one
+    pre_one = normed_one * gain_one + mods_one[:, 1]
+    acted_one = flat(jax.nn.silu(pre_one).astype(bf16))
+    pairs = row_gather(jnp.stack([acted_one, flat(inputs)], axis=0))
+    sizes = (conv_first.shape[0],)
+    down, up = lax.rem(spot + 3, 4), lax.rem(spot + 1, 4)
+    held = place_cores(None, [spot, down, up], jnp.stack([turned, below[1], above[1]]), sizes)
+    below.append(step_below(after(below[2], *pairs), 3))
+    above.append(step_above(after(above[2], *pairs), 3))
+    middle = jnp.where(spot >= 2, below[2], above[2])
+    held = place_cores(held, [lax.rem(spot + 2, 4)], middle[None], sizes)
+    below[3], above[3] = after(below[3], *held), after(above[3], *held)
+    last = jnp.where(spot == 3, below[3], jnp.where(spot == 0, above[3], turned))
+    end = jnp.where(spot == 3, 0, jnp.where(spot == 0, 3, spot))
+    (weight_one,) = place_cores(held, [end], last[None], sizes)
+    weight_one = weight_one.reshape(9, ranks * c_in, c_out)
+
+    hidden, sums_high = conv_one(row, pairs, weight_one, (h, w, n))
+    other = jnp.concatenate([conv_second.T, conv_skip.T], axis=1).astype(bf16)
+    other = jnp.pad(other, ((0, 0), (0, -other.shape[1] % 128)))
+    others = lax.all_gather(after(other, below[3], above[3]), GROUP, axis=0)
+    weight_two, weight_skip = place(
+        None,
+        list(range(groups)),
+        others[: groups // 2],
+        others[groups // 2 :],
+        (conv_second.shape[0], conv_skip.shape[0]),
+    )
+    weight_two = weight_two.reshape(9, ranks * c_out, c_out)
+    totals_high = near_sum(sums_high)
+    centre_two, spread_two = moments_of(totals_high, count_high)
+    centre_two, spread_two = per_image(centre_two, n), per_image(spread_two, n)
+    normed_two = (hidden - centre_two) * spread_two
+    pre_two = normed_two * gain_two + mods_two[:, 1]
+    acted_two = jax.nn.silu(pre_two).astype(bf16)
+    twos = row_gather(acted_two)
+    kept_pairs = [after(pair, sums_high) for pair in pairs]
+    turned = jnp.concatenate([jnp.transpose(pair[0]) for pair in kept_pairs], axis=0)
+    ones_all = lax.all_gather(after(turned, others), GROUP, axis=0)
+
+    colour = jnp.pad(
+        jnp.transpose(colour_conv, (0, 2, 1)).astype(bf16), ((0, 0), (0, PAD - 3), (0, 0))
+    )
+    summed, active, picture = conv_two(row, twos, pairs, weight_two, weight_skip, colour)
+    picture = row_sum(picture)
+
+    first_taps = jnp.pad(disc_first.reshape(9, 3, -1), ((0, 0), (0, PAD - 3), (0, 0)))
+    second_taps = disc_second.reshape(9, -1, disc_second.shape[-1])
+    skip_taps = jnp.pad(disc_skip, ((0, PAD - 3), (0, 0)))
+    mark = counted.astype(f32)[:, None]
+    grads, loss_part = critic(
+        picture,
+        first_taps,
+        second_taps,
+        skip_taps,
+        disc_head[None, :] + class_disc,
+        mark,
+        (2 * h, 2 * w, n),
+    )
+    colour_rows = jnp.pad(colour.reshape(9 * PAD, c_out), ((0, 128 - 9 * PAD), (0, 0)))
+    backs = back_two(row, grads, summed, active, colour_rows, weight_two, ranks)
+    gpad, grad_colour = backs[0], backs[1]
+    pieces = row_exchange(list(backs[2:]))
+    packed = weight_pack(
+        row,
+        gpad,
+        [jnp.transpose(flat(after(two, active))) for two in twos],
+        [jnp.transpose(after(pair, active)[1]) for pair in pairs],
+        groups,
+    )
+    kept = near_halves(packed.reshape((2, groups // 2) + packed.shape[1:]))
+    pieces[-1] = after(pieces[-1], packed)
+    grad_acted_two = sum(piece.astype(f32) for piece in pieces).reshape(hidden.shape)
+
+    grad_pre_two = grad_acted_two * silu_slope(pre_two)
+    gains_two = jnp.sum(grad_pre_two * normed_two, axis=(0, 1))
+    shifts_two = jnp.sum(grad_pre_two, axis=(0, 1))
+    back_sums = jnp.concatenate(
+        [per_micro(gain_two * shifts_two), per_micro(gain_two * gains_two)], axis=0
+    )
+    back_sums = near_sum(back_sums)
+    mean_g = per_image(back_sums[:MICRO] / count_high, n)
+    mean_gy = per_image(back_sums[MICRO:] / count_high, n)
+    grad_hidden = (spread_two * (grad_pre_two * gain_two - mean_g - normed_two * mean_gy)).astype(
+        bf16
+    )
+    hidden_all = straight(grad_hidden)
+    pieces = back_in(row, after(grad_hidden, hidden_all[1]), weight_one, ranks)
+    hidden_all = both_cores(hidden_all)
+    kept = after(kept, *hidden_all)
+    shares = near_blocks(kept, kept.astype(bf16))
+    scaled = inverse.reshape(1, 1)
+    moment_one, low_one = weight_one_moment(
+        where, scaled, hidden_all, ones_all, momentum_first.T
+    )
+    one_held = row_gather(low_one)
+    one_held[1] = after(one_held[1], *shares)
+    panel = gram_rows(row, one_held, [(0, conv_first.shape[0])])
+    panel = panel.reshape(2, 4, 1, c_out // 8, -1)
+    shares[0] = after(shares[0], panel)
+    moment_two, moment_skip, low_two = moments_two(
+        scaled, shares, momentum_second.T, momentum_skip.T
+    )
+    total_one = gram_total(gram_terms(panel))
+    two_held = row_gather(low_two)
+    spans = [(0, conv_second.shape[0]), (conv_second.shape[0], low_two.shape[1])]
+    panels = gram_rows(row, [after(two_held[0], total_one)] + two_held[1:], spans)
+    total_two = gram_total(gram_terms(panels.reshape(2, 4, 1, c_out // 4, -1)))
+    grams_one = both_cores(row_gather(total_one))
+    grams_one[0] = after(grams_one[0], total_two)
+    maps_one = newton(where, grams_one, ranks)
+    factor = 0.2 * math.sqrt(max(conv_first.shape[0] * groups, c_out * ranks))
+    (first_out,) = update(
+        row, maps_one, one_held, [conv_first.T], [(0, conv_first.shape[0])], [factor]
+    )
+    grams_two = row_gather(total_two)
+    grams_two[0] = after(grams_two[0], maps_one)
+    maps_two = newton(where, grams_two, ranks)
+    other_map = axis_swap(maps_two, "half", 1)
+    maps_two = jnp.where(
+        half == 0,
+        jnp.concatenate([maps_two, other_map], axis=0),
+        jnp.concatenate([other_map, maps_two], axis=0),
+    )
+    factors = [
+        0.2 * math.sqrt(max(rows * groups, c_out * ranks))
+        for rows in (conv_second.shape[0], conv_skip.shape[0])
+    ]
+    second_out, skip_out = update(
+        row, maps_two, two_held, [conv_second.T, conv_skip.T], spans, factors
+    )
+    weights_new = (first_out.T, second_out.T, skip_out.T)
+    moments_new = (moment_one.T, moment_two.T, moment_skip.T)
+    grad_acted_one = row_scatter(list(pieces)).reshape(raw.shape)
+    grad_pre_one = grad_acted_one * silu_slope(pre_one)
+    gains_one = jnp.sum(grad_pre_one * normed_one, axis=(0, 1))
+    shifts_one = jnp.sum(grad_pre_one, axis=(0, 1))
+    grad_mods_one = jnp.stack([gains_one, shifts_one], axis=1)
+    grad_mods_two = jnp.stack([gains_two, shifts_two], axis=1)
+
+    grad_cond = jnp.einsum("bgc,kgc->bk", grad_mods_one, norm_first[:EMB], precision=highest)
+    grad_cond = grad_cond + jnp.einsum(
+        "bgc,kgc->bk", grad_mods_two, norm_second[:EMB], precision=highest
+    )
+    grad_cond = jnp.sum(spread(after(grad_cond, total_one), ("row",)), axis=0)
+
+    small = jnp.concatenate(
+        [
+            grad_colour[: 9 * PAD],
+            jnp.broadcast_to(loss_part[:1, :1], (1, c_out)),
+        ],
+        axis=0,
+    )
+
+    found = jnp.concatenate(
+        [
+            grad_mods_one.reshape(n, -1),
+            grad_mods_two.reshape(n, -1),
+            grad_cond,
+            conds,
+            labels.astype(f32)[:, None],
+        ],
+        axis=1,
+    )
+    found = jnp.pad(found, ((0, 0), (0, -found.shape[1] % 128)))
+    wide = found.shape[1]
+    extra = small.reshape(-1)
+    extra = jnp.pad(extra, (0, -extra.shape[0] % (8 * wide))).reshape(-1, wide)
+    packet = spread(after(jnp.concatenate([found, extra], axis=0), total_two), GROUP)
+    found = packet[:, :n].reshape(-1, wide)
+    small = jnp.sum(packet[:, n:], axis=0).reshape(-1)[: small.size].reshape(small.shape)
+    loss_sum = small[9 * PAD, 0]
+    g_colour = jnp.transpose(small[: 9 * PAD].reshape(9, PAD, c_out)[:, :3], (0, 2, 1))
+    cut = 2 * c_in + 2 * c_out + EMB
+    found, known = found[:, :cut], found[:, cut : cut + conds.shape[1] + 1]
+    conds_all, labels_all = known[:, :-1], known[:, -1].astype(jnp.int32)
+    onehot_all = (labels_all[:, None] == jnp.arange(NCLS)[None, :]).astype(f32)
+    cut_one, cut_two = 2 * c_in, 2 * c_in + 2 * c_out
+    g_norm = lax.dot_general(
+        conds_all,
+        found[:, :cut_two],
+        (((0,), (0,)), ((), ())),
+        precision=highest,
+        preferred_element_type=f32,
+    )
+    g_norm_one = g_norm[:, :cut_one].reshape(norm_first.shape)
+    g_norm_two = g_norm[:, cut_one:].reshape(norm_second.shape)
+    g_table = lax.dot_general(
+        onehot_all,
+        found[:, cut_two:],
+        (((0,), (0,)), ((), ())),
+        precision=highest,
+        preferred_element_type=f32,
+    )
+
+    table_new = adam_update(class_table, g_table * inverse, table_mean, table_square, ADAM_RATE)
+    first_new = adam_update(norm_first, g_norm_one * inverse, first_mean, first_square, ADAM_RATE)
+    second_new = adam_update(
+        norm_second, g_norm_two * inverse, second_mean, second_square, ADAM_RATE
+    )
+    colour_new = adam_update(
+        colour_conv, g_colour * inverse, colour_mean, colour_square, COLOUR_RATE
+    )
+    return (
+        (loss_sum, fake_count)
+        + weights_new
+        + moments_new
+        + table_new
+        + first_new
+        + second_new
+        + colour_new
+    )
+
+
 def weight_two_grads(row, gpad, twos, raws):
     turned = [jnp.transpose(flat(two)) for two in twos]
     return weight_two(row, gpad, turned, [jnp.transpose(one) for one in raws])
@@ -795,8 +1568,9 @@
         + (P(None, None, "row"),) * 6
         + (P(None, "row", None),) * 3
     )
+    near = mesh.shape["dp"] == 4 and mesh.shape["half"] == 2 and mesh.shape["row"] == 4
     return jax.shard_map(
-        per_device,
+        near_device if near else wide_device,
         mesh=mesh,
         in_specs=placed,
         out_specs=(P(), P())

time: 861 us -> 555 us (0.64)
  matrix products: 201 us -> 6.87 us
  local copies, waits for them, and re-layouts: 183 us -> 75.6 us
  Pallas kernels: 55.7 us -> 136 us
  starting transfers between devices: 153 us -> 92.6 us
  waiting for transfers between devices: 199 us -> 172 us
  other arithmetic: 54.2 us -> 36 us
  blocking collectives: 0 us -> 10.2 us
  between operations: 7.49 us -> 17.5 us
    dot_general x83 -> x8, matrix products: 201 us -> 6.87 us  [the longest x1 3.49 us: near_device(): lax.dot_general(onehot_all, found[:, cut_two:], (((0,), (0,)), ((), ())),...]
    pallas_call x2 -> x14, Pallas kernels: 19.2 us -> 108 us  [the longest x2 62.8 us: newton(): pl.pallas_call(functools.partial(newton_kernel, count, sides), out_shape=...]
    ppermute x54 -> x18, starting transfers between devices: 99.8 us -> 26.6 us  [axis_shift(): return lax.ppermute(value, axis, [(i, (i + k) % n) for i in range(n)])]
    dynamic_update_slice x48 -> x0, local copies, waits for them, and re-layouts: 62.7 us -> none  [the longest x24 31.8 us: group_gather(): lax.dynamic_update_slice_in_dim(full, other, ((1 - h) * n + place) * rows...]
    dynamic_slice x31 -> x2, local copies, waits for them, and re-layouts: 42 us -> 0.08 us  [placed_in_order(): return lax.dynamic_slice_in_dim(piled, start, n, 0)]
    ppermute x81 -> x42, waiting for transfers between devices: 106 us -> 65.9 us  [axis_swap(): return lax.ppermute(value, axis, [(i, i ^ k) for i in range(n)])]
    ppermute x81 -> x42, starting transfers between devices: 53.6 us -> 35.8 us  [axis_swap(): return lax.ppermute(value, axis, [(i, i ^ k) for i in range(n)])]
    all_to_all x0 -> x4, starting transfers between devices: none -> 17.3 us  [spread(): lax.all_to_all(jnp.broadcast_to(value[None], (n,) + value.shape), axis, 0...]
  transfers between devices with their start and end apart: 135 -> 72, of which waited for: 51 -> 27; matrix products, arithmetic and copies ran while one was open for 39% -> 13% of each run, Pallas kernels for 3% -> 24%
where the time goes in v2:
time: 555 us; the launch traced here: 547 us
  waiting for transfers between devices  172 us (31%)
  Pallas kernels  136 us (25%)
  starting transfers between devices  92.6 us (17%)
  local copies, waits for them, and re-layouts  75.6 us (14%)
  other arithmetic  36 us (6%)
  between operations  17.5 us (3%)
  blocking collectives  10.2 us (2%)
  matrix products  6.87 us (1%)
    ppermute x18, waiting for transfers between devices, axis_shift(): return lax.ppermute(value, axis, [(i, (i + k) % n) for i in range(n)])  85.5 us
    ppermute x42, waiting for transfers between devices, axis_swap(): return lax.ppermute(value, axis, [(i, i ^ k) for i in range(n)])  65.9 us
    pallas_call x2, Pallas kernels, newton(): pl.pallas_call(functools.partial(newton_kernel, count, sides), out_shape=...  62.8 us
    ppermute x42, starting transfers between devices, axis_swap(): return lax.ppermute(value, axis, [(i, i ^ k) for i in range(n)])  35.8 us
    unnamed x255, local copies, waits for them, and re-layouts  35.5 us
    ppermute x18, starting transfers between devices, axis_shift(): return lax.ppermute(value, axis, [(i, (i + k) % n) for i in range(n)])  26.6 us
    all_to_all x4, starting transfers between devices, spread(): lax.all_to_all(jnp.broadcast_to(value[None], (n,) + value.shape), axis, 0...  17.3 us
    pallas_call x4, Pallas kernels, place(): pl.pallas_call(functools.partial(place_kernel, count, sizes), out_shape=t...  12.9 us
  transfers between devices with their start and end apart: 72, of which 27 were waited for; matrix products, arithmetic and copies ran while one was open for 13% of the time, Pallas kernels for 24%

profile of v2, /device:TPU:0, one launch (start us, length us, event | category | flops | bytes accessed | tf_op | source)
XLA Modules:
  0.0 547.1 jit_solution(5499376067111471749)
XLA Ops:
  9.6 6.0 %collective-permute-start.3 = (bf16[192,1728]{1,0:T(8,128)(2,1)}, bf16[192,1728]{1,0:T(8,128)(2,1)}, u32[]{:S(2)}, u32[]{:S(2)}) collective-permute-start(bf16[192,1728]{1,0:T(8,128)(2,1)} %bitcast_convert_fusion.2), channel_id=1, source_target_pairs={{0,4},{4,8},{8,12},{1,5},{5,9},{9,13},{2,6},{6,10},{10,14},{3,7},{... | collective-permute-start | bytes 1990664 | tf_op jit(solution)/shard_map/ppermute | solution.py:117
  19.6 5.9 %all-to-all-start = ((f32[8,5,384]{2,1,0:T(8,128)}), f32[8,5,384]{2,1,0:T(8,128)S(1)}, u32[]{:S(2)}, u32[]{:S(2)}) async-start(f32[8,5,384]{2,1,0:T(8,128)} %broadcast_in_dim.35), calls=%async_computation | async-start | bytes 196608 | tf_op jit(solution)/shard_map/all_to_all | solution.py:104
  27.4 9.8 %all-to-all-done = f32[8,5,384]{2,1,0:T(8,128)S(1)} async-done(((f32[8,5,384]{2,1,0:T(8,128)}), f32[8,5,384]{2,1,0:T(8,128)S(1)}, u32[]{:S(2)}, u32[]{:S(2)}) %all-to-all-start) | async-done | bytes 61472 | tf_op jit(solution)/shard_map/all_to_all | solution.py:104
  42.5 2.9 pad_maximum_fusion.mine_ref
  52.8 12.5 %collective-permute-done.1 = bf16[2,256,384]{1,2,0:T(8,128)(2,1)S(1)} collective-permute-done((bf16[2,256,384]{1,2,0:T(8,128)(2,1)S(1)}, bf16[2,256,384]{1,2,0:T(8,128)(2,1)S(1)}, u32[]{:S(2)}, u32[]{:S(2)}) %collective-permute-start.1) | collective-permute-done | bytes 393248 | tf_op jit(solution)/shard_map/ppermute | solution.py:59
  70.5 5.6 %place.4.refs_0_ = bf16[13824,192]{1,0:T(8,128)(2,1)S(1)} custom-call(s32[6]{0:T(128)S(1)} %stack.131.index_ref, bf16[3,192,1728]{2,1,0:T(8,128)(2,1)} %pad_maximum_fusion.mine_ref, bf16[3,192,1728]{2,1,0:T(8,128)(2,1)} %collective-permute-done.9.other_ref), custom_call_target="tpu_custom_call" | custom-call | tf_op jit(solution)/shard_map/place/pallas_call | solution.py:628
  78.5 2.9 copy-done.2
  81.4 7.0 %collective-permute-done.10 = bf16[192,1728]{1,0:T(8,128)(2,1)} collective-permute-done((bf16[192,1728]{1,0:T(8,128)(2,1)}, bf16[192,1728]{1,0:T(8,128)(2,1)}, u32[]{:S(2)}, u32[]{:S(2)}) %collective-permute-start.10) | collective-permute-done | bytes 663584 | tf_op jit(solution)/shard_map/ppermute | solution.py:122
  97.0 3.0 copy-done.3
  102.6 4.4 conv_one.1
  111.6 3.9 all-to-all-start.1
  130.5 2.6 place.7
  133.1 4.7 collective-permute-done.12.refs_1_
  137.8 9.9 %collective-permute-done.13.refs_2_ = bf16[8,8,16,192]{3,2,1,0:T(8,128)(2,1)} collective-permute-done((bf16[8,8,16,192]{3,2,1,0:T(8,128)(2,1)S(1)}, bf16[8,8,16,192]{3,2,1,0:T(8,128)(2,1)}, u32[]{:S(2)}, u32[]{:S(2)}) %collective-permute-start.13) | collective-permute-done | bytes 393248 | tf_op jit(solution)/shard_map/ppermute | solution.py:59
  149.2 10.9 %conv_two.1 = (f32[8,8,16,192]{3,2,1,0:T(8,128)S(1)}, bf16[8,8,16,192]{3,2,1,0:T(8,128)(2,1)S(1)}, f32[8,1024]{1,0:T(8,128)}) custom-call(s32[1]{0:T(128)} %bitcast.row_ref, bf16[8,8,16,192]{3,2,1,0:T(8,128)(2,1)S(1)} %multiply_convert_fusion.1.refs_0_, bf16[8,8,16,192]{3,2,1,0:T(8,128)(2,1)} %collective-permute-done.12.refs_1_, ...), custom_call_target="tpu_custom_call" | custom-call | tf_op jit(solution)/shard_map/conv_two/pallas_call | solution.py:274
  176.8 5.7 %critic.1 = (bf16[1024,128]{1,0:T(8,128)(2,1)S(1)}, f32[8,128]{1,0:T(8,128)S(1)}) custom-call(f32[8,1024]{1,0:T(8,128)S(1)} %add_add_fusion.pic_ref, bf16[9,8,96]{2,1,0:T(8,128)(2,1)S(1)} %copy-done.57, bf16[9,96,96]{2,1,0:T(8,128)(2,1)S(1)} %bitcast.260, bf16[8,96]{1,0:T(8,128)(2,1)S(1)} %copy-done.58, f32[16,96]{1,0:T(8,128)S(1)} %convolution_add_fusion.head_ref, ...), custom_call_target="tpu_custom_call" | custom-call | tf_op jit(solution)/shard_map/critic/pallas_call | solution.py:354
  186.7 7.7 %back_two.1 = (bf16[10,10,16,192]{3,2,1,0:T(8,128)(2,1)S(1)}, f32[128,192]{1,0:T(8,128)S(1)}, bf16[1024,192]{1,0:T(8,128)(2,1)S(1)}, bf16[1024,192]{1,0:T(8,128)...) custom-call(s32[1]{0:T(128)} %bitcast.row_ref, bf16[1024,128]{1,0:T(8,128)(2,1)S(1)} %get-tuple-element.84.g_ref, ...), custom_call_target="tpu_custom_call" | custom-call | tf_op jit(solution)/shard_map/back_two/pallas_call | solution.py:399
  198.0 7.7 %weight_two.1 = bf16[8,528,384]{2,1,0:T(8,128)(2,1)S(1)} custom-call(s32[1]{0:T(128)} %bitcast.row_ref, bf16[10,10,16,192]{3,2,1,0:T(8,128)(2,1)S(1)} %get-tuple-element.91.gpad_ref, bf16[192,1024]{1,0:T(8,128)(2,1)S(1)} %bitcast.265, bf16[192,1024]{1,0:T(8,128)(2,1)S(1)} %bitcast.266, bf16[192,1024]{1,0:T(8,128)(2,1)S(1)} %bitcast.267, ...), custom_call_target="tpu_custom_call" | custom-call | flops 8153726976 | tf_op jit(solution)/shard_map/weight_two/pallas_call | solution.py:763
  210.2 8.6 %collective-permute-done.19 = bf16[1024,192]{1,0:T(8,128)(2,1)S(1)} collective-permute-done((bf16[1024,192]{1,0:T(8,128)(2,1)S(1)}, bf16[1024,192]{1,0:T(8,128)(2,1)S(1)}, u32[]{:S(2)}, u32[]{:S(2)}) %collective-permute-start.19) | collective-permute-done | bytes 393248 | tf_op jit(solution)/shard_map/ppermute | solution.py:59
  220.7 10.2 %all_to_all.25 = f32[8,4,192]{2,1,0:T(4,128)S(1)} all-to-all(f32[8,4,192]{2,1,0:T(4,128)S(1)} %broadcast_in_dim.86), channel_id=1, replica_groups=mesh['half'=2,'dp'=4,'row'=4] {'half','dp'}, dimensions={0} | all-to-all | bytes 49152 | tf_op jit(solution)/shard_map/all_to_all | solution.py:104
  233.6 2.7 collective-permute-start.26
  236.4 12.9 %collective-permute-done.21.refs_1_ = bf16[8,8,16,192]{3,2,1,0:T(8,128)(2,1)S(1)} collective-permute-done((bf16[8,8,16,192]{3,2,1,0:T(8,128)(2,1)S(1)}, bf16[8,8,16,192]{3,2,1,0:T(8,128)(2,1)S(1)}, u32[]{:S(2)}, u32[]{:S(2)}) %collective-permute-start.21) | collective-permute-done | bytes 393248 | tf_op jit(solution)/shard_map/ppermute | solution.py:64
  249.3 21.6 %collective-permute-done.25.refs_2_ = bf16[8,8,16,192]{3,2,1,0:T(8,128)(2,1)S(1)} collective-permute-done((bf16[8,8,16,192]{3,2,1,0:T(8,128)(2,1)S(1)}, bf16[8,8,16,192]{3,2,1,0:T(8,128)(2,1)S(1)}, u32[]{:S(2)}, u32[]{:S(2)}) %collective-permute-start.25) | collective-permute-done | bytes 393248 | tf_op jit(solution)/shard_map/ppermute | solution.py:64
  278.4 10.6 %collective-permute-start.33 = (bf16[528,384]{1,0:T(8,128)(2,1)}, bf16[528,384]{1,0:T(8,128)(2,1)}, u32[]{:S(2)}, u32[]{:S(2)}) collective-permute-start(bf16[528,384]{1,0:T(8,128)(2,1)} %get-tuple-element.257), channel_id=1, source_target_pairs={{0,4},{4,8},{8,12},{12,0},{1,5},{5,9},{9,13},{13,1},{2,6},{6,10},{... | collective-permute-start | bytes 1216520 | tf_op jit(solution)/shard_map/ppermute | solution.py:64
  289.0 2.8 copy-done.59
  295.2 6.7 %weight_one.1 = (f32[192,1728]{1,0:T(8,128)}, bf16[192,1728]{1,0:T(8,128)(2,1)S(1)}) custom-call(s32[3]{0:T(128)S(1)} %pad_add_fusion.2.where_ref, f32[1,1]{1,0:T(1,128)} %bitcast.73.inverse_ref, bf16[8,8,16,192]{3,2,1,0:T(8,128)(2,1)S(1)} %copy-done.29, bf16[8,8,16,192]{3,2,1,0:T(8,128)(2,1)S(1)} %copy-done.62, bf16[8,8,16,192]{3,2,1,0:T(8,128)(2,1)S(1)} %copy-done.64, ...), custom_call_target="tpu_custom_call" | custom-call | flops 5435817984 | tf_op jit(solution)/shard_map/weight_one/pallas_call | solution.py:702
  309.3 16.8 %collective-permute-done.34.refs_2_ = bf16[528,384]{1,0:T(8,128)(2,1)} collective-permute-done((bf16[528,384]{1,0:T(8,128)(2,1)}, bf16[528,384]{1,0:T(8,128)(2,1)}, u32[]{:S(2)}, u32[]{:S(2)}) %collective-permute-start.34) | collective-permute-done | bytes 405536 | tf_op jit(solution)/shard_map/ppermute | solution.py:64
  326.1 8.7 %collective-permute-done.36.refs_2_ = bf16[192,1728]{1,0:T(8,128)(2,1)} collective-permute-done((bf16[192,1728]{1,0:T(8,128)(2,1)S(1)}, bf16[192,1728]{1,0:T(8,128)(2,1)}, u32[]{:S(2)}, u32[]{:S(2)}) %collective-permute-start.36) | collective-permute-done | bytes 663584 | tf_op jit(solution)/shard_map/ppermute | solution.py:59
  334.8 2.6 gram.2
  348.3 4.3 collective-permute-done.40
  354.4 3.0 copy-done.5
  358.4 5.3 back_one.1
  367.3 3.4 moments.1
  373.2 5.6 %collective-permute-done.43 = f32[1,24,768]{2,1,0:T(8,128)S(1)} collective-permute-done((f32[1,24,768]{2,1,0:T(8,128)S(1)}, f32[1,24,768]{2,1,0:T(8,128)S(1)}, u32[]{:S(2)}, u32[]{:S(2)}) %collective-permute-start.43) | collective-permute-done | bytes 73760 | tf_op jit(solution)/shard_map/ppermute | solution.py:64
  379.4 5.7 %collective-permute-done.44 = f32[1,24,768]{2,1,0:T(8,128)S(1)} collective-permute-done((f32[1,24,768]{2,1,0:T(8,128)S(1)}, f32[1,24,768]{2,1,0:T(8,128)S(1)}, u32[]{:S(2)}, u32[]{:S(2)}) %collective-permute-start.44) | collective-permute-done | bytes 73760 | tf_op jit(solution)/shard_map/ppermute | solution.py:64
  387.4 3.6 collective-permute-done.46.refs_2_
  391.0 5.4 collective-permute-done.47.refs_3_
  406.6 3.3 all-to-all-start.3
  415.4 3.2 collective-permute-done.50
  420.4 6.3 %collective-permute-done.56.refs_2_ = f32[4,1,24,768]{3,2,1,0:T(8,128)S(1)} collective-permute-done((f32[4,1,24,768]{3,2,1,0:T(8,128)S(1)}, f32[4,1,24,768]{3,2,1,0:T(8,128)S(1)}, u32[]{:S(2)}, u32[]{:S(2)}) %collective-permute-start.56) | collective-permute-done | bytes 294944 | tf_op jit(solution)/shard_map/ppermute | solution.py:59
  427.2 2.7 collective-permute-start.53
  429.9 7.2 %collective-permute-done.53 = f32[1,48,768]{2,1,0:T(8,128)S(1)} collective-permute-done((f32[1,48,768]{2,1,0:T(8,128)S(1)}, f32[1,48,768]{2,1,0:T(8,128)S(1)}, u32[]{:S(2)}, u32[]{:S(2)}) %collective-permute-start.53) | collective-permute-done | bytes 147488 | tf_op jit(solution)/shard_map/ppermute | solution.py:64
  437.4 6.7 %collective-permute-done.54 = f32[1,48,768]{2,1,0:T(8,128)S(1)} collective-permute-done((f32[1,48,768]{2,1,0:T(8,128)S(1)}, f32[1,48,768]{2,1,0:T(8,128)S(1)}, u32[]{:S(2)}, u32[]{:S(2)}) %collective-permute-start.54) | collective-permute-done | bytes 147488 | tf_op jit(solution)/shard_map/ppermute | solution.py:64
  447.1 4.3 all-to-all-start.4
  454.5 30.8 %newton.2.map_ref = bf16[1,4,192,192]{3,2,1,0:T(8,128)(2,1)S(1)} custom-call(s32[3]{0:T(128)S(1)} %pad_add_fusion.2.where_ref, f32[4,1,24,768]{3,2,1,0:T(8,128)S(1)} %constant_dynamic-slice_fusion.1.refs_0_, f32[4,1,24,768]{3,2,1,0:T(8,128)S(1)} %collective-permute-done.55.refs_1_, f32[4,1,24,768]{3,2,1,0:T(8,128)S(1)} %collective-permute-done.56.refs_2_, ...), custom_call_target="tpu_custom_call" | custom-call | flops 28991029248 | tf_op jit(solution)/shard_map/newton/pallas_call | solution.py:955
  486.1 32.0 %newton.3 = bf16[1,4,192,192]{3,2,1,0:T(8,128)(2,1)} custom-call(s32[3]{0:T(128)S(1)} %pad_add_fusion.2.where_ref, f32[4,1,48,768]{3,2,1,0:T(8,128)S(1)} %constant_dynamic-slice_fusion.refs_0_, f32[4,1,48,768]{3,2,1,0:T(8,128)} %collective-permute-done.62.refs_1_, f32[4,1,48,768]{3,2,1,0:T(8,128)S(1)} %collective-permute-done.63.refs_2_, ...), custom_call_target="tpu_custom_call" | custom-call | flops 28991029248 | tf_op jit(solution)/shard_map/newton/pallas_call | solution.py:955
  519.9 3.6 update.2
  531.2 3.5 multiply_subtract_fusion
  (503 shorter events, 172.4 us)
Async XLA Ops:
  9.6 30.0 %collective-permute-start.3 = (bf16[192,1728]{1,0:T(8,128)(2,1)}, bf16[192,1728]{1,0:T(8,128)(2,1)}, u32[]{:S(2)}, u32[]{:S(2)}) collective-permute-start(bf16[192,1728]{1,0:T(8,128)(2,1)} %bitcast_convert_fusion.2), channel_id=1, source_target_pairs={{0,4},{4,8},{8,12},{1,5},{5,9},{9,13},{2,6},{6,10},{10,14},{3,7},{... | collective-permute-start | bytes 1990664 | tf_op jit(solution)/shard_map/ppermute | solution.py:117
  15.6 25.6 %collective-permute-start.6 = (bf16[192,1728]{1,0:T(8,128)(2,1)}, bf16[192,1728]{1,0:T(8,128)(2,1)}, u32[]{:S(2)}, u32[]{:S(2)}) collective-permute-start(bf16[192,1728]{1,0:T(8,128)(2,1)} %bitcast_convert_fusion.2), channel_id=1, source_target_pairs={{4,0},{8,4},{12,8},{5,1},{9,5},{13,9},{6,2},{10,6},{14,10},{7,3},{... | collective-permute-start | bytes 1990664 | tf_op jit(solution)/shard_map/ppermute | solution.py:122
  19.6 17.6 %all-to-all-start = ((f32[8,5,384]{2,1,0:T(8,128)}), f32[8,5,384]{2,1,0:T(8,128)S(1)}, u32[]{:S(2)}, u32[]{:S(2)}) async-start(f32[8,5,384]{2,1,0:T(8,128)} %broadcast_in_dim.35), calls=%async_computation | async-start | bytes 196608 | tf_op jit(solution)/shard_map/all_to_all | solution.py:104
  25.5 102.6 %all-gather.5.cloned.1.call-start = ((), (), s32[]{:S(2)}) async-start(), calls=%async_computation.5 | async-start | bytes 3981312 | tf_op jit(solution)/shard_map/all_gather | solution.py:1362
  39.6 25.7 %collective-permute-start.4 = (bf16[192,1728]{1,0:T(8,128)(2,1)}, bf16[192,1728]{1,0:T(8,128)(2,1)}, u32[]{:S(2)}, u32[]{:S(2)}) collective-permute-start(bf16[192,1728]{1,0:T(8,128)(2,1)} %collective-permute-done.3), channel_id=1, source_target_pairs={{4,8},{8,12},{5,9},{9,13},{6,10},{10,14},{7,11},{11,15},{20,24},{2... | collective-permute-start | bytes 1990664 | tf_op jit(solution)/shard_map/ppermute | solution.py:117
  41.2 25.7 %collective-permute-start.7 = (bf16[192,1728]{1,0:T(8,128)(2,1)}, bf16[192,1728]{1,0:T(8,128)(2,1)}, u32[]{:S(2)}, u32[]{:S(2)}) collective-permute-start(bf16[192,1728]{1,0:T(8,128)(2,1)} %collective-permute-done.6), channel_id=1, source_target_pairs={{4,0},{8,4},{5,1},{9,5},{6,2},{10,6},{7,3},{11,7},{20,16},{24,20},... | collective-permute-start | bytes 1990664 | tf_op jit(solution)/shard_map/ppermute | solution.py:122
  45.3 25.2 %collective-permute-start.9 = (bf16[3,192,1728]{2,1,0:T(8,128)(2,1)}, bf16[3,192,1728]{2,1,0:T(8,128)(2,1)}, u32[]{:S(2)}, u32[]{:S(2)}) collective-permute-start(bf16[3,192,1728]{2,1,0:T(8,128)(2,1)} %pad_maximum_fusion.mine_ref), channel_id=1, source_target_pairs={{0,16},{16,0},{1,17},{17,1},{2,18},{18,2},{3,19},{19,3},{4,20},{20... | collective-permute-start | bytes 5971976 | tf_op jit(solution)/shard_map/ppermute | solution.py:59
  45.4 20.0 %collective-permute-start.1 = (bf16[2,256,384]{1,2,0:T(8,128)(2,1)S(1)}, bf16[2,256,384]{1,2,0:T(8,128)(2,1)S(1)}, u32[]{:S(2)}, u32[]{:S(2)}) collective-permute-start(bf16[2,256,384]{1,2,0:T(8,128)(2,1)S(1)} %pad_maximum_fusion.2), channel_id=1, source_target_pairs={{0,2},{1,3},{2,0},{3,1},{4,6},{5,7},{6,4},{7,5},{8,10},{9,11},{10,... | collective-permute-start | bytes 1179656 | tf_op jit(solution)/shard_map/ppermute | solution.py:59
  49.3 16.0 %collective-permute-start.2 = (bf16[2,256,384]{1,2,0:T(8,128)(2,1)S(1)}, bf16[2,256,384]{1,2,0:T(8,128)(2,1)}, u32[]{:S(2)}, u32[]{:S(2)}) collective-permute-start(bf16[2,256,384]{1,2,0:T(8,128)(2,1)S(1)} %pad_maximum_fusion.2), channel_id=1, source_target_pairs={{0,3},{1,2},{2,1},{3,0},{4,7},{5,6},{6,5},{7,4},{8,11},{9,10},{10,... | collective-permute-start | bytes 1179656 | tf_op jit(solution)/shard_map/ppermute | solution.py:59
  65.3 16.1 %collective-permute-start.5 = (bf16[192,1728]{1,0:T(8,128)(2,1)}, bf16[192,1728]{1,0:T(8,128)(2,1)}, u32[]{:S(2)}, u32[]{:S(2)}) collective-permute-start(bf16[192,1728]{1,0:T(8,128)(2,1)} %collective-permute-done.4), channel_id=1, source_target_pairs={{8,12},{9,13},{10,14},{11,15},{24,28},{25,29},{26,30},{27,31}} | collective-permute-start | bytes 1990664 | tf_op jit(solution)/shard_map/ppermute | solution.py:117
  68.1 20.3 %collective-permute-start.10 = (bf16[192,1728]{1,0:T(8,128)(2,1)}, bf16[192,1728]{1,0:T(8,128)(2,1)}, u32[]{:S(2)}, u32[]{:S(2)}) collective-permute-start(bf16[192,1728]{1,0:T(8,128)(2,1)} %collective-permute-done.7), channel_id=1, source_target_pairs={{4,0},{5,1},{6,2},{7,3},{20,16},{21,17},{22,18},{23,19}} | collective-permute-start | bytes 1990664 | tf_op jit(solution)/shard_map/ppermute | solution.py:122
  88.4 200.6 %all-gather.7.cloned.1.call-start = ((), (), s32[]{:S(2)}) async-start(), calls=%async_computation.6 | async-start | bytes 7077888 | tf_op jit(solution)/shard_map/all_gather | solution.py:1380
  122.8 14.9 %collective-permute-start.12 = (bf16[8,8,16,192]{3,2,1,0:T(8,128)(2,1)S(1)}, bf16[8,8,16,192]{3,2,1,0:T(8,128)(2,1)}, u32[]{:S(2)}, u32[]{:S(2)}) collective-permute-start(bf16[8,8,16,192]{3,2,1,0:T(8,128)(2,1)S(1)} %multiply_convert_fusion.1.refs_0_), channel_id=1, source_target_pairs={{0,1},{1,0},{2,3},{3,2},{4,5},{5,4},{6,7},{7,6},{8,9},{9,8},{10,11... | collective-permute-start | bytes 1179656 | tf_op jit(solution)/shard_map/ppermute | solution.py:59
  123.4 24.3 %collective-permute-start.13 = (bf16[8,8,16,192]{3,2,1,0:T(8,128)(2,1)S(1)}, bf16[8,8,16,192]{3,2,1,0:T(8,128)(2,1)}, u32[]{:S(2)}, u32[]{:S(2)}) collective-permute-start(bf16[8,8,16,192]{3,2,1,0:T(8,128)(2,1)S(1)} %multiply_convert_fusion.1.refs_0_), channel_id=1, source_target_pairs={{0,2},{1,3},{2,0},{3,1},{4,6},{5,7},{6,4},{7,5},{8,10},{9,11},{10,... | collective-permute-start | bytes 1179656 | tf_op jit(solution)/shard_map/ppermute | solution.py:59
  124.9 24.2 %collective-permute-start.14 = (bf16[8,8,16,192]{3,2,1,0:T(8,128)(2,1)S(1)}, bf16[8,8,16,192]{3,2,1,0:T(8,128)(2,1)}, u32[]{:S(2)}, u32[]{:S(2)}) collective-permute-start(bf16[8,8,16,192]{3,2,1,0:T(8,128)(2,1)S(1)} %multiply_convert_fusion.1.refs_0_), channel_id=1, source_target_pairs={{0,3},{1,2},{2,1},{3,0},{4,7},{5,6},{6,5},{7,4},{8,11},{9,10},{10,... | collective-permute-start | bytes 1179656 | tf_op jit(solution)/shard_map/ppermute | solution.py:59
  161.8 14.2 %collective-permute-start.17 = (f32[8,1024]{1,0:T(8,128)}, f32[8,1024]{1,0:T(8,128)S(1)}, u32[]{:S(2)}, u32[]{:S(2)}) collective-permute-start(f32[8,1024]{1,0:T(8,128)} %get-tuple-element.83), channel_id=1, source_target_pairs={{0,3},{1,2},{2,1},{3,0},{4,7},{5,6},{6,5},{7,4},{8,11},{9,10},{10,... | collective-permute-start | bytes 98312 | tf_op jit(solution)/shard_map/ppermute | solution.py:59
  163.6 12.4 %collective-permute-start.16 = (f32[8,1024]{1,0:T(8,128)}, f32[8,1024]{1,0:T(8,128)S(1)}, u32[]{:S(2)}, u32[]{:S(2)}) collective-permute-start(f32[8,1024]{1,0:T(8,128)} %get-tuple-element.83), channel_id=1, source_target_pairs={{0,2},{1,3},{2,0},{3,1},{4,6},{5,7},{6,4},{7,5},{8,10},{9,11},{10,... | collective-permute-start | bytes 98312 | tf_op jit(solution)/shard_map/ppermute | solution.py:59
  194.4 15.8 %collective-permute-start.20 = (bf16[1024,192]{1,0:T(8,128)(2,1)S(1)}, bf16[1024,192]{1,0:T(8,128)(2,1)S(1)}, u32[]{:S(2)}, u32[]{:S(2)}) collective-permute-start(bf16[1024,192]{1,0:T(8,128)(2,1)S(1)} %get-tuple-element.90), channel_id=1, source_target_pairs={{0,3},{1,2},{2,1},{3,0},{4,7},{5,6},{6,5},{7,4},{8,11},{9,10},{10,... | collective-permute-start | bytes 1179656 | tf_op jit(solution)/shard_map/ppermute | solution.py:59
  196.2 22.6 %collective-permute-start.19 = (bf16[1024,192]{1,0:T(8,128)(2,1)S(1)}, bf16[1024,192]{1,0:T(8,128)(2,1)S(1)}, u32[]{:S(2)}, u32[]{:S(2)}) collective-permute-start(bf16[1024,192]{1,0:T(8,128)(2,1)S(1)} %get-tuple-element.89), channel_id=1, source_target_pairs={{0,2},{1,3},{2,0},{3,1},{4,6},{5,7},{6,4},{7,5},{8,10},{9,11},{10,... | collective-permute-start | bytes 1179656 | tf_op jit(solution)/shard_map/ppermute | solution.py:59
  196.7 22.1 %collective-permute-start.18 = (bf16[1024,192]{1,0:T(8,128)(2,1)S(1)}, bf16[1024,192]{1,0:T(8,128)(2,1)S(1)}, u32[]{:S(2)}, u32[]{:S(2)}) collective-permute-start(bf16[1024,192]{1,0:T(8,128)(2,1)S(1)} %get-tuple-element.88), channel_id=1, source_target_pairs={{0,1},{1,0},{2,3},{3,2},{4,5},{5,4},{6,7},{7,6},{8,9},{9,8},{10,11... | collective-permute-start | bytes 1179656 | tf_op jit(solution)/shard_map/ppermute | solution.py:59
  207.9 65.4 %collective-permute-start.32 = (bf16[4,528,384]{2,1,0:T(8,128)(2,1)}, bf16[4,528,384]{2,1,0:T(8,128)(2,1)}, u32[]{:S(2)}, u32[]{:S(2)}) collective-permute-start(bf16[4,528,384]{2,1,0:T(8,128)(2,1)} %dynamic-slice_bitcast_fusion), channel_id=1, source_target_pairs={{0,16},{16,0},{1,17},{17,1},{2,18},{18,2},{3,19},{19,3},{4,20},{20... | collective-permute-start | bytes 4866056 | tf_op jit(solution)/shard_map/ppermute | solution.py:59
  232.5 16.8 %collective-permute-start.21 = (bf16[8,8,16,192]{3,2,1,0:T(8,128)(2,1)S(1)}, bf16[8,8,16,192]{3,2,1,0:T(8,128)(2,1)S(1)}, u32[]{:S(2)}, u32[]{:S(2)}) collective-permute-start(bf16[8,8,16,192]{3,2,1,0:T(8,128)(2,1)S(1)} %multiply_convert_fusion.g_ref.refs_0_), channel_id=1, source_target_pairs={{0,4},{4,8},{8,12},{12,0},{1,5},{5,9},{9,13},{13,1},{2,6},{6,10},{... | collective-permute-start | bytes 1179656 | tf_op jit(solution)/shard_map/ppermute | solution.py:64
  233.0 37.9 %collective-permute-start.25 = (bf16[8,8,16,192]{3,2,1,0:T(8,128)(2,1)S(1)}, bf16[8,8,16,192]{3,2,1,0:T(8,128)(2,1)S(1)}, u32[]{:S(2)}, u32[]{:S(2)}) collective-permute-start(bf16[8,8,16,192]{3,2,1,0:T(8,128)(2,1)S(1)} %multiply_convert_fusion.g_ref.refs_0_), channel_id=1, source_target_pairs={{0,8},{4,12},{8,0},{12,4},{1,9},{5,13},{9,1},{13,5},{2,10},{6,14},... | collective-permute-start | bytes 1179656 | tf_op jit(solution)/shard_map/ppermute | solution.py:64
  233.6 37.3 %collective-permute-start.26 = (bf16[8,8,16,192]{3,2,1,0:T(8,128)(2,1)S(1)}, bf16[8,8,16,192]{3,2,1,0:T(8,128)(2,1)}, u32[]{:S(2)}, u32[]{:S(2)}) collective-permute-start(bf16[8,8,16,192]{3,2,1,0:T(8,128)(2,1)S(1)} %multiply_convert_fusion.g_ref.refs_0_), channel_id=1, source_target_pairs={{0,12},{4,0},{8,4},{12,8},{1,13},{5,1},{9,5},{13,9},{2,14},{6,2},{... | collective-permute-start | bytes 1179656 | tf_op jit(solution)/shard_map/ppermute | solution.py:64
  236.4 39.3 %collective-permute-start.27 = (bf16[8,8,16,192]{3,2,1,0:T(8,128)(2,1)S(1)}, bf16[8,8,16,192]{3,2,1,0:T(8,128)(2,1)}, u32[]{:S(2)}, u32[]{:S(2)}) collective-permute-start(bf16[8,8,16,192]{3,2,1,0:T(8,128)(2,1)S(1)} %multiply_convert_fusion.g_ref.refs_0_), channel_id=1, source_target_pairs={{0,16},{16,0},{1,17},{17,1},{2,18},{18,2},{3,19},{19,3},{4,20},{20... | collective-permute-start | bytes 1179656 | tf_op jit(solution)/shard_map/ppermute | solution.py:59
  249.3 26.4 %collective-permute-start.28 = (bf16[8,8,16,192]{3,2,1,0:T(8,128)(2,1)S(1)}, bf16[8,8,16,192]{3,2,1,0:T(8,128)(2,1)}, u32[]{:S(2)}, u32[]{:S(2)}) collective-permute-start(bf16[8,8,16,192]{3,2,1,0:T(8,128)(2,1)S(1)} %collective-permute-done.21.refs_1_), channel_id=1, source_target_pairs={{0,16},{16,0},{1,17},{17,1},{2,18},{18,2},{3,19},{19,3},{4,20},{20... | collective-permute-start | bytes 1179656 | tf_op jit(solution)/shard_map/ppermute | solution.py:59
  278.4 27.7 %collective-permute-start.33 = (bf16[528,384]{1,0:T(8,128)(2,1)}, bf16[528,384]{1,0:T(8,128)(2,1)}, u32[]{:S(2)}, u32[]{:S(2)}) collective-permute-start(bf16[528,384]{1,0:T(8,128)(2,1)} %get-tuple-element.257), channel_id=1, source_target_pairs={{0,4},{4,8},{8,12},{12,0},{1,5},{5,9},{9,13},{13,1},{2,6},{6,10},{... | collective-permute-start | bytes 1216520 | tf_op jit(solution)/shard_map/ppermute | solution.py:64
  302.0 24.2 %collective-permute-start.31 = (bf16[192,1728]{1,0:T(8,128)(2,1)S(1)}, bf16[192,1728]{1,0:T(8,128)(2,1)}, u32[]{:S(2)}, u32[]{:S(2)}) collective-permute-start(bf16[192,1728]{1,0:T(8,128)(2,1)S(1)} %get-tuple-element.111.refs_0_), channel_id=1, source_target_pairs={{0,1},{1,0},{2,3},{3,2},{4,5},{5,4},{6,7},{7,6},{8,9},{9,8},{10,11... | collective-permute-start | bytes 1990664 | tf_op jit(solution)/shard_map/ppermute | solution.py:59
  302.6 32.1 %collective-permute-start.36 = (bf16[192,1728]{1,0:T(8,128)(2,1)S(1)}, bf16[192,1728]{1,0:T(8,128)(2,1)}, u32[]{:S(2)}, u32[]{:S(2)}) collective-permute-start(bf16[192,1728]{1,0:T(8,128)(2,1)S(1)} %get-tuple-element.111.refs_0_), channel_id=1, source_target_pairs={{0,2},{1,3},{2,0},{3,1},{4,6},{5,7},{6,4},{7,5},{8,10},{9,11},{10,... | collective-permute-start | bytes 1990664 | tf_op jit(solution)/shard_map/ppermute | solution.py:59
  304.1 30.7 %collective-permute-start.37 = (bf16[192,1728]{1,0:T(8,128)(2,1)S(1)}, bf16[192,1728]{1,0:T(8,128)(2,1)}, u32[]{:S(2)}, u32[]{:S(2)}) collective-permute-start(bf16[192,1728]{1,0:T(8,128)(2,1)S(1)} %get-tuple-element.111.refs_0_), channel_id=1, source_target_pairs={{0,3},{1,2},{2,1},{3,0},{4,7},{5,6},{6,5},{7,4},{8,11},{9,10},{10,... | collective-permute-start | bytes 1990664 | tf_op jit(solution)/shard_map/ppermute | solution.py:59
  305.5 20.6 %collective-permute-start.34 = (bf16[528,384]{1,0:T(8,128)(2,1)}, bf16[528,384]{1,0:T(8,128)(2,1)}, u32[]{:S(2)}, u32[]{:S(2)}) collective-permute-start(bf16[528,384]{1,0:T(8,128)(2,1)} %get-tuple-element.256), channel_id=1, source_target_pairs={{0,8},{4,12},{8,0},{12,4},{1,9},{5,13},{9,1},{13,5},{2,10},{6,14},... | collective-permute-start | bytes 1216520 | tf_op jit(solution)/shard_map/ppermute | solution.py:64
  306.1 20.0 %collective-permute-start.35 = (bf16[528,384]{1,0:T(8,128)(2,1)}, bf16[528,384]{1,0:T(8,128)(2,1)}, u32[]{:S(2)}, u32[]{:S(2)}) collective-permute-start(bf16[528,384]{1,0:T(8,128)(2,1)} %get-tuple-element.255), channel_id=1, source_target_pairs={{0,12},{4,0},{8,4},{12,8},{1,13},{5,1},{9,5},{13,9},{2,14},{6,2},{... | collective-permute-start | bytes 1216520 | tf_op jit(solution)/shard_map/ppermute | solution.py:64
  353.5 19.3 %collective-permute-start.42 = (f32[1,24,768]{2,1,0:T(8,128)S(1)}, f32[1,24,768]{2,1,0:T(8,128)S(1)}, u32[]{:S(2)}, u32[]{:S(2)}) collective-permute-start(f32[1,24,768]{2,1,0:T(8,128)S(1)} %get-tuple-element.251), channel_id=1, source_target_pairs={{0,12},{4,0},{8,4},{12,8},{1,13},{5,1},{9,5},{13,9},{2,14},{6,2},{... | collective-permute-start | bytes 221192 | tf_op jit(solution)/shard_map/ppermute | solution.py:64
  364.4 34.5 %collective-permute-start.24 = (bf16[256,384]{1,0:T(8,128)(2,1)}, bf16[256,384]{1,0:T(8,128)(2,1)}, u32[]{:S(2)}, u32[]{:S(2)}) collective-permute-start(bf16[256,384]{1,0:T(8,128)(2,1)} %get-tuple-element.105), channel_id=1, source_target_pairs={{0,3},{1,2},{2,1},{3,0},{4,7},{5,6},{6,5},{7,4},{8,11},{9,10},{10,... | collective-permute-start | bytes 589832 | tf_op jit(solution)/shard_map/ppermute | solution.py:59
  365.9 33.0 %collective-permute-start.23 = (bf16[256,384]{1,0:T(8,128)(2,1)}, bf16[256,384]{1,0:T(8,128)(2,1)}, u32[]{:S(2)}, u32[]{:S(2)}) collective-permute-start(bf16[256,384]{1,0:T(8,128)(2,1)} %get-tuple-element.104), channel_id=1, source_target_pairs={{0,2},{1,3},{2,0},{3,1},{4,6},{5,7},{6,4},{7,5},{8,10},{9,11},{10,... | collective-permute-start | bytes 589832 | tf_op jit(solution)/shard_map/ppermute | solution.py:59
  370.7 16.0 %collective-permute-start.45 = (bf16[192,1056]{1,0:T(8,128)(2,1)S(1)}, bf16[192,1056]{1,0:T(8,128)(2,1)S(1)}, u32[]{:S(2)}, u32[]{:S(2)}) collective-permute-start(bf16[192,1056]{1,0:T(8,128)(2,1)S(1)} %get-tuple-element.119.refs_0_), channel_id=1, source_target_pairs={{0,1},{1,0},{2,3},{3,2},{4,5},{5,4},{6,7},{7,6},{8,9},{9,8},{10,11... | collective-permute-start | bytes 1216520 | tf_op jit(solution)/shard_map/ppermute | solution.py:59
  371.3 19.7 %collective-permute-start.46 = (bf16[192,1056]{1,0:T(8,128)(2,1)S(1)}, bf16[192,1056]{1,0:T(8,128)(2,1)S(1)}, u32[]{:S(2)}, u32[]{:S(2)}) collective-permute-start(bf16[192,1056]{1,0:T(8,128)(2,1)S(1)} %get-tuple-element.119.refs_0_), channel_id=1, source_target_pairs={{0,2},{1,3},{2,0},{3,1},{4,6},{5,7},{6,4},{7,5},{8,10},{9,11},{10,... | collective-permute-start | bytes 1216520 | tf_op jit(solution)/shard_map/ppermute | solution.py:59
  404.6 14.0 %collective-permute-start.50 = (f32[1,48,768]{2,1,0:T(8,128)}, f32[1,48,768]{2,1,0:T(8,128)S(1)}, u32[]{:S(2)}, u32[]{:S(2)}) collective-permute-start(f32[1,48,768]{2,1,0:T(8,128)} %get-tuple-element.262), channel_id=1, source_target_pairs={{0,8},{4,12},{8,0},{12,4},{1,9},{5,13},{9,1},{13,5},{2,10},{6,14},... | collective-permute-start | bytes 442376 | tf_op jit(solution)/shard_map/ppermute | solution.py:64
  405.0 13.6 %collective-permute-start.49 = (f32[1,48,768]{2,1,0:T(8,128)}, f32[1,48,768]{2,1,0:T(8,128)}, u32[]{:S(2)}, u32[]{:S(2)}) collective-permute-start(f32[1,48,768]{2,1,0:T(8,128)} %get-tuple-element.260), channel_id=1, source_target_pairs={{0,4},{4,8},{8,12},{12,0},{1,5},{5,9},{9,13},{13,1},{2,6},{6,10},{... | collective-permute-start | bytes 442376 | tf_op jit(solution)/shard_map/ppermute | solution.py:64
  412.0 14.7 %collective-permute-start.56 = (f32[4,1,24,768]{3,2,1,0:T(8,128)S(1)}, f32[4,1,24,768]{3,2,1,0:T(8,128)S(1)}, u32[]{:S(2)}, u32[]{:S(2)}) collective-permute-start(f32[4,1,24,768]{3,2,1,0:T(8,128)S(1)} %constant_dynamic-slice_fusion.1.refs_0_), channel_id=1, source_target_pairs={{0,2},{1,3},{2,0},{3,1},{4,6},{5,7},{6,4},{7,5},{8,10},{9,11},{10,... | collective-permute-start | bytes 884744 | tf_op jit(solution)/shard_map/ppermute | solution.py:59
  418.6 32.8 %collective-permute-start.58 = (f32[4,1,24,768]{3,2,1,0:T(8,128)S(1)}, f32[4,1,24,768]{3,2,1,0:T(8,128)}, u32[]{:S(2)}, u32[]{:S(2)}) collective-permute-start(f32[4,1,24,768]{3,2,1,0:T(8,128)S(1)} %constant_dynamic-slice_fusion.1.refs_0_), channel_id=1, source_target_pairs={{0,16},{16,0},{1,17},{17,1},{2,18},{18,2},{3,19},{19,3},{4,20},{20... | collective-permute-start | bytes 884744 | tf_op jit(solution)/shard_map/ppermute | solution.py:59
  420.3 31.7 %collective-permute-start.59 = (f32[4,1,24,768]{3,2,1,0:T(8,128)S(1)}, f32[4,1,24,768]{3,2,1,0:T(8,128)}, u32[]{:S(2)}, u32[]{:S(2)}) collective-permute-start(f32[4,1,24,768]{3,2,1,0:T(8,128)S(1)} %collective-permute-done.55.refs_1_), channel_id=1, source_target_pairs={{0,16},{16,0},{1,17},{17,1},{2,18},{18,2},{3,19},{19,3},{4,20},{20... | collective-permute-start | bytes 884744 | tf_op jit(solution)/shard_map/ppermute | solution.py:59
  426.7 26.9 %collective-permute-start.60 = (f32[4,1,24,768]{3,2,1,0:T(8,128)S(1)}, f32[4,1,24,768]{3,2,1,0:T(8,128)}, u32[]{:S(2)}, u32[]{:S(2)}) collective-permute-start(f32[4,1,24,768]{3,2,1,0:T(8,128)S(1)} %collective-permute-done.56.refs_2_), channel_id=1, source_target_pairs={{0,16},{16,0},{1,17},{17,1},{2,18},{18,2},{3,19},{19,3},{4,20},{20... | collective-permute-start | bytes 884744 | tf_op jit(solution)/shard_map/ppermute | solution.py:59
  426.7 26.9 %collective-permute-start.61 = (f32[4,1,24,768]{3,2,1,0:T(8,128)S(1)}, f32[4,1,24,768]{3,2,1,0:T(8,128)}, u32[]{:S(2)}, u32[]{:S(2)}) collective-permute-start(f32[4,1,24,768]{3,2,1,0:T(8,128)S(1)} %collective-permute-done.57.refs_3_), channel_id=1, source_target_pairs={{0,16},{16,0},{1,17},{17,1},{2,18},{18,2},{3,19},{19,3},{4,20},{20... | collective-permute-start | bytes 884744 | tf_op jit(solution)/shard_map/ppermute | solution.py:59
  444.2 41.9 %collective-permute-start.62 = (f32[4,1,48,768]{3,2,1,0:T(8,128)S(1)}, f32[4,1,48,768]{3,2,1,0:T(8,128)}, u32[]{:S(2)}, u32[]{:S(2)}) collective-permute-start(f32[4,1,48,768]{3,2,1,0:T(8,128)S(1)} %constant_dynamic-slice_fusion.refs_0_), channel_id=1, source_target_pairs={{0,1},{1,0},{2,3},{3,2},{4,5},{5,4},{6,7},{7,6},{8,9},{9,8},{10,11... | collective-permute-start | bytes 1769480 | tf_op jit(solution)/shard_map/ppermute | solution.py:59
  447.1 80.4 %all-to-all-start.4 = ((f32[8,32,1536]{2,1,0:T(8,128)}), f32[8,32,1536]{2,1,0:T(8,128)}, u32[]{:S(2)}, u32[]{:S(2)}) async-start(f32[8,32,1536]{2,1,0:T(8,128)} %broadcast_in_dim.92), calls=%async_computation.4 | async-start | bytes 3145728 | tf_op jit(solution)/shard_map/all_to_all | solution.py:104
  451.4 34.7 %collective-permute-start.63 = (f32[4,1,48,768]{3,2,1,0:T(8,128)S(1)}, f32[4,1,48,768]{3,2,1,0:T(8,128)S(1)}, u32[]{:S(2)}, u32[]{:S(2)}) collective-permute-start(f32[4,1,48,768]{3,2,1,0:T(8,128)S(1)} %constant_dynamic-slice_fusion.refs_0_), channel_id=1, source_target_pairs={{0,2},{1,3},{2,0},{3,1},{4,6},{5,7},{6,4},{7,5},{8,10},{9,11},{10,... | collective-permute-start | bytes 1769480 | tf_op jit(solution)/shard_map/ppermute | solution.py:59
  452.0 34.1 %collective-permute-start.64 = (f32[4,1,48,768]{3,2,1,0:T(8,128)S(1)}, f32[4,1,48,768]{3,2,1,0:T(8,128)S(1)}, u32[]{:S(2)}, u32[]{:S(2)}) collective-permute-start(f32[4,1,48,768]{3,2,1,0:T(8,128)S(1)} %constant_dynamic-slice_fusion.refs_0_), channel_id=1, source_target_pairs={{0,3},{1,2},{2,1},{3,0},{4,7},{5,6},{6,5},{7,4},{8,11},{9,10},{10,... | collective-permute-start | bytes 1769480 | tf_op jit(solution)/shard_map/ppermute | solution.py:59
  (144 other events, 1356.9 us)
Sparse Core Ops, SparseCore 0:
  88.6 39.4 all-gather.4
  130.3 63.5 all-gather.6

commit v3 on v2

--- a/solution.py
+++ b/solution.py
@@ -106,6 +106,10 @@
 
 def near_sum(value):
     return jnp.sum(spread(value, GROUP), axis=0)
+
+
+def together(*values):
+    return lax.optimization_barrier(values)
 
 
 def after(value, *others):
@@ -856,7 +860,7 @@
 
 def newton_kernel(count, sides, where_ref, *refs):
     pieces = refs[: sides * count]
-    out_ref, a_ref, ah, al, ph, pl_low, th, tl = refs[sides * count :]
+    out_ref, a_ref, ah, al, maps_ref, th, tl = refs[sides * count :]
     size = a_ref.shape[0]
     own = size // count
     block = size // 3
@@ -888,12 +892,10 @@
 
     spans = [slice(i * block, (i + 1) * block) for i in range(3)]
 
-    def symmetric(xh, xl, yh, yl, write):
+    def symmetric(product, write):
         for i in range(3):
             for j in range(i, 3):
-                a, b = spans[i], spans[j]
-                value = three(xh[a, :], xl[a, :], yh[:, b], yl[:, b])
-                write(i, j, value)
+                write(i, j, product(spans[i], spans[j]))
 
     def store(high_ref, low_ref, i, j, value):
         top, low = split(value)
@@ -910,16 +912,21 @@
     al[...] = low
 
     def step(k, carry):
-        hp, lp = ph.at[k], pl_low.at[k]
+        top = maps_ref.at[k]
 
         def write_map(i, j, value):
             value = NS_COEF[1] * a_ref[spans[i], spans[j]] + NS_COEF[2] * value
             if i == j:
                 value = value + jnp.where(eye(value.shape, 0), NS_COEF[0], 0.0)
-            store(hp, lp, i, j, value)
-
-        symmetric(ah, al, ah, al, write_map)
-        symmetric(ah, al, hp, lp, functools.partial(store, th, tl))
+            top[spans[i], spans[j]] = value.astype(bf16)
+            if i != j:
+                top[spans[j], spans[i]] = jnp.transpose(value).astype(bf16)
+
+        symmetric(lambda a, b: three(ah[a, :], al[a, :], ah[:, b], al[:, b]), write_map)
+        symmetric(
+            lambda a, b: times(ah[a, :], top[:, b]) + times(al[a, :], top[:, b]),
+            functools.partial(store, th, tl),
+        )
 
         def write_gram(i, j, value):
             a_ref[spans[i], spans[j]] = value
@@ -927,7 +934,7 @@
             if i != j:
                 a_ref[spans[j], spans[i]] = jnp.transpose(value)
 
-        symmetric(hp, lp, th, tl, write_gram)
+        symmetric(lambda a, b: times(top[a, :], th[:, b]) + times(top[a, :], tl[:, b]), write_gram)
         return carry
 
     lax.fori_loop(0, NS_ITERS - 1, step, 0)
@@ -938,8 +945,8 @@
 
     def fold(k, columns):
         high_part, low_part = split(columns)
-        k = NS_ITERS - 2 - k
-        return three(high_part, low_part, ph[k], pl_low[k])
+        top = maps_ref[NS_ITERS - 2 - k]
+        return times(high_part, top) + times(low_part, top)
 
     columns = lax.fori_loop(0, NS_ITERS - 1, fold, columns) * scale
     for j in range(count):
@@ -965,14 +972,13 @@
                 pltpu.VMEM(square, bf16),
                 pltpu.VMEM(square, bf16),
                 pltpu.VMEM(maps, bf16),
-                pltpu.VMEM(maps, bf16),
                 pltpu.VMEM(square, bf16),
                 pltpu.VMEM(square, bf16),
             ],
         ),
         compiler_params=kernel_params(36),
         cost_estimate=pl.CostEstimate(
-            flops=m * 64 * size**3, bytes_accessed=0, transcendentals=0
+            flops=m * 50 * size**3, bytes_accessed=0, transcendentals=0
         ),
         name="newton",
     )(where, *pieces)
@@ -1426,53 +1432,47 @@
         bf16
     )
     hidden_all = straight(grad_hidden)
-    pieces = back_in(row, after(grad_hidden, hidden_all[1]), weight_one, ranks)
-    hidden_all = both_cores(hidden_all)
-    kept = after(kept, *hidden_all)
-    shares = near_blocks(kept, kept.astype(bf16))
     scaled = inverse.reshape(1, 1)
+    hidden_all = straight(grad_hidden)
+    hidden_all = both_cores(list(together(*hidden_all)))
     moment_one, low_one = weight_one_moment(
         where, scaled, hidden_all, ones_all, momentum_first.T
     )
+    kept, grad_hidden = after(kept, low_one), after(grad_hidden, low_one)
     one_held = row_gather(low_one)
-    one_held[1] = after(one_held[1], *shares)
+    shares = near_blocks(kept, kept.astype(bf16))
+    backs = back_in(row, grad_hidden, weight_one, ranks)
+    *one_held, shares[1], shares[2], shares[3], backs = together(
+        *one_held, *shares[1:], jnp.stack(backs, axis=0)
+    )
     panel = gram_rows(row, one_held, [(0, conv_first.shape[0])])
-    panel = panel.reshape(2, 4, 1, c_out // 8, -1)
-    shares[0] = after(shares[0], panel)
+    kept_one = near_halves(panel.reshape(2, 4, 1, c_out // 8, -1))
     moment_two, moment_skip, low_two = moments_two(
-        scaled, shares, momentum_second.T, momentum_skip.T
-    )
-    total_one = gram_total(gram_terms(panel))
-    two_held = row_gather(low_two)
+        scaled, [after(shares[0], panel)] + shares[1:], momentum_second.T, momentum_skip.T
+    )
+    kept_one = after(kept_one, low_two)
+    two_held = spread(low_two, ("row",))
+    total_one = gram_total(near_blocks(kept_one, kept_one))
+    grams_one = row_gather(total_one)
+    two_held = after(two_held, *grams_one[1:])
+    two_held = [
+        lax.dynamic_index_in_dim(two_held, lax.bitwise_xor(row[0], k), 0, keepdims=False)
+        for k in range(ranks)
+    ]
     spans = [(0, conv_second.shape[0]), (conv_second.shape[0], low_two.shape[1])]
-    panels = gram_rows(row, [after(two_held[0], total_one)] + two_held[1:], spans)
-    total_two = gram_total(gram_terms(panels.reshape(2, 4, 1, c_out // 4, -1)))
-    grams_one = both_cores(row_gather(total_one))
-    grams_one[0] = after(grams_one[0], total_two)
+    panels = gram_rows(row, two_held, spans)
+    kept_two = near_halves(panels.reshape(2, 4, 1, c_out // 4, -1))
+    backs = after(backs, *grams_one[1:])
+    inward = lax.all_to_all(in_order(list(backs[:, None]), "row"), "row", 0, 0)
+    grams_one = both_cores(grams_one)
+    kept_two = after(kept_two, *grams_one)
+    terms_two = near_blocks(kept_two, kept_two)
+    terms_two[0] = after(terms_two[0], inward)
+    total_two = placed_in_order(straight(sum(terms_two)))
+    *grams_one, total_two = together(*grams_one, total_two)
     maps_one = newton(where, grams_one, ranks)
     factor = 0.2 * math.sqrt(max(conv_first.shape[0] * groups, c_out * ranks))
-    (first_out,) = update(
-        row, maps_one, one_held, [conv_first.T], [(0, conv_first.shape[0])], [factor]
-    )
-    grams_two = row_gather(total_two)
-    grams_two[0] = after(grams_two[0], maps_one)
-    maps_two = newton(where, grams_two, ranks)
-    other_map = axis_swap(maps_two, "half", 1)
-    maps_two = jnp.where(
-        half == 0,
-        jnp.concatenate([maps_two, other_map], axis=0),
-        jnp.concatenate([other_map, maps_two], axis=0),
-    )
-    factors = [
-        0.2 * math.sqrt(max(rows * groups, c_out * ranks))
-        for rows in (conv_second.shape[0], conv_skip.shape[0])
-    ]
-    second_out, skip_out = update(
-        row, maps_two, two_held, [conv_second.T, conv_skip.T], spans, factors
-    )
-    weights_new = (first_out.T, second_out.T, skip_out.T)
-    moments_new = (moment_one.T, moment_two.T, moment_skip.T)
-    grad_acted_one = row_scatter(list(pieces)).reshape(raw.shape)
+    grad_acted_one = jnp.sum(inward.astype(f32), axis=0).reshape(raw.shape)
     grad_pre_one = grad_acted_one * silu_slope(pre_one)
     gains_one = jnp.sum(grad_pre_one * normed_one, axis=(0, 1))
     shifts_one = jnp.sum(grad_pre_one, axis=(0, 1))
@@ -1483,7 +1483,6 @@
     grad_cond = grad_cond + jnp.einsum(
         "bgc,kgc->bk", grad_mods_two, norm_second[:EMB], precision=highest
     )
-    grad_cond = jnp.sum(spread(after(grad_cond, total_one), ("row",)), axis=0)
 
     small = jnp.concatenate(
         [
@@ -1493,6 +1492,7 @@
         axis=0,
     )
 
+    grad_cond = jnp.sum(spread(grad_cond, ("row",)), axis=0)
     found = jnp.concatenate(
         [
             grad_mods_one.reshape(n, -1),
@@ -1507,7 +1507,8 @@
     wide = found.shape[1]
     extra = small.reshape(-1)
     extra = jnp.pad(extra, (0, -extra.shape[0] % (8 * wide))).reshape(-1, wide)
-    packet = spread(after(jnp.concatenate([found, extra], axis=0), total_two), GROUP)
+    packet = jnp.concatenate([found, extra], axis=0)
+    packet = spread(after(packet, total_two), GROUP)
     found = packet[:, :n].reshape(-1, wide)
     small = jnp.sum(packet[:, n:], axis=0).reshape(-1)[: small.size].reshape(small.shape)
     loss_sum = small[9 * PAD, 0]
@@ -1542,6 +1543,27 @@
     colour_new = adam_update(
         colour_conv, g_colour * inverse, colour_mean, colour_square, COLOUR_RATE
     )
+    grams_two = row_gather(total_two)
+    (first_out,) = update(
+        row, maps_one, one_held, [conv_first.T], [(0, conv_first.shape[0])], [factor]
+    )
+    grams_two[0] = after(grams_two[0], first_out)
+    maps_two = newton(where, grams_two, ranks)
+    other_map = axis_swap(maps_two, "half", 1)
+    maps_two = jnp.where(
+        half == 0,
+        jnp.concatenate([maps_two, other_map], axis=0),
+        jnp.concatenate([other_map, maps_two], axis=0),
+    )
+    factors = [
+        0.2 * math.sqrt(max(rows * groups, c_out * ranks))
+        for rows in (conv_second.shape[0], conv_skip.shape[0])
+    ]
+    second_out, skip_out = update(
+        row, maps_two, two_held, [conv_second.T, conv_skip.T], spans, factors
+    )
+    weights_new = (first_out.T, second_out.T, skip_out.T)
+    moments_new = (moment_one.T, moment_two.T, moment_skip.T)
     return (
         (loss_sum, fake_count)
         + weights_new

time: 555 us -> 544 us (0.980)
  Pallas kernels: 136 us -> 120 us
  starting transfers between devices: 92.6 us -> 103 us
  local copies, waits for them, and re-layouts: 75.6 us -> 66.7 us
    pallas_call x2, Pallas kernels: 62.8 us -> 50.5 us  [newton(): pl.pallas_call(functools.partial(newton_kernel, count, sides), out_shape=...]
    ppermute x18, starting transfers between devices: 26.6 us -> 34.3 us  [axis_shift(): return lax.ppermute(value, axis, [(i, (i + k) % n) for i in range(n)])]
    unnamed x255 -> x267, local copies, waits for them, and re-layouts: 35.5 us -> 27.9 us
    ppermute x18, waiting for transfers between devices: 85.5 us -> 78.8 us  [axis_shift(): return lax.ppermute(value, axis, [(i, (i + k) % n) for i in range(n)])]
    ppermute x42 -> x36, starting transfers between devices: 35.8 us -> 29.4 us  [axis_swap(): return lax.ppermute(value, axis, [(i, i ^ k) for i in range(n)])]
    all_to_all x4 -> x5, waiting for transfers between devices: 11.8 us -> 17.5 us  [spread(): lax.all_to_all(jnp.broadcast_to(value[None], (n,) + value.shape), axis, 0...]
    all_to_all x4 -> x5, starting transfers between devices: 17.3 us -> 21.6 us  [spread(): lax.all_to_all(jnp.broadcast_to(value[None], (n,) + value.shape), axis, 0...]
    ppermute x42 -> x36, waiting for transfers between devices: 65.9 us -> 64.2 us  [axis_swap(): return lax.ppermute(value, axis, [(i, i ^ k) for i in range(n)])]
  transfers between devices with their start and end apart: 72 -> 68, of which waited for: 27 -> 28; matrix products, arithmetic and copies ran while one was open for 13% -> 13% of each run, Pallas kernels for 24% -> 21%
where the time goes in v3:
time: 544 us; the launch traced here: 536 us
  waiting for transfers between devices  177 us (33%)
  Pallas kernels  120 us (22%)
  starting transfers between devices  103 us (19%)
  local copies, waits for them, and re-layouts  66.7 us (12%)
  other arithmetic  36.4 us (7%)
  between operations  17.8 us (3%)
  blocking collectives  8.54 us (2%)
  matrix products  7.96 us (1%)
    ppermute x18, waiting for transfers between devices, axis_shift(): return lax.ppermute(value, axis, [(i, (i + k) % n) for i in range(n)])  78.8 us
    ppermute x36, waiting for transfers between devices, axis_swap(): return lax.ppermute(value, axis, [(i, i ^ k) for i in range(n)])  64.2 us
    pallas_call x2, Pallas kernels, newton(): pl.pallas_call(functools.partial(newton_kernel, count, sides), out_shape=...  50.5 us
    ppermute x18, starting transfers between devices, axis_shift(): return lax.ppermute(value, axis, [(i, (i + k) % n) for i in range(n)])  34.3 us
    ppermute x36, starting transfers between devices, axis_swap(): return lax.ppermute(value, axis, [(i, i ^ k) for i in range(n)])  29.4 us
    unnamed x267, local copies, waits for them, and re-layouts  27.9 us
    all_to_all x5, starting transfers between devices, spread(): lax.all_to_all(jnp.broadcast_to(value[None], (n,) + value.shape), axis, 0...  21.6 us
    all_to_all x5, waiting for transfers between devices, spread(): lax.all_to_all(jnp.broadcast_to(value[None], (n,) + value.shape), axis, 0...  17.5 us
  transfers between devices with their start and end apart: 68, of which 28 were waited for; matrix products, arithmetic and copies ran while one was open for 13% of the time, Pallas kernels for 21%

profile of v3, /device:TPU:0, one launch (start us, length us, event | category | flops | bytes accessed | tf_op | source)
XLA Modules:
  0.0 536.1 jit_solution(6985566840837345793)
XLA Ops:
  9.6 6.0 %collective-permute-start.3 = (bf16[192,1728]{1,0:T(8,128)(2,1)}, bf16[192,1728]{1,0:T(8,128)(2,1)}, u32[]{:S(2)}, u32[]{:S(2)}) collective-permute-start(bf16[192,1728]{1,0:T(8,128)(2,1)} %bitcast_convert_fusion.2), channel_id=1, source_target_pairs={{0,4},{4,8},{8,12},{1,5},{5,9},{9,13},{2,6},{6,10},{10,14},{3,7},{... | collective-permute-start | bytes 1990664 | tf_op jit(solution)/shard_map/ppermute | solution.py:121
  19.1 5.9 %all-to-all-start = ((f32[8,5,384]{2,1,0:T(8,128)}), f32[8,5,384]{2,1,0:T(8,128)S(1)}, u32[]{:S(2)}, u32[]{:S(2)}) async-start(f32[8,5,384]{2,1,0:T(8,128)} %broadcast_in_dim.37), calls=%async_computation | async-start | bytes 196608 | tf_op jit(solution)/shard_map/all_to_all | solution.py:104
  27.1 10.1 %all-to-all-done = f32[8,5,384]{2,1,0:T(8,128)S(1)} async-done(((f32[8,5,384]{2,1,0:T(8,128)}), f32[8,5,384]{2,1,0:T(8,128)S(1)}, u32[]{:S(2)}, u32[]{:S(2)}) %all-to-all-start) | async-done | bytes 61472 | tf_op jit(solution)/shard_map/all_to_all | solution.py:104
  42.5 2.9 pad_maximum_fusion.mine_ref
  51.9 13.6 %collective-permute-done.1 = bf16[2,256,384]{1,2,0:T(8,128)(2,1)} collective-permute-done((bf16[2,256,384]{1,2,0:T(8,128)(2,1)S(1)}, bf16[2,256,384]{1,2,0:T(8,128)(2,1)}, u32[]{:S(2)}, u32[]{:S(2)}) %collective-permute-start.1) | collective-permute-done | bytes 393248 | tf_op jit(solution)/shard_map/ppermute | solution.py:59
  70.7 5.6 %place.4.refs_0_ = bf16[13824,192]{1,0:T(8,128)(2,1)S(1)} custom-call(s32[6]{0:T(128)S(1)} %stack.155.index_ref, bf16[3,192,1728]{2,1,0:T(8,128)(2,1)} %pad_maximum_fusion.mine_ref, bf16[3,192,1728]{2,1,0:T(8,128)(2,1)} %collective-permute-done.9.other_ref), custom_call_target="tpu_custom_call" | custom-call | tf_op jit(solution)/shard_map/place/pallas_call | solution.py:632
  78.7 2.9 copy-done.2
  81.6 7.0 %collective-permute-done.10 = bf16[192,1728]{1,0:T(8,128)(2,1)} collective-permute-done((bf16[192,1728]{1,0:T(8,128)(2,1)}, bf16[192,1728]{1,0:T(8,128)(2,1)}, u32[]{:S(2)}, u32[]{:S(2)}) %collective-permute-start.10) | collective-permute-done | bytes 663584 | tf_op jit(solution)/shard_map/ppermute | solution.py:126
  94.1 3.2 copy-done.3
  99.7 4.4 conv_one.1
  108.8 3.5 all-to-all-start.1
  115.8 2.7 all-to-all-done.1
  123.2 5.0 all-gather.5.cloned.1.call-done
  134.8 10.0 %collective-permute-done.13.refs_2_ = bf16[8,8,16,192]{3,2,1,0:T(8,128)(2,1)} collective-permute-done((bf16[8,8,16,192]{3,2,1,0:T(8,128)(2,1)}, bf16[8,8,16,192]{3,2,1,0:T(8,128)(2,1)}, u32[]{:S(2)}, u32[]{:S(2)}) %collective-permute-start.13) | collective-permute-done | bytes 393248 | tf_op jit(solution)/shard_map/ppermute | solution.py:59
  146.7 11.1 %conv_two.1 = (f32[8,8,16,192]{3,2,1,0:T(8,128)S(1)}, bf16[8,8,16,192]{3,2,1,0:T(8,128)(2,1)S(1)}, f32[8,1024]{1,0:T(8,128)}) custom-call(s32[1]{0:T(128)} %bitcast.row_ref, bf16[8,8,16,192]{3,2,1,0:T(8,128)(2,1)} %multiply_convert_fusion.1.refs_0_, bf16[8,8,16,192]{3,2,1,0:T(8,128)(2,1)} %collective-permute-done.12.refs_1_, ...), custom_call_target="tpu_custom_call" | custom-call | tf_op jit(solution)/shard_map/conv_two/pallas_call | solution.py:278
  178.8 5.7 %critic.1 = (bf16[1024,128]{1,0:T(8,128)(2,1)S(1)}, f32[8,128]{1,0:T(8,128)S(1)}) custom-call(f32[8,1024]{1,0:T(8,128)S(1)} %add_add_fusion.1.pic_ref, bf16[9,8,96]{2,1,0:T(8,128)(2,1)S(1)} %copy-done.54, bf16[9,96,96]{2,1,0:T(8,128)(2,1)S(1)} %bitcast.284, bf16[8,96]{1,0:T(8,128)(2,1)S(1)} %copy-done.57, f32[16,96]{1,0:T(8,128)S(1)} %convolution_add_fusion.head_ref, ...), custom_call_target="tpu_custom_call" | custom-call | tf_op jit(solution)/shard_map/critic/pallas_call | solution.py:358
  188.2 7.8 %back_two.1 = (bf16[10,10,16,192]{3,2,1,0:T(8,128)(2,1)S(1)}, f32[128,192]{1,0:T(8,128)S(1)}, bf16[1024,192]{1,0:T(8,128)(2,1)S(1)}, bf16[1024,192]{1,0:T(8,128)...) custom-call(s32[1]{0:T(128)} %bitcast.row_ref, bf16[1024,128]{1,0:T(8,128)(2,1)S(1)} %get-tuple-element.106.g_ref, ...), custom_call_target="tpu_custom_call" | custom-call | tf_op jit(solution)/shard_map/back_two/pallas_call | solution.py:403
  200.2 7.7 %weight_two.1 = bf16[8,528,384]{2,1,0:T(8,128)(2,1)S(1)} custom-call(s32[1]{0:T(128)} %bitcast.row_ref, bf16[10,10,16,192]{3,2,1,0:T(8,128)(2,1)S(1)} %get-tuple-element.113.gpad_ref, bf16[192,1024]{1,0:T(8,128)(2,1)S(1)} %bitcast.289, bf16[192,1024]{1,0:T(8,128)(2,1)S(1)} %bitcast.290, bf16[192,1024]{1,0:T(8,128)(2,1)S(1)} %bitcast.291, ...), custom_call_target="tpu_custom_call" | custom-call | flops 8153726976 | tf_op jit(solution)/shard_map/weight_two/pallas_call | solution.py:767
  212.4 9.1 %collective-permute-done.19 = bf16[1024,192]{1,0:T(8,128)(2,1)S(1)} collective-permute-done((bf16[1024,192]{1,0:T(8,128)(2,1)S(1)}, bf16[1024,192]{1,0:T(8,128)(2,1)S(1)}, u32[]{:S(2)}, u32[]{:S(2)}) %collective-permute-start.19) | collective-permute-done | bytes 393248 | tf_op jit(solution)/shard_map/ppermute | solution.py:59
  222.6 8.5 %all_to_all.35 = f32[8,4,192]{2,1,0:T(4,128)S(1)} all-to-all(f32[8,4,192]{2,1,0:T(4,128)S(1)} %broadcast_in_dim.46), channel_id=1, replica_groups=mesh['half'=2,'dp'=4,'row'=4] {'half','dp'}, dimensions={0} | all-to-all | bytes 49152 | tf_op jit(solution)/shard_map/all_to_all | solution.py:104
  232.6 2.7 collective-permute-start.23
  235.3 13.0 %collective-permute-done.21.refs_1_ = bf16[8,8,16,192]{3,2,1,0:T(8,128)(2,1)} collective-permute-done((bf16[8,8,16,192]{3,2,1,0:T(8,128)(2,1)S(1)}, bf16[8,8,16,192]{3,2,1,0:T(8,128)(2,1)}, u32[]{:S(2)}, u32[]{:S(2)}) %collective-permute-start.21) | collective-permute-done | bytes 393248 | tf_op jit(solution)/shard_map/ppermute | solution.py:64
  248.3 21.7 %collective-permute-done.22.refs_2_ = bf16[8,8,16,192]{3,2,1,0:T(8,128)(2,1)} collective-permute-done((bf16[8,8,16,192]{3,2,1,0:T(8,128)(2,1)S(1)}, bf16[8,8,16,192]{3,2,1,0:T(8,128)(2,1)}, u32[]{:S(2)}, u32[]{:S(2)}) %collective-permute-start.22) | collective-permute-done | bytes 393248 | tf_op jit(solution)/shard_map/ppermute | solution.py:64
  273.0 4.1 convert_add_fusion
  277.2 2.8 copy-done.58
  281.3 7.3 %weight_one.1 = (f32[192,1728]{1,0:T(8,128)}, bf16[192,1728]{1,0:T(8,128)(2,1)S(1)}) custom-call(s32[3]{0:T(128)S(1)} %pad_add_fusion.where_ref, f32[1,1]{1,0:T(1,128)} %bitcast.7.inverse_ref, bf16[8,8,16,192]{3,2,1,0:T(8,128)(2,1)S(1)} %multiply_convert_fusion.refs_0_.g_ref, bf16[8,8,16,192]{3,2,1,0:T(8,128)(2,1)} %collective-permute-done.21.refs_1_, ...), custom_call_target="tpu_custom_call" | custom-call | flops 5435817984 | tf_op jit(solution)/shard_map/weight_one/pallas_call | solution.py:706
  289.0 11.0 %collective-permute-start.32 = (bf16[528,384]{1,0:T(8,128)(2,1)S(1)}, bf16[528,384]{1,0:T(8,128)(2,1)S(1)}, u32[]{:S(2)}, u32[]{:S(2)}) collective-permute-start(bf16[528,384]{1,0:T(8,128)(2,1)S(1)} %get-tuple-element.305), channel_id=1, source_target_pairs={{0,4},{4,8},{8,12},{12,0},{1,5},{5,9},{9,13},{13,1},{2,6},{6,10},{... | collective-permute-start | bytes 1216520 | tf_op jit(solution)/shard_map/ppermute | solution.py:64
  303.7 6.2 %collective-permute-done.32.refs_1_ = bf16[528,384]{1,0:T(8,128)(2,1)S(1)} collective-permute-done((bf16[528,384]{1,0:T(8,128)(2,1)S(1)}, bf16[528,384]{1,0:T(8,128)(2,1)S(1)}, u32[]{:S(2)}, u32[]{:S(2)}) %collective-permute-start.32) | collective-permute-done | bytes 405536 | tf_op jit(solution)/shard_map/ppermute | solution.py:64
  310.9 4.5 back_one.1
  316.4 10.3 %collective-permute-done.33.refs_2_ = bf16[528,384]{1,0:T(8,128)(2,1)S(1)} collective-permute-done((bf16[528,384]{1,0:T(8,128)(2,1)S(1)}, bf16[528,384]{1,0:T(8,128)(2,1)S(1)}, u32[]{:S(2)}, u32[]{:S(2)}) %collective-permute-start.33) | collective-permute-done | bytes 405536 | tf_op jit(solution)/shard_map/ppermute | solution.py:64
  328.6 3.5 collective-permute-done.29.refs_2_
  338.6 6.4 %collective-permute-start.38 = (f32[1,24,768]{2,1,0:T(8,128)S(1)}, f32[1,24,768]{2,1,0:T(8,128)S(1)}, u32[]{:S(2)}, u32[]{:S(2)}) collective-permute-start(f32[1,24,768]{2,1,0:T(8,128)S(1)} %get-tuple-element.321), channel_id=1, source_target_pairs={{0,12},{4,0},{8,4},{12,8},{1,13},{5,1},{9,5},{13,9},{2,14},{6,2},{... | collective-permute-start | bytes 221192 | tf_op jit(solution)/shard_map/ppermute | solution.py:64
  347.7 5.0 collective-permute-done.37
  355.7 4.5 all-to-all-start.5
  362.7 5.0 collective-permute-done.40
  374.3 15.0 %collective-permute-done.42.refs_1_ = f32[4,1,24,768]{3,2,1,0:T(8,128)S(1)} collective-permute-done((f32[4,1,24,768]{3,2,1,0:T(8,128)S(1)}, f32[4,1,24,768]{3,2,1,0:T(8,128)S(1)}, u32[]{:S(2)}, u32[]{:S(2)}) %collective-permute-start.42) | collective-permute-done | bytes 294944 | tf_op jit(solution)/shard_map/ppermute | solution.py:59
  389.3 5.2 collective-permute-done.44.refs_3_
  395.9 4.2 all-to-all-start.3
  405.7 3.9 all-to-all-done.3
  415.6 2.7 collective-permute-start.52
  420.4 3.3 all-to-all-start.4
  423.7 4.7 all-to-all-done.4
  428.5 3.2 collective-permute-done.51
  438.5 8.2 %collective-permute-done.54 = f32[1,48,768]{2,1,0:T(8,128)S(1)} collective-permute-done((f32[1,48,768]{2,1,0:T(8,128)S(1)}, f32[1,48,768]{2,1,0:T(8,128)S(1)}, u32[]{:S(2)}, u32[]{:S(2)}) %collective-permute-start.54) | collective-permute-done | bytes 147488 | tf_op jit(solution)/shard_map/ppermute | solution.py:64
  451.8 4.5 all-to-all-start.6
  458.2 25.2 %newton.2.map_ref = bf16[1,4,192,192]{3,2,1,0:T(8,128)(2,1)S(1)} custom-call(s32[3]{0:T(128)S(1)} %pad_add_fusion.where_ref, f32[4,1,24,768]{3,2,1,0:T(8,128)S(1)} %constant_dynamic-slice_fusion.1.refs_0_, f32[4,1,24,768]{3,2,1,0:T(8,128)S(1)} %collective-permute-done.42.refs_1_, f32[4,1,24,768]{3,2,1,0:T(8,128)S(1)} %copy-done.61, ...), custom_call_target="tpu_custom_call" | custom-call | flops 22649241600 | tf_op jit(solution)/shard_map/newton/pallas_call | solution.py:962
  485.6 25.3 %newton.3 = bf16[1,4,192,192]{3,2,1,0:T(8,128)(2,1)S(1)} custom-call(s32[3]{0:T(128)S(1)} %pad_add_fusion.where_ref, f32[4,1,48,768]{3,2,1,0:T(8,128)S(1)} %constant_dynamic-slice_fusion.refs_0_, f32[4,1,48,768]{3,2,1,0:T(8,128)} %collective-permute-done.56.refs_1_, f32[4,1,48,768]{3,2,1,0:T(8,128)} %collective-permute-done.57.refs_2_, ...), custom_call_target="tpu_custom_call" | custom-call | flops 22649241600 | tf_op jit(solution)/shard_map/newton/pallas_call | solution.py:962
  520.5 3.2 multiply_subtract_fusion
  (515 shorter events, 169.0 us)
Async XLA Ops:
  9.6 30.0 %collective-permute-start.3 = (bf16[192,1728]{1,0:T(8,128)(2,1)}, bf16[192,1728]{1,0:T(8,128)(2,1)}, u32[]{:S(2)}, u32[]{:S(2)}) collective-permute-start(bf16[192,1728]{1,0:T(8,128)(2,1)} %bitcast_convert_fusion.2), channel_id=1, source_target_pairs={{0,4},{4,8},{8,12},{1,5},{5,9},{9,13},{2,6},{6,10},{10,14},{3,7},{... | collective-permute-start | bytes 1990664 | tf_op jit(solution)/shard_map/ppermute | solution.py:121
  15.6 25.6 %collective-permute-start.6 = (bf16[192,1728]{1,0:T(8,128)(2,1)}, bf16[192,1728]{1,0:T(8,128)(2,1)}, u32[]{:S(2)}, u32[]{:S(2)}) collective-permute-start(bf16[192,1728]{1,0:T(8,128)(2,1)} %bitcast_convert_fusion.2), channel_id=1, source_target_pairs={{4,0},{8,4},{12,8},{5,1},{9,5},{13,9},{6,2},{10,6},{14,10},{7,3},{... | collective-permute-start | bytes 1990664 | tf_op jit(solution)/shard_map/ppermute | solution.py:126
  19.1 18.1 %all-to-all-start = ((f32[8,5,384]{2,1,0:T(8,128)}), f32[8,5,384]{2,1,0:T(8,128)S(1)}, u32[]{:S(2)}, u32[]{:S(2)}) async-start(f32[8,5,384]{2,1,0:T(8,128)} %broadcast_in_dim.37), calls=%async_computation | async-start | bytes 196608 | tf_op jit(solution)/shard_map/all_to_all | solution.py:104
  25.0 103.3 %all-gather.5.cloned.1.call-start = ((), (), s32[]{:S(2)}) async-start(), calls=%async_computation.7 | async-start | bytes 3981312 | tf_op jit(solution)/shard_map/all_gather | solution.py:1368
  38.1 11.2 %collective-permute-start = (bf16[2,256,384]{1,2,0:T(8,128)(2,1)S(1)}, bf16[2,256,384]{1,2,0:T(8,128)(2,1)S(1)}, u32[]{:S(2)}, u32[]{:S(2)}) collective-permute-start(bf16[2,256,384]{1,2,0:T(8,128)(2,1)S(1)} %pad_maximum_fusion.5), channel_id=1, source_target_pairs={{0,1},{1,0},{2,3},{3,2},{4,5},{5,4},{6,7},{7,6},{8,9},{9,8},{10,11... | collective-permute-start | bytes 1179656 | tf_op jit(solution)/shard_map/ppermute | solution.py:59
  39.6 25.9 %collective-permute-start.4 = (bf16[192,1728]{1,0:T(8,128)(2,1)}, bf16[192,1728]{1,0:T(8,128)(2,1)}, u32[]{:S(2)}, u32[]{:S(2)}) collective-permute-start(bf16[192,1728]{1,0:T(8,128)(2,1)} %collective-permute-done.3), channel_id=1, source_target_pairs={{4,8},{8,12},{5,9},{9,13},{6,10},{10,14},{7,11},{11,15},{20,24},{2... | collective-permute-start | bytes 1990664 | tf_op jit(solution)/shard_map/ppermute | solution.py:121
  41.2 25.8 %collective-permute-start.7 = (bf16[192,1728]{1,0:T(8,128)(2,1)}, bf16[192,1728]{1,0:T(8,128)(2,1)}, u32[]{:S(2)}, u32[]{:S(2)}) collective-permute-start(bf16[192,1728]{1,0:T(8,128)(2,1)} %collective-permute-done.6), channel_id=1, source_target_pairs={{4,0},{8,4},{5,1},{9,5},{6,2},{10,6},{7,3},{11,7},{20,16},{24,20},... | collective-permute-start | bytes 1990664 | tf_op jit(solution)/shard_map/ppermute | solution.py:126
  45.4 25.3 %collective-permute-start.9 = (bf16[3,192,1728]{2,1,0:T(8,128)(2,1)}, bf16[3,192,1728]{2,1,0:T(8,128)(2,1)}, u32[]{:S(2)}, u32[]{:S(2)}) collective-permute-start(bf16[3,192,1728]{2,1,0:T(8,128)(2,1)} %pad_maximum_fusion.mine_ref), channel_id=1, source_target_pairs={{0,16},{16,0},{1,17},{17,1},{2,18},{18,2},{3,19},{19,3},{4,20},{20... | collective-permute-start | bytes 5971976 | tf_op jit(solution)/shard_map/ppermute | solution.py:59
  45.4 20.1 %collective-permute-start.1 = (bf16[2,256,384]{1,2,0:T(8,128)(2,1)S(1)}, bf16[2,256,384]{1,2,0:T(8,128)(2,1)}, u32[]{:S(2)}, u32[]{:S(2)}) collective-permute-start(bf16[2,256,384]{1,2,0:T(8,128)(2,1)S(1)} %pad_maximum_fusion.5), channel_id=1, source_target_pairs={{0,2},{1,3},{2,0},{3,1},{4,6},{5,7},{6,4},{7,5},{8,10},{9,11},{10,... | collective-permute-start | bytes 1179656 | tf_op jit(solution)/shard_map/ppermute | solution.py:59
  49.3 16.2 %collective-permute-start.2 = (bf16[2,256,384]{1,2,0:T(8,128)(2,1)S(1)}, bf16[2,256,384]{1,2,0:T(8,128)(2,1)}, u32[]{:S(2)}, u32[]{:S(2)}) collective-permute-start(bf16[2,256,384]{1,2,0:T(8,128)(2,1)S(1)} %pad_maximum_fusion.5), channel_id=1, source_target_pairs={{0,3},{1,2},{2,1},{3,0},{4,7},{5,6},{6,5},{7,4},{8,11},{9,10},{10,... | collective-permute-start | bytes 1179656 | tf_op jit(solution)/shard_map/ppermute | solution.py:59
  65.5 16.1 %collective-permute-start.5 = (bf16[192,1728]{1,0:T(8,128)(2,1)}, bf16[192,1728]{1,0:T(8,128)(2,1)}, u32[]{:S(2)}, u32[]{:S(2)}) collective-permute-start(bf16[192,1728]{1,0:T(8,128)(2,1)} %collective-permute-done.4), channel_id=1, source_target_pairs={{8,12},{9,13},{10,14},{11,15},{24,28},{25,29},{26,30},{27,31}} | collective-permute-start | bytes 1990664 | tf_op jit(solution)/shard_map/ppermute | solution.py:121
  68.2 20.3 %collective-permute-start.10 = (bf16[192,1728]{1,0:T(8,128)(2,1)}, bf16[192,1728]{1,0:T(8,128)(2,1)}, u32[]{:S(2)}, u32[]{:S(2)}) collective-permute-start(bf16[192,1728]{1,0:T(8,128)(2,1)} %collective-permute-done.7), channel_id=1, source_target_pairs={{4,0},{5,1},{6,2},{7,3},{20,16},{21,17},{22,18},{23,19}} | collective-permute-start | bytes 1990664 | tf_op jit(solution)/shard_map/ppermute | solution.py:126
  88.6 188.6 %all-gather.7.cloned.1.call-start = ((), (), s32[]{:S(2)}) async-start(), calls=%async_computation.8 | async-start | bytes 7077888 | tf_op jit(solution)/shard_map/all_gather | solution.py:1386
  119.7 15.1 %collective-permute-start.12 = (bf16[8,8,16,192]{3,2,1,0:T(8,128)(2,1)}, bf16[8,8,16,192]{3,2,1,0:T(8,128)(2,1)}, u32[]{:S(2)}, u32[]{:S(2)}) collective-permute-start(bf16[8,8,16,192]{3,2,1,0:T(8,128)(2,1)} %multiply_convert_fusion.1.refs_0_), channel_id=1, source_target_pairs={{0,1},{1,0},{2,3},{3,2},{4,5},{5,4},{6,7},{7,6},{8,9},{9,8},{10,11... | collective-permute-start | bytes 1179656 | tf_op jit(solution)/shard_map/ppermute | solution.py:59
  120.6 24.3 %collective-permute-start.13 = (bf16[8,8,16,192]{3,2,1,0:T(8,128)(2,1)}, bf16[8,8,16,192]{3,2,1,0:T(8,128)(2,1)}, u32[]{:S(2)}, u32[]{:S(2)}) collective-permute-start(bf16[8,8,16,192]{3,2,1,0:T(8,128)(2,1)} %multiply_convert_fusion.1.refs_0_), channel_id=1, source_target_pairs={{0,2},{1,3},{2,0},{3,1},{4,6},{5,7},{6,4},{7,5},{8,10},{9,11},{10,... | collective-permute-start | bytes 1179656 | tf_op jit(solution)/shard_map/ppermute | solution.py:59
  122.1 24.6 %collective-permute-start.14 = (bf16[8,8,16,192]{3,2,1,0:T(8,128)(2,1)}, bf16[8,8,16,192]{3,2,1,0:T(8,128)(2,1)}, u32[]{:S(2)}, u32[]{:S(2)}) collective-permute-start(bf16[8,8,16,192]{3,2,1,0:T(8,128)(2,1)} %multiply_convert_fusion.1.refs_0_), channel_id=1, source_target_pairs={{0,3},{1,2},{2,1},{3,0},{4,7},{5,6},{6,5},{7,4},{8,11},{9,10},{10,... | collective-permute-start | bytes 1179656 | tf_op jit(solution)/shard_map/ppermute | solution.py:59
  159.6 16.0 %collective-permute-start.17 = (f32[8,1024]{1,0:T(8,128)}, f32[8,1024]{1,0:T(8,128)}, u32[]{:S(2)}, u32[]{:S(2)}) collective-permute-start(f32[8,1024]{1,0:T(8,128)} %get-tuple-element.105), channel_id=1, source_target_pairs={{0,3},{1,2},{2,1},{3,0},{4,7},{5,6},{6,5},{7,4},{8,11},{9,10},{10,... | collective-permute-start | bytes 98312 | tf_op jit(solution)/shard_map/ppermute | solution.py:59
  161.3 14.3 %collective-permute-start.16 = (f32[8,1024]{1,0:T(8,128)}, f32[8,1024]{1,0:T(8,128)}, u32[]{:S(2)}, u32[]{:S(2)}) collective-permute-start(f32[8,1024]{1,0:T(8,128)} %get-tuple-element.105), channel_id=1, source_target_pairs={{0,2},{1,3},{2,0},{3,1},{4,6},{5,7},{6,4},{7,5},{8,10},{9,11},{10,... | collective-permute-start | bytes 98312 | tf_op jit(solution)/shard_map/ppermute | solution.py:59
  161.6 14.0 %collective-permute-start.15 = (f32[8,1024]{1,0:T(8,128)}, f32[8,1024]{1,0:T(8,128)}, u32[]{:S(2)}, u32[]{:S(2)}) collective-permute-start(f32[8,1024]{1,0:T(8,128)} %get-tuple-element.105), channel_id=1, source_target_pairs={{0,1},{1,0},{2,3},{3,2},{4,5},{5,4},{6,7},{7,6},{8,9},{9,8},{10,11... | collective-permute-start | bytes 98312 | tf_op jit(solution)/shard_map/ppermute | solution.py:59
  196.6 15.8 %collective-permute-start.20 = (bf16[1024,192]{1,0:T(8,128)(2,1)S(1)}, bf16[1024,192]{1,0:T(8,128)(2,1)S(1)}, u32[]{:S(2)}, u32[]{:S(2)}) collective-permute-start(bf16[1024,192]{1,0:T(8,128)(2,1)S(1)} %get-tuple-element.112), channel_id=1, source_target_pairs={{0,3},{1,2},{2,1},{3,0},{4,7},{5,6},{6,5},{7,4},{8,11},{9,10},{10,... | collective-permute-start | bytes 1179656 | tf_op jit(solution)/shard_map/ppermute | solution.py:59
  198.4 23.1 %collective-permute-start.19 = (bf16[1024,192]{1,0:T(8,128)(2,1)S(1)}, bf16[1024,192]{1,0:T(8,128)(2,1)S(1)}, u32[]{:S(2)}, u32[]{:S(2)}) collective-permute-start(bf16[1024,192]{1,0:T(8,128)(2,1)S(1)} %get-tuple-element.111), channel_id=1, source_target_pairs={{0,2},{1,3},{2,0},{3,1},{4,6},{5,7},{6,4},{7,5},{8,10},{9,11},{10,... | collective-permute-start | bytes 1179656 | tf_op jit(solution)/shard_map/ppermute | solution.py:59
  198.7 22.8 %collective-permute-start.18 = (bf16[1024,192]{1,0:T(8,128)(2,1)S(1)}, bf16[1024,192]{1,0:T(8,128)(2,1)S(1)}, u32[]{:S(2)}, u32[]{:S(2)}) collective-permute-start(bf16[1024,192]{1,0:T(8,128)(2,1)S(1)} %get-tuple-element.110), channel_id=1, source_target_pairs={{0,1},{1,0},{2,3},{3,2},{4,5},{5,4},{6,7},{7,6},{8,9},{9,8},{10,11... | collective-permute-start | bytes 1179656 | tf_op jit(solution)/shard_map/ppermute | solution.py:59
  211.0 62.0 %collective-permute-start.31 = (bf16[4,528,384]{2,1,0:T(8,128)(2,1)}, bf16[4,528,384]{2,1,0:T(8,128)(2,1)}, u32[]{:S(2)}, u32[]{:S(2)}) collective-permute-start(bf16[4,528,384]{2,1,0:T(8,128)(2,1)} %dynamic-slice_bitcast_fusion), channel_id=1, source_target_pairs={{0,16},{16,0},{1,17},{17,1},{2,18},{18,2},{3,19},{19,3},{4,20},{20... | collective-permute-start | bytes 4866056 | tf_op jit(solution)/shard_map/ppermute | solution.py:59
  231.5 16.9 %collective-permute-start.21 = (bf16[8,8,16,192]{3,2,1,0:T(8,128)(2,1)S(1)}, bf16[8,8,16,192]{3,2,1,0:T(8,128)(2,1)}, u32[]{:S(2)}, u32[]{:S(2)}) collective-permute-start(bf16[8,8,16,192]{3,2,1,0:T(8,128)(2,1)S(1)} %multiply_convert_fusion.refs_0_.g_ref), channel_id=1, source_target_pairs={{0,4},{4,8},{8,12},{12,0},{1,5},{5,9},{9,13},{13,1},{2,6},{6,10},{... | collective-permute-start | bytes 1179656 | tf_op jit(solution)/shard_map/ppermute | solution.py:64
  232.0 38.0 %collective-permute-start.22 = (bf16[8,8,16,192]{3,2,1,0:T(8,128)(2,1)S(1)}, bf16[8,8,16,192]{3,2,1,0:T(8,128)(2,1)}, u32[]{:S(2)}, u32[]{:S(2)}) collective-permute-start(bf16[8,8,16,192]{3,2,1,0:T(8,128)(2,1)S(1)} %multiply_convert_fusion.refs_0_.g_ref), channel_id=1, source_target_pairs={{0,8},{4,12},{8,0},{12,4},{1,9},{5,13},{9,1},{13,5},{2,10},{6,14},... | collective-permute-start | bytes 1179656 | tf_op jit(solution)/shard_map/ppermute | solution.py:64
  232.6 37.4 %collective-permute-start.23 = (bf16[8,8,16,192]{3,2,1,0:T(8,128)(2,1)S(1)}, bf16[8,8,16,192]{3,2,1,0:T(8,128)(2,1)}, u32[]{:S(2)}, u32[]{:S(2)}) collective-permute-start(bf16[8,8,16,192]{3,2,1,0:T(8,128)(2,1)S(1)} %multiply_convert_fusion.refs_0_.g_ref), channel_id=1, source_target_pairs={{0,12},{4,0},{8,4},{12,8},{1,13},{5,1},{9,5},{13,9},{2,14},{6,2},{... | collective-permute-start | bytes 1179656 | tf_op jit(solution)/shard_map/ppermute | solution.py:64
  289.0 20.9 %collective-permute-start.32 = (bf16[528,384]{1,0:T(8,128)(2,1)S(1)}, bf16[528,384]{1,0:T(8,128)(2,1)S(1)}, u32[]{:S(2)}, u32[]{:S(2)}) collective-permute-start(bf16[528,384]{1,0:T(8,128)(2,1)S(1)} %get-tuple-element.305), channel_id=1, source_target_pairs={{0,4},{4,8},{8,12},{12,0},{1,5},{5,9},{9,13},{13,1},{2,6},{6,10},{... | collective-permute-start | bytes 1216520 | tf_op jit(solution)/shard_map/ppermute | solution.py:64
  300.0 28.6 %collective-permute-start.28 = (bf16[192,1728]{1,0:T(8,128)(2,1)S(1)}, bf16[192,1728]{1,0:T(8,128)(2,1)S(1)}, u32[]{:S(2)}, u32[]{:S(2)}) collective-permute-start(bf16[192,1728]{1,0:T(8,128)(2,1)S(1)} %get-tuple-element.140.refs_0_), channel_id=1, source_target_pairs={{0,1},{1,0},{2,3},{3,2},{4,5},{5,4},{6,7},{7,6},{8,9},{9,8},{10,11... | collective-permute-start | bytes 1990664 | tf_op jit(solution)/shard_map/ppermute | solution.py:59
  300.6 31.5 %collective-permute-start.29 = (bf16[192,1728]{1,0:T(8,128)(2,1)S(1)}, bf16[192,1728]{1,0:T(8,128)(2,1)S(1)}, u32[]{:S(2)}, u32[]{:S(2)}) collective-permute-start(bf16[192,1728]{1,0:T(8,128)(2,1)S(1)} %get-tuple-element.140.refs_0_), channel_id=1, source_target_pairs={{0,2},{1,3},{2,0},{3,1},{4,6},{5,7},{6,4},{7,5},{8,10},{9,11},{10,... | collective-permute-start | bytes 1990664 | tf_op jit(solution)/shard_map/ppermute | solution.py:59
  302.0 30.1 %collective-permute-start.30 = (bf16[192,1728]{1,0:T(8,128)(2,1)S(1)}, bf16[192,1728]{1,0:T(8,128)(2,1)S(1)}, u32[]{:S(2)}, u32[]{:S(2)}) collective-permute-start(bf16[192,1728]{1,0:T(8,128)(2,1)S(1)} %get-tuple-element.140.refs_0_), channel_id=1, source_target_pairs={{0,3},{1,2},{2,1},{3,0},{4,7},{5,6},{6,5},{7,4},{8,11},{9,10},{10,... | collective-permute-start | bytes 1990664 | tf_op jit(solution)/shard_map/ppermute | solution.py:59
  303.5 23.2 %collective-permute-start.33 = (bf16[528,384]{1,0:T(8,128)(2,1)S(1)}, bf16[528,384]{1,0:T(8,128)(2,1)S(1)}, u32[]{:S(2)}, u32[]{:S(2)}) collective-permute-start(bf16[528,384]{1,0:T(8,128)(2,1)S(1)} %get-tuple-element.304), channel_id=1, source_target_pairs={{0,8},{4,12},{8,0},{12,4},{1,9},{5,13},{9,1},{13,5},{2,10},{6,14},... | collective-permute-start | bytes 1216520 | tf_op jit(solution)/shard_map/ppermute | solution.py:64
  309.9 18.7 %collective-permute-start.34 = (bf16[528,384]{1,0:T(8,128)(2,1)S(1)}, bf16[528,384]{1,0:T(8,128)(2,1)S(1)}, u32[]{:S(2)}, u32[]{:S(2)}) collective-permute-start(bf16[528,384]{1,0:T(8,128)(2,1)S(1)} %get-tuple-element.303), channel_id=1, source_target_pairs={{0,12},{4,0},{8,4},{12,8},{1,13},{5,1},{9,5},{13,9},{2,14},{6,2},{... | collective-permute-start | bytes 1216520 | tf_op jit(solution)/shard_map/ppermute | solution.py:64
  352.7 9.9 %collective-permute-start.39 = (f32[1,24,768]{2,1,0:T(8,128)S(1)}, f32[1,24,768]{2,1,0:T(8,128)S(1)}, u32[]{:S(2)}, u32[]{:S(2)}) collective-permute-start(f32[1,24,768]{2,1,0:T(8,128)S(1)} %get-tuple-element.295), channel_id=1, source_target_pairs={{0,12},{4,0},{8,4},{12,8},{1,13},{5,1},{9,5},{13,9},{2,14},{6,2},{... | collective-permute-start | bytes 221192 | tf_op jit(solution)/shard_map/ppermute | solution.py:64
  355.7 40.2 %all-to-all-start.5 = ((bf16[4,192,1056]{2,1,0:T(8,128)(2,1)}), bf16[4,192,1056]{2,1,0:T(8,128)(2,1)}, u32[]{:S(2)}, u32[]{:S(2)}) async-start(bf16[4,192,1056]{2,1,0:T(8,128)(2,1)} %broadcast_in_dim.99), calls=%async_computation.5 | async-start | bytes 3538944 | tf_op jit(solution)/shard_map/all_to_all | solution.py:104
  367.7 21.5 %collective-permute-start.42 = (f32[4,1,24,768]{3,2,1,0:T(8,128)S(1)}, f32[4,1,24,768]{3,2,1,0:T(8,128)S(1)}, u32[]{:S(2)}, u32[]{:S(2)}) collective-permute-start(f32[4,1,24,768]{3,2,1,0:T(8,128)S(1)} %constant_dynamic-slice_fusion.1.refs_0_), channel_id=1, source_target_pairs={{0,1},{1,0},{2,3},{3,2},{4,5},{5,4},{6,7},{7,6},{8,9},{9,8},{10,11... | collective-permute-start | bytes 884744 | tf_op jit(solution)/shard_map/ppermute | solution.py:59
  369.4 19.9 %collective-permute-start.43 = (f32[4,1,24,768]{3,2,1,0:T(8,128)S(1)}, f32[4,1,24,768]{3,2,1,0:T(8,128)S(1)}, u32[]{:S(2)}, u32[]{:S(2)}) collective-permute-start(f32[4,1,24,768]{3,2,1,0:T(8,128)S(1)} %constant_dynamic-slice_fusion.1.refs_0_), channel_id=1, source_target_pairs={{0,2},{1,3},{2,0},{3,1},{4,6},{5,7},{6,4},{7,5},{8,10},{9,11},{10,... | collective-permute-start | bytes 884744 | tf_op jit(solution)/shard_map/ppermute | solution.py:59
  370.9 23.6 %collective-permute-start.44 = (f32[4,1,24,768]{3,2,1,0:T(8,128)S(1)}, f32[4,1,24,768]{3,2,1,0:T(8,128)S(1)}, u32[]{:S(2)}, u32[]{:S(2)}) collective-permute-start(f32[4,1,24,768]{3,2,1,0:T(8,128)S(1)} %constant_dynamic-slice_fusion.1.refs_0_), channel_id=1, source_target_pairs={{0,3},{1,2},{2,1},{3,0},{4,7},{5,6},{6,5},{7,4},{8,11},{9,10},{10,... | collective-permute-start | bytes 884744 | tf_op jit(solution)/shard_map/ppermute | solution.py:59
  395.9 13.7 %all-to-all-start.3 = ((bf16[4,256,384]{2,1,0:T(8,128)(2,1)}), bf16[4,256,384]{2,1,0:T(8,128)(2,1)}, u32[]{:S(2)}, u32[]{:S(2)}) async-start(bf16[4,256,384]{2,1,0:T(8,128)(2,1)} %pad_maximum_fusion.4), calls=%async_computation.3 | async-start | bytes 1572864 | tf_op jit(solution)/shard_map/all_to_all | solution.py:1466
  404.6 10.2 %collective-permute-start.45 = (f32[4,1,24,768]{3,2,1,0:T(8,128)S(1)}, f32[4,1,24,768]{3,2,1,0:T(8,128)}, u32[]{:S(2)}, u32[]{:S(2)}) collective-permute-start(f32[4,1,24,768]{3,2,1,0:T(8,128)S(1)} %constant_dynamic-slice_fusion.1.refs_0_), channel_id=1, source_target_pairs={{0,16},{16,0},{1,17},{17,1},{2,18},{18,2},{3,19},{19,3},{4,20},{20... | collective-permute-start | bytes 884744 | tf_op jit(solution)/shard_map/ppermute | solution.py:59
  415.6 12.9 %collective-permute-start.52 = (f32[1,48,768]{2,1,0:T(8,128)}, f32[1,48,768]{2,1,0:T(8,128)}, u32[]{:S(2)}, u32[]{:S(2)}) collective-permute-start(f32[1,48,768]{2,1,0:T(8,128)} %get-tuple-element.317), channel_id=1, source_target_pairs={{0,12},{4,0},{8,4},{12,8},{1,13},{5,1},{9,5},{13,9},{2,14},{6,2},{... | collective-permute-start | bytes 442376 | tf_op jit(solution)/shard_map/ppermute | solution.py:64
  418.2 13.4 %collective-permute-start.51 = (f32[1,48,768]{2,1,0:T(8,128)S(1)}, f32[1,48,768]{2,1,0:T(8,128)}, u32[]{:S(2)}, u32[]{:S(2)}) collective-permute-start(f32[1,48,768]{2,1,0:T(8,128)S(1)} %get-tuple-element.318), channel_id=1, source_target_pairs={{0,8},{4,12},{8,0},{12,4},{1,9},{5,13},{9,1},{13,5},{2,10},{6,14},... | collective-permute-start | bytes 442376 | tf_op jit(solution)/shard_map/ppermute | solution.py:64
  419.1 12.5 %collective-permute-start.50 = (f32[1,48,768]{2,1,0:T(8,128)S(1)}, f32[1,48,768]{2,1,0:T(8,128)}, u32[]{:S(2)}, u32[]{:S(2)}) collective-permute-start(f32[1,48,768]{2,1,0:T(8,128)S(1)} %get-tuple-element.316), channel_id=1, source_target_pairs={{0,4},{4,8},{8,12},{12,0},{1,5},{5,9},{9,13},{13,1},{2,6},{6,10},{... | collective-permute-start | bytes 442376 | tf_op jit(solution)/shard_map/ppermute | solution.py:64
  433.2 13.6 %collective-permute-start.54 = (f32[1,48,768]{2,1,0:T(8,128)S(1)}, f32[1,48,768]{2,1,0:T(8,128)S(1)}, u32[]{:S(2)}, u32[]{:S(2)}) collective-permute-start(f32[1,48,768]{2,1,0:T(8,128)S(1)} %get-tuple-element.293), channel_id=1, source_target_pairs={{0,8},{4,12},{8,0},{12,4},{1,9},{5,13},{9,1},{13,5},{2,10},{6,14},... | collective-permute-start | bytes 442376 | tf_op jit(solution)/shard_map/ppermute | solution.py:64
  434.1 12.6 %collective-permute-start.55 = (f32[1,48,768]{2,1,0:T(8,128)S(1)}, f32[1,48,768]{2,1,0:T(8,128)S(1)}, u32[]{:S(2)}, u32[]{:S(2)}) collective-permute-start(f32[1,48,768]{2,1,0:T(8,128)S(1)} %get-tuple-element.293), channel_id=1, source_target_pairs={{0,4},{4,8},{8,12},{12,0},{1,5},{5,9},{9,13},{13,1},{2,6},{6,10},{... | collective-permute-start | bytes 442376 | tf_op jit(solution)/shard_map/ppermute | solution.py:64
  446.9 38.7 %collective-permute-start.56 = (f32[4,1,48,768]{3,2,1,0:T(8,128)S(1)}, f32[4,1,48,768]{3,2,1,0:T(8,128)}, u32[]{:S(2)}, u32[]{:S(2)}) collective-permute-start(f32[4,1,48,768]{3,2,1,0:T(8,128)S(1)} %constant_dynamic-slice_fusion.refs_0_), channel_id=1, source_target_pairs={{0,1},{1,0},{2,3},{3,2},{4,5},{5,4},{6,7},{7,6},{8,9},{9,8},{10,11... | collective-permute-start | bytes 1769480 | tf_op jit(solution)/shard_map/ppermute | solution.py:59
  447.4 38.2 %collective-permute-start.57 = (f32[4,1,48,768]{3,2,1,0:T(8,128)S(1)}, f32[4,1,48,768]{3,2,1,0:T(8,128)}, u32[]{:S(2)}, u32[]{:S(2)}) collective-permute-start(f32[4,1,48,768]{3,2,1,0:T(8,128)S(1)} %constant_dynamic-slice_fusion.refs_0_), channel_id=1, source_target_pairs={{0,2},{1,3},{2,0},{3,1},{4,6},{5,7},{6,4},{7,5},{8,10},{9,11},{10,... | collective-permute-start | bytes 1769480 | tf_op jit(solution)/shard_map/ppermute | solution.py:59
  448.3 37.2 %collective-permute-start.58 = (f32[4,1,48,768]{3,2,1,0:T(8,128)S(1)}, f32[4,1,48,768]{3,2,1,0:T(8,128)}, u32[]{:S(2)}, u32[]{:S(2)}) collective-permute-start(f32[4,1,48,768]{3,2,1,0:T(8,128)S(1)} %constant_dynamic-slice_fusion.refs_0_), channel_id=1, source_target_pairs={{0,3},{1,2},{2,1},{3,0},{4,7},{5,6},{6,5},{7,4},{8,11},{9,10},{10,... | collective-permute-start | bytes 1769480 | tf_op jit(solution)/shard_map/ppermute | solution.py:59
  451.8 64.9 %all-to-all-start.6 = ((f32[8,32,1536]{2,1,0:T(8,128)}), f32[8,32,1536]{2,1,0:T(8,128)}, u32[]{:S(2)}, u32[]{:S(2)}) async-start(f32[8,32,1536]{2,1,0:T(8,128)} %broadcast_in_dim.100), calls=%async_computation.6 | async-start | bytes 3145728 | tf_op jit(solution)/shard_map/all_to_all | solution.py:104
  (146 other events, 1488.1 us)
Sparse Core Ops, SparseCore 0:
  88.7 39.4 all-gather.4
  129.8 63.5 all-gather.6

commit v4 on v3

--- a/solution.py
+++ b/solution.py
@@ -657,11 +657,14 @@
 
 def weight_one_kernel(groups, where_ref, inverse_ref, *refs):
     pieces = refs[:groups]
-    all_ref, moment_ref, out_ref, low_ref, pad_ref, pool_ref, grads, inputs_ref, sem = refs[groups:]
+    all_ref, old_ref, out_ref, low_ref, pad_ref, pool_ref, grads, inputs_ref, moment_ref, sem = refs[
+        groups:
+    ]
     copies = [
         pltpu.make_async_copy(piece, grads.at[g], sem.at[g]) for g, piece in enumerate(pieces)
     ]
     copies.append(pltpu.make_async_copy(all_ref, inputs_ref, sem.at[groups]))
+    copies.append(pltpu.make_async_copy(old_ref, moment_ref, sem.at[groups + 1]))
     for copy in copies:
         copy.start()
     h2, w2, n, c = grads.shape[1:]
@@ -681,6 +684,7 @@
             shifted = pad_ref[pl.ds(2 - dy, h2), pl.ds(2 - dx, w2)].astype(f32)
             pool_ref[j, g * size : (g + 1) * size, :] = flat(sum_two(shifted)).astype(bf16)
     copies[groups].wait()
+    copies[groups + 1].wait()
     inverse = inverse_ref[0, 0]
     for q in range(groups + 1):
         i = lax.rem(d + q, groups)
@@ -709,14 +713,15 @@
             jax.ShapeDtypeStruct(moment.shape, f32),
             jax.ShapeDtypeStruct(moment.shape, bf16),
         ),
-        in_specs=[smem, smem] + [pl.BlockSpec(memory_space=pl.ANY)] * (groups + 1) + [vmem],
+        in_specs=[smem, smem] + [pl.BlockSpec(memory_space=pl.ANY)] * (groups + 2),
         out_specs=(vmem, vmem),
         scratch_shapes=[
             pltpu.VMEM((h2 + 2, w2 + 2, n, c), bf16),
             pltpu.VMEM((2, groups * h2 * w2 * n // 4, c), bf16),
             pltpu.VMEM((groups,) + grads[0].shape, bf16),
             pltpu.VMEM(inputs.shape, bf16),
-            pltpu.SemaphoreType.DMA((groups + 1,)),
+            pltpu.VMEM(moment.shape, f32),
+            pltpu.SemaphoreType.DMA((groups + 2,)),
         ],
         compiler_params=kernel_params(28),
         cost_estimate=pl.CostEstimate(flops=4 * flops, bytes_accessed=0, transcendentals=0),
@@ -1363,6 +1368,7 @@
     weight_one = weight_one.reshape(9, ranks * c_in, c_out)
 
     hidden, sums_high = conv_one(row, pairs, weight_one, (h, w, n))
+    totals_high = near_sum(sums_high)
     other = jnp.concatenate([conv_second.T, conv_skip.T], axis=1).astype(bf16)
     other = jnp.pad(other, ((0, 0), (0, -other.shape[1] % 128)))
     others = lax.all_gather(after(other, below[3], above[3]), GROUP, axis=0)
@@ -1374,21 +1380,20 @@
         (conv_second.shape[0], conv_skip.shape[0]),
     )
     weight_two = weight_two.reshape(9, ranks * c_out, c_out)
-    totals_high = near_sum(sums_high)
     centre_two, spread_two = moments_of(totals_high, count_high)
     centre_two, spread_two = per_image(centre_two, n), per_image(spread_two, n)
     normed_two = (hidden - centre_two) * spread_two
     pre_two = normed_two * gain_two + mods_two[:, 1]
     acted_two = jax.nn.silu(pre_two).astype(bf16)
     twos = row_gather(acted_two)
-    kept_pairs = [after(pair, sums_high) for pair in pairs]
+    colour = jnp.pad(
+        jnp.transpose(colour_conv, (0, 2, 1)).astype(bf16), ((0, 0), (0, PAD - 3), (0, 0))
+    )
+    summed, active, picture = conv_two(row, twos, pairs, weight_two, weight_skip, colour)
+    kept_pairs = [after(pair, active) for pair in pairs]
     turned = jnp.concatenate([jnp.transpose(pair[0]) for pair in kept_pairs], axis=0)
     ones_all = lax.all_gather(after(turned, others), GROUP, axis=0)
 
-    colour = jnp.pad(
-        jnp.transpose(colour_conv, (0, 2, 1)).astype(bf16), ((0, 0), (0, PAD - 3), (0, 0))
-    )
-    summed, active, picture = conv_two(row, twos, pairs, weight_two, weight_skip, colour)
     picture = row_sum(picture)
 
     first_taps = jnp.pad(disc_first.reshape(9, 3, -1), ((0, 0), (0, PAD - 3), (0, 0)))
@@ -1411,8 +1416,8 @@
     packed = weight_pack(
         row,
         gpad,
-        [jnp.transpose(flat(after(two, active))) for two in twos],
-        [jnp.transpose(after(pair, active)[1]) for pair in pairs],
+        [jnp.transpose(flat(after(two, gpad))) for two in twos],
+        [jnp.transpose(after(pair, gpad)[1]) for pair in pairs],
         groups,
     )
     kept = near_halves(packed.reshape((2, groups // 2) + packed.shape[1:]))
@@ -1434,13 +1439,14 @@
     hidden_all = straight(grad_hidden)
     scaled = inverse.reshape(1, 1)
     hidden_all = straight(grad_hidden)
-    hidden_all = both_cores(list(together(*hidden_all)))
+    *hidden_all, kept, wire = together(*hidden_all, kept, kept.astype(bf16))
+    hidden_all = both_cores(hidden_all)
     moment_one, low_one = weight_one_moment(
         where, scaled, hidden_all, ones_all, momentum_first.T
     )
-    kept, grad_hidden = after(kept, low_one), after(grad_hidden, low_one)
+    kept, wire, grad_hidden, _ = together(kept, wire, grad_hidden, low_one)
     one_held = row_gather(low_one)
-    shares = near_blocks(kept, kept.astype(bf16))
+    shares = near_blocks(kept, wire)
     backs = back_in(row, grad_hidden, weight_one, ranks)
     *one_held, shares[1], shares[2], shares[3], backs = together(
         *one_held, *shares[1:], jnp.stack(backs, axis=0)

time: 544 us -> 528 us (0.971)
  waiting for transfers between devices: 177 us -> 166 us
  local copies, waits for them, and re-layouts: 66.7 us -> 58.5 us
    ppermute x36, waiting for transfers between devices: 64.2 us -> 54.4 us  [axis_swap(): return lax.ppermute(value, axis, [(i, i ^ k) for i in range(n)])]
    ppermute x18, waiting for transfers between devices: 78.8 us -> 73 us  [axis_shift(): return lax.ppermute(value, axis, [(i, (i + k) % n) for i in range(n)])]
    unnamed x267 -> x257, local copies, waits for them, and re-layouts: 27.9 us -> 27.3 us
  transfers between devices with their start and end apart: 68 -> 68, of which waited for: 28 -> 31; matrix products, arithmetic and copies ran while one was open for 13% -> 12% of each run, Pallas kernels for 21% -> 20%
where the time goes in v4:
time: 528 us; the launch traced here: 519 us
  waiting for transfers between devices  166 us (31%)
  Pallas kernels  121 us (23%)
  starting transfers between devices  102 us (19%)
  local copies, waits for them, and re-layouts  58.5 us (11%)
  other arithmetic  39.7 us (8%)
  between operations  17.7 us (3%)
  blocking collectives  8.15 us (2%)
  matrix products  5.9 us (1%)
    ppermute x18, waiting for transfers between devices, axis_shift(): return lax.ppermute(value, axis, [(i, (i + k) % n) for i in range(n)])  73 us
    ppermute x36, waiting for transfers between devices, axis_swap(): return lax.ppermute(value, axis, [(i, i ^ k) for i in range(n)])  54.4 us
    pallas_call x2, Pallas kernels, newton(): pl.pallas_call(functools.partial(newton_kernel, count, sides), out_shape=...  50.5 us
    ppermute x18, starting transfers between devices, axis_shift(): return lax.ppermute(value, axis, [(i, (i + k) % n) for i in range(n)])  33.8 us
    ppermute x36, starting transfers between devices, axis_swap(): return lax.ppermute(value, axis, [(i, i ^ k) for i in range(n)])  29.6 us
    unnamed x257, local copies, waits for them, and re-layouts  27.3 us
    all_to_all x5, starting transfers between devices, spread(): lax.all_to_all(jnp.broadcast_to(value[None], (n,) + value.shape), axis, 0...  21.5 us
    all_to_all x5, waiting for transfers between devices, spread(): lax.all_to_all(jnp.broadcast_to(value[None], (n,) + value.shape), axis, 0...  19.2 us
  transfers between devices with their start and end apart: 68, of which 31 were waited for; matrix products, arithmetic and copies ran while one was open for 12% of the time, Pallas kernels for 20%

profile of v4, /device:TPU:0, one launch (start us, length us, event | category | flops | bytes accessed | tf_op | source)
XLA Modules:
  0.0 519.1 jit_solution(9979591061574802976)
XLA Ops:
  9.6 6.0 %collective-permute-start.3 = (bf16[192,1728]{1,0:T(8,128)(2,1)}, bf16[192,1728]{1,0:T(8,128)(2,1)}, u32[]{:S(2)}, u32[]{:S(2)}) collective-permute-start(bf16[192,1728]{1,0:T(8,128)(2,1)} %bitcast_convert_fusion.2), channel_id=1, source_target_pairs={{0,4},{4,8},{8,12},{1,5},{5,9},{9,13},{2,6},{6,10},{10,14},{3,7},{... | collective-permute-start | bytes 1990664 | tf_op jit(solution)/shard_map/ppermute | solution.py:121
  19.6 5.9 %all-to-all-start = ((f32[8,5,384]{2,1,0:T(8,128)}), f32[8,5,384]{2,1,0:T(8,128)S(1)}, u32[]{:S(2)}, u32[]{:S(2)}) async-start(f32[8,5,384]{2,1,0:T(8,128)} %broadcast_in_dim.37), calls=%async_computation | async-start | bytes 196608 | tf_op jit(solution)/shard_map/all_to_all | solution.py:104
  27.4 9.8 %all-to-all-done = f32[8,5,384]{2,1,0:T(8,128)S(1)} async-done(((f32[8,5,384]{2,1,0:T(8,128)}), f32[8,5,384]{2,1,0:T(8,128)S(1)}, u32[]{:S(2)}, u32[]{:S(2)}) %all-to-all-start) | async-done | bytes 61472 | tf_op jit(solution)/shard_map/all_to_all | solution.py:104
  42.4 3.1 pad_maximum_fusion.mine_ref
  52.7 12.7 %collective-permute-done.1 = bf16[2,256,384]{1,2,0:T(8,128)(2,1)S(1)} collective-permute-done((bf16[2,256,384]{1,2,0:T(8,128)(2,1)S(1)}, bf16[2,256,384]{1,2,0:T(8,128)(2,1)S(1)}, u32[]{:S(2)}, u32[]{:S(2)}) %collective-permute-start.1) | collective-permute-done | bytes 393248 | tf_op jit(solution)/shard_map/ppermute | solution.py:59
  70.7 5.6 %place.4.refs_0_ = bf16[13824,192]{1,0:T(8,128)(2,1)S(1)} custom-call(s32[6]{0:T(128)S(1)} %stack.155.index_ref, bf16[3,192,1728]{2,1,0:T(8,128)(2,1)} %pad_maximum_fusion.mine_ref, bf16[3,192,1728]{2,1,0:T(8,128)(2,1)} %collective-permute-done.9.other_ref), custom_call_target="tpu_custom_call" | custom-call | tf_op jit(solution)/shard_map/place/pallas_call | solution.py:632
  78.7 2.9 copy-done.2
  81.6 7.0 %collective-permute-done.10 = bf16[192,1728]{1,0:T(8,128)(2,1)} collective-permute-done((bf16[192,1728]{1,0:T(8,128)(2,1)}, bf16[192,1728]{1,0:T(8,128)(2,1)}, u32[]{:S(2)}, u32[]{:S(2)}) %collective-permute-start.10) | collective-permute-done | bytes 663584 | tf_op jit(solution)/shard_map/ppermute | solution.py:126
  93.8 3.3 copy-done.3
  99.4 4.4 conv_one.1
  104.5 3.3 all-to-all-start.1
  108.5 5.5 %all-to-all-done.1 = f32[8,4,192]{2,1,0:T(4,128)S(1)} async-done(((f32[8,4,192]{2,1,0:T(4,128)}), f32[8,4,192]{2,1,0:T(4,128)S(1)}, u32[]{:S(2)}, u32[]{:S(2)}) %all-to-all-start.1) | async-done | bytes 24608 | tf_op jit(solution)/shard_map/all_to_all | solution.py:104
  118.7 9.6 %all-gather.5.cloned.1.call-done = bf16[1536,1152]{1,0:T(8,128)(2,1)} async-done(((bf16[192,1152]{1,0:T(8,128)(2,1)}), bf16[1536,1152]{1,0:T(8,128)(2,1)}) %all-gather.5.cloned.1.call-update) | async-done | bytes 3538960 | tf_op jit(solution)/shard_map/all_gather | solution.py:1374
  130.6 2.8 place.7
  133.4 8.5 %collective-permute-done.14.refs_3_ = bf16[8,8,16,192]{3,2,1,0:T(8,128)(2,1)} collective-permute-done((bf16[8,8,16,192]{3,2,1,0:T(8,128)(2,1)S(1)}, bf16[8,8,16,192]{3,2,1,0:T(8,128)(2,1)}, u32[]{:S(2)}, u32[]{:S(2)}) %collective-permute-start.14) | collective-permute-done | bytes 393248 | tf_op jit(solution)/shard_map/ppermute | solution.py:59
  141.9 10.2 %conv_two.1 = (f32[8,8,16,192]{3,2,1,0:T(8,128)S(1)}, bf16[8,8,16,192]{3,2,1,0:T(8,128)(2,1)S(1)}, f32[8,1024]{1,0:T(8,128)S(1)}) custom-call(s32[1]{0:T(128)} %bitcast.row_ref, bf16[8,8,16,192]{3,2,1,0:T(8,128)(2,1)S(1)} %multiply_convert_fusion.1.refs_0_, bf16[8,8,16,192]{3,2,1,0:T(8,128)(2,1)} %collective-permute-done.12.refs_1_, ...), custom_call_target="tpu_custom_call" | custom-call | tf_op jit(solution)/shard_map/conv_two/pallas_call | solution.py:278
  161.9 5.7 %critic.1 = (bf16[1024,128]{1,0:T(8,128)(2,1)S(1)}, f32[8,128]{1,0:T(8,128)S(1)}) custom-call(f32[8,1024]{1,0:T(8,128)S(1)} %add_add_fusion.1.pic_ref, bf16[9,8,96]{2,1,0:T(8,128)(2,1)S(1)} %pad.31.first_ref, bf16[9,96,96]{2,1,0:T(8,128)(2,1)S(1)} %bitcast.286, bf16[8,96]{1,0:T(8,128)(2,1)S(1)} %pad.32.skip_ref, f32[16,96]{1,0:T(8,128)S(1)} %convolution_add_fusion.head_ref, ...), custom_call_target="tpu_custom_call" | custom-call | tf_op jit(solution)/shard_map/critic/pallas_call | solution.py:358
  171.5 8.5 %back_two.1 = (bf16[10,10,16,192]{3,2,1,0:T(8,128)(2,1)S(1)}, f32[128,192]{1,0:T(8,128)S(1)}, bf16[1024,192]{1,0:T(8,128)(2,1)S(1)}, bf16[1024,192]{1,0:T(8,128)...) custom-call(s32[1]{0:T(128)} %bitcast.row_ref, bf16[1024,128]{1,0:T(8,128)(2,1)S(1)} %get-tuple-element.109.g_ref, ...), custom_call_target="tpu_custom_call" | custom-call | tf_op jit(solution)/shard_map/back_two/pallas_call | solution.py:403
  195.6 7.7 %weight_two.1 = bf16[8,528,384]{2,1,0:T(8,128)(2,1)S(1)} custom-call(s32[1]{0:T(128)} %bitcast.row_ref, bf16[10,10,16,192]{3,2,1,0:T(8,128)(2,1)S(1)} %copy-done.44, bf16[192,1024]{1,0:T(8,128)(2,1)S(1)} %bitcast.291, bf16[192,1024]{1,0:T(8,128)(2,1)S(1)} %bitcast.292, bf16[192,1024]{1,0:T(8,128)(2,1)S(1)} %bitcast.293, bf16[192,1024]{1,0:T(8,128)(2,1)S(1)} %bitcast.294, ...), custom_call_target="tpu_custom_call" | custom-call | flops 8153726976 | tf_op jit(solution)/shard_map/weight_two/pallas_call | solution.py:772
  209.6 8.1 %all_to_all.35 = f32[8,4,192]{2,1,0:T(4,128)S(1)} all-to-all(f32[8,4,192]{2,1,0:T(4,128)S(1)} %broadcast_in_dim.46), channel_id=1, replica_groups=mesh['half'=2,'dp'=4,'row'=4] {'half','dp'}, dimensions={0} | all-to-all | bytes 49152 | tf_op jit(solution)/shard_map/all_to_all | solution.py:104
  220.0 3.1 collective-permute-start.23
  223.1 4.7 fusion.62
  227.8 8.1 %collective-permute-done.21.refs_1_ = bf16[8,8,16,192]{3,2,1,0:T(8,128)(2,1)} collective-permute-done((bf16[8,8,16,192]{3,2,1,0:T(8,128)(2,1)}, bf16[8,8,16,192]{3,2,1,0:T(8,128)(2,1)}, u32[]{:S(2)}, u32[]{:S(2)}) %collective-permute-start.21) | collective-permute-done | bytes 393248 | tf_op jit(solution)/shard_map/ppermute | solution.py:64
  236.0 21.7 %collective-permute-done.22.refs_2_ = bf16[8,8,16,192]{3,2,1,0:T(8,128)(2,1)} collective-permute-done((bf16[8,8,16,192]{3,2,1,0:T(8,128)(2,1)}, bf16[8,8,16,192]{3,2,1,0:T(8,128)(2,1)}, u32[]{:S(2)}, u32[]{:S(2)}) %collective-permute-start.22) | collective-permute-done | bytes 393248 | tf_op jit(solution)/shard_map/ppermute | solution.py:64
  262.1 2.8 copy-done.41
  266.3 7.3 %weight_one.1 = (f32[192,1728]{1,0:T(8,128)}, bf16[192,1728]{1,0:T(8,128)(2,1)S(1)}) custom-call(s32[3]{0:T(128)S(1)} %pad_add_fusion.where_ref, f32[1,1]{1,0:T(1,128)} %bitcast.7.inverse_ref, bf16[8,8,16,192]{3,2,1,0:T(8,128)(2,1)} %multiply_convert_fusion.refs_0_.g_ref, bf16[8,8,16,192]{3,2,1,0:T(8,128)(2,1)} %collective-permute-done.21.refs_1_, ...), custom_call_target="tpu_custom_call" | custom-call | flops 5435817984 | tf_op jit(solution)/shard_map/weight_one/pallas_call | solution.py:710
  273.8 11.0 %collective-permute-start.32 = (bf16[528,384]{1,0:T(8,128)(2,1)S(1)}, bf16[528,384]{1,0:T(8,128)(2,1)S(1)}, u32[]{:S(2)}, u32[]{:S(2)}) collective-permute-start(bf16[528,384]{1,0:T(8,128)(2,1)S(1)} %get-tuple-element.313), channel_id=1, source_target_pairs={{0,4},{4,8},{8,12},{12,0},{1,5},{5,9},{9,13},{13,1},{2,6},{6,10},{... | collective-permute-start | bytes 1216520 | tf_op jit(solution)/shard_map/ppermute | solution.py:64
  288.5 6.2 %collective-permute-done.32.refs_1_ = bf16[528,384]{1,0:T(8,128)(2,1)S(1)} collective-permute-done((bf16[528,384]{1,0:T(8,128)(2,1)S(1)}, bf16[528,384]{1,0:T(8,128)(2,1)S(1)}, u32[]{:S(2)}, u32[]{:S(2)}) %collective-permute-start.32) | collective-permute-done | bytes 405536 | tf_op jit(solution)/shard_map/ppermute | solution.py:64
  295.9 5.5 %back_one.1 = (bf16[256,384]{1,0:T(8,128)(2,1)S(1)}, bf16[256,384]{1,0:T(8,128)(2,1)S(1)}, bf16[256,384]{1,0:T(8,128)(2,1)S(1)}, bf16[256,384]{1,0:T(8,128)(2,1)S(1)}) custom-call(s32[1]{0:T(128)} %bitcast.row_ref, bf16[8,8,16,192]{3,2,1,0:T(8,128)(2,1)} %multiply_convert_fusion.refs_0_.g_ref, bf16[9,1536,192]{2,1,0:T(8,128)(2,1)S(1)} %bitcast.273), custom_call_target="tpu_custom_call" | custom-call | flops 4076863488 | tf_op jit(solution)/shard_map/back_one/pallas_call | solution.py:1043
  302.4 9.2 %collective-permute-done.33.refs_2_ = bf16[528,384]{1,0:T(8,128)(2,1)S(1)} collective-permute-done((bf16[528,384]{1,0:T(8,128)(2,1)S(1)}, bf16[528,384]{1,0:T(8,128)(2,1)S(1)}, u32[]{:S(2)}, u32[]{:S(2)}) %collective-permute-start.33) | collective-permute-done | bytes 405536 | tf_op jit(solution)/shard_map/ppermute | solution.py:64
  313.7 4.4 collective-permute-done.30.refs_2_
  324.6 5.4 %collective-permute-start.38 = (f32[1,24,768]{2,1,0:T(8,128)S(1)}, f32[1,24,768]{2,1,0:T(8,128)S(1)}, u32[]{:S(2)}, u32[]{:S(2)}) collective-permute-start(f32[1,24,768]{2,1,0:T(8,128)S(1)} %get-tuple-element.329), channel_id=1, source_target_pairs={{0,12},{4,0},{8,4},{12,8},{1,13},{5,1},{9,5},{13,9},{2,14},{6,2},{... | collective-permute-start | bytes 221192 | tf_op jit(solution)/shard_map/ppermute | solution.py:64
  332.6 5.0 collective-permute-done.37
  340.7 4.5 all-to-all-start.5
  347.6 5.0 collective-permute-done.40
  359.2 15.1 %collective-permute-done.42.refs_1_ = f32[4,1,24,768]{3,2,1,0:T(8,128)S(1)} collective-permute-done((f32[4,1,24,768]{3,2,1,0:T(8,128)S(1)}, f32[4,1,24,768]{3,2,1,0:T(8,128)S(1)}, u32[]{:S(2)}, u32[]{:S(2)}) %collective-permute-start.42) | collective-permute-done | bytes 294944 | tf_op jit(solution)/shard_map/ppermute | solution.py:59
  374.3 5.2 %collective-permute-done.44.refs_3_ = f32[4,1,24,768]{3,2,1,0:T(8,128)S(1)} collective-permute-done((f32[4,1,24,768]{3,2,1,0:T(8,128)S(1)}, f32[4,1,24,768]{3,2,1,0:T(8,128)S(1)}, u32[]{:S(2)}, u32[]{:S(2)}) %collective-permute-start.44) | collective-permute-done | bytes 294944 | tf_op jit(solution)/shard_map/ppermute | solution.py:59
  380.8 4.2 all-to-all-start.3
  391.2 3.3 all-to-all-done.3
  398.6 2.7 collective-permute-start.52
  403.4 3.3 all-to-all-start.4
  407.5 4.0 all-to-all-done.4
  411.5 3.2 collective-permute-done.51
  421.6 8.2 %collective-permute-done.54 = f32[1,48,768]{2,1,0:T(8,128)S(1)} collective-permute-done((f32[1,48,768]{2,1,0:T(8,128)S(1)}, f32[1,48,768]{2,1,0:T(8,128)S(1)}, u32[]{:S(2)}, u32[]{:S(2)}) %collective-permute-start.54) | collective-permute-done | bytes 147488 | tf_op jit(solution)/shard_map/ppermute | solution.py:64
  434.9 4.5 all-to-all-start.6
  441.3 25.2 %newton.2.map_ref = bf16[1,4,192,192]{3,2,1,0:T(8,128)(2,1)S(1)} custom-call(s32[3]{0:T(128)S(1)} %pad_add_fusion.where_ref, f32[4,1,24,768]{3,2,1,0:T(8,128)S(1)} %constant_dynamic-slice_fusion.1.refs_0_, f32[4,1,24,768]{3,2,1,0:T(8,128)S(1)} %collective-permute-done.42.refs_1_, f32[4,1,24,768]{3,2,1,0:T(8,128)S(1)} %copy-done.48, ...), custom_call_target="tpu_custom_call" | custom-call | flops 22649241600 | tf_op jit(solution)/shard_map/newton/pallas_call | solution.py:967
  468.6 25.3 %newton.3 = bf16[1,4,192,192]{3,2,1,0:T(8,128)(2,1)S(1)} custom-call(s32[3]{0:T(128)S(1)} %pad_add_fusion.where_ref, f32[4,1,48,768]{3,2,1,0:T(8,128)S(1)} %constant_dynamic-slice_fusion.refs_0_, f32[4,1,48,768]{3,2,1,0:T(8,128)} %collective-permute-done.56.refs_1_, f32[4,1,48,768]{3,2,1,0:T(8,128)} %collective-permute-done.57.refs_2_, ...), custom_call_target="tpu_custom_call" | custom-call | flops 22649241600 | tf_op jit(solution)/shard_map/newton/pallas_call | solution.py:967
  503.6 3.2 multiply_subtract_fusion
  (504 shorter events, 159.7 us)
Async XLA Ops:
  9.6 29.9 %collective-permute-start.3 = (bf16[192,1728]{1,0:T(8,128)(2,1)}, bf16[192,1728]{1,0:T(8,128)(2,1)}, u32[]{:S(2)}, u32[]{:S(2)}) collective-permute-start(bf16[192,1728]{1,0:T(8,128)(2,1)} %bitcast_convert_fusion.2), channel_id=1, source_target_pairs={{0,4},{4,8},{8,12},{1,5},{5,9},{9,13},{2,6},{6,10},{10,14},{3,7},{... | collective-permute-start | bytes 1990664 | tf_op jit(solution)/shard_map/ppermute | solution.py:121
  15.6 25.5 %collective-permute-start.6 = (bf16[192,1728]{1,0:T(8,128)(2,1)}, bf16[192,1728]{1,0:T(8,128)(2,1)}, u32[]{:S(2)}, u32[]{:S(2)}) collective-permute-start(bf16[192,1728]{1,0:T(8,128)(2,1)} %bitcast_convert_fusion.2), channel_id=1, source_target_pairs={{4,0},{8,4},{12,8},{5,1},{9,5},{13,9},{6,2},{10,6},{14,10},{7,3},{... | collective-permute-start | bytes 1990664 | tf_op jit(solution)/shard_map/ppermute | solution.py:126
  19.6 17.6 %all-to-all-start = ((f32[8,5,384]{2,1,0:T(8,128)}), f32[8,5,384]{2,1,0:T(8,128)S(1)}, u32[]{:S(2)}, u32[]{:S(2)}) async-start(f32[8,5,384]{2,1,0:T(8,128)} %broadcast_in_dim.37), calls=%async_computation | async-start | bytes 196608 | tf_op jit(solution)/shard_map/all_to_all | solution.py:104
  25.5 102.8 %all-gather.5.cloned.1.call-start = ((), (), s32[]{:S(2)}) async-start(), calls=%async_computation.7 | async-start | bytes 3981312 | tf_op jit(solution)/shard_map/all_gather | solution.py:1374
  38.0 11.2 %collective-permute-start = (bf16[2,256,384]{1,2,0:T(8,128)(2,1)S(1)}, bf16[2,256,384]{1,2,0:T(8,128)(2,1)S(1)}, u32[]{:S(2)}, u32[]{:S(2)}) collective-permute-start(bf16[2,256,384]{1,2,0:T(8,128)(2,1)S(1)} %pad_maximum_fusion.5), channel_id=1, source_target_pairs={{0,1},{1,0},{2,3},{3,2},{4,5},{5,4},{6,7},{7,6},{8,9},{9,8},{10,11... | collective-permute-start | bytes 1179656 | tf_op jit(solution)/shard_map/ppermute | solution.py:59
  39.6 25.9 %collective-permute-start.4 = (bf16[192,1728]{1,0:T(8,128)(2,1)}, bf16[192,1728]{1,0:T(8,128)(2,1)}, u32[]{:S(2)}, u32[]{:S(2)}) collective-permute-start(bf16[192,1728]{1,0:T(8,128)(2,1)} %collective-permute-done.3), channel_id=1, source_target_pairs={{4,8},{8,12},{5,9},{9,13},{6,10},{10,14},{7,11},{11,15},{20,24},{2... | collective-permute-start | bytes 1990664 | tf_op jit(solution)/shard_map/ppermute | solution.py:121
  41.1 25.9 %collective-permute-start.7 = (bf16[192,1728]{1,0:T(8,128)(2,1)}, bf16[192,1728]{1,0:T(8,128)(2,1)}, u32[]{:S(2)}, u32[]{:S(2)}) collective-permute-start(bf16[192,1728]{1,0:T(8,128)(2,1)} %collective-permute-done.6), channel_id=1, source_target_pairs={{4,0},{8,4},{5,1},{9,5},{6,2},{10,6},{7,3},{11,7},{20,16},{24,20},... | collective-permute-start | bytes 1990664 | tf_op jit(solution)/shard_map/ppermute | solution.py:126
  45.5 25.2 %collective-permute-start.9 = (bf16[3,192,1728]{2,1,0:T(8,128)(2,1)}, bf16[3,192,1728]{2,1,0:T(8,128)(2,1)}, u32[]{:S(2)}, u32[]{:S(2)}) collective-permute-start(bf16[3,192,1728]{2,1,0:T(8,128)(2,1)} %pad_maximum_fusion.mine_ref), channel_id=1, source_target_pairs={{0,16},{16,0},{1,17},{17,1},{2,18},{18,2},{3,19},{19,3},{4,20},{20... | collective-permute-start | bytes 5971976 | tf_op jit(solution)/shard_map/ppermute | solution.py:59
  45.5 20.0 %collective-permute-start.1 = (bf16[2,256,384]{1,2,0:T(8,128)(2,1)S(1)}, bf16[2,256,384]{1,2,0:T(8,128)(2,1)S(1)}, u32[]{:S(2)}, u32[]{:S(2)}) collective-permute-start(bf16[2,256,384]{1,2,0:T(8,128)(2,1)S(1)} %pad_maximum_fusion.5), channel_id=1, source_target_pairs={{0,2},{1,3},{2,0},{3,1},{4,6},{5,7},{6,4},{7,5},{8,10},{9,11},{10,... | collective-permute-start | bytes 1179656 | tf_op jit(solution)/shard_map/ppermute | solution.py:59
  49.2 16.3 %collective-permute-start.2 = (bf16[2,256,384]{1,2,0:T(8,128)(2,1)S(1)}, bf16[2,256,384]{1,2,0:T(8,128)(2,1)}, u32[]{:S(2)}, u32[]{:S(2)}) collective-permute-start(bf16[2,256,384]{1,2,0:T(8,128)(2,1)S(1)} %pad_maximum_fusion.5), channel_id=1, source_target_pairs={{0,3},{1,2},{2,1},{3,0},{4,7},{5,6},{6,5},{7,4},{8,11},{9,10},{10,... | collective-permute-start | bytes 1179656 | tf_op jit(solution)/shard_map/ppermute | solution.py:59
  65.5 16.1 %collective-permute-start.5 = (bf16[192,1728]{1,0:T(8,128)(2,1)}, bf16[192,1728]{1,0:T(8,128)(2,1)}, u32[]{:S(2)}, u32[]{:S(2)}) collective-permute-start(bf16[192,1728]{1,0:T(8,128)(2,1)} %collective-permute-done.4), channel_id=1, source_target_pairs={{8,12},{9,13},{10,14},{11,15},{24,28},{25,29},{26,30},{27,31}} | collective-permute-start | bytes 1990664 | tf_op jit(solution)/shard_map/ppermute | solution.py:121
  68.2 8.1 %collective-permute-start.8 = (bf16[1,192,1728]{2,1,0:T(8,128)(2,1)S(1)}, bf16[1,192,1728]{2,1,0:T(8,128)(2,1)}, u32[]{:S(2)}, u32[]{:S(2)}) collective-permute-start(bf16[1,192,1728]{2,1,0:T(8,128)(2,1)S(1)} %select_bitcast_fusion.1.mine_ref), channel_id=1, source_target_pairs={{0,16},{16,0},{1,17},{17,1},{2,18},{18,2},{3,19},{19,3},{4,20},{20... | collective-permute-start | bytes 1990664 | tf_op jit(solution)/shard_map/ppermute | solution.py:59
  68.3 20.3 %collective-permute-start.10 = (bf16[192,1728]{1,0:T(8,128)(2,1)}, bf16[192,1728]{1,0:T(8,128)(2,1)}, u32[]{:S(2)}, u32[]{:S(2)}) collective-permute-start(bf16[192,1728]{1,0:T(8,128)(2,1)} %collective-permute-done.7), channel_id=1, source_target_pairs={{4,0},{5,1},{6,2},{7,3},{20,16},{21,17},{22,18},{23,19}} | collective-permute-start | bytes 1990664 | tf_op jit(solution)/shard_map/ppermute | solution.py:126
  104.5 9.5 %all-to-all-start.1 = ((f32[8,4,192]{2,1,0:T(4,128)}), f32[8,4,192]{2,1,0:T(4,128)S(1)}, u32[]{:S(2)}, u32[]{:S(2)}) async-start(f32[8,4,192]{2,1,0:T(4,128)} %broadcast_in_dim.42), calls=%async_computation.1 | async-start | bytes 65536 | tf_op jit(solution)/shard_map/all_to_all | solution.py:104
  107.8 154.3 %all-gather.7.cloned.1.call-start = ((), (), s32[]{:S(2)}) async-start(), calls=%async_computation.8 | async-start | bytes 7077888 | tf_op jit(solution)/shard_map/all_gather | solution.py:1395
  115.2 18.2 %collective-permute-start.12 = (bf16[8,8,16,192]{3,2,1,0:T(8,128)(2,1)S(1)}, bf16[8,8,16,192]{3,2,1,0:T(8,128)(2,1)}, u32[]{:S(2)}, u32[]{:S(2)}) collective-permute-start(bf16[8,8,16,192]{3,2,1,0:T(8,128)(2,1)S(1)} %multiply_convert_fusion.1.refs_0_), channel_id=1, source_target_pairs={{0,1},{1,0},{2,3},{3,2},{4,5},{5,4},{6,7},{7,6},{8,9},{9,8},{10,11... | collective-permute-start | bytes 1179656 | tf_op jit(solution)/shard_map/ppermute | solution.py:59
  115.9 17.5 %collective-permute-start.13 = (bf16[8,8,16,192]{3,2,1,0:T(8,128)(2,1)S(1)}, bf16[8,8,16,192]{3,2,1,0:T(8,128)(2,1)}, u32[]{:S(2)}, u32[]{:S(2)}) collective-permute-start(bf16[8,8,16,192]{3,2,1,0:T(8,128)(2,1)S(1)} %multiply_convert_fusion.1.refs_0_), channel_id=1, source_target_pairs={{0,2},{1,3},{2,0},{3,1},{4,6},{5,7},{6,4},{7,5},{8,10},{9,11},{10,... | collective-permute-start | bytes 1179656 | tf_op jit(solution)/shard_map/ppermute | solution.py:59
  117.4 24.5 %collective-permute-start.14 = (bf16[8,8,16,192]{3,2,1,0:T(8,128)(2,1)S(1)}, bf16[8,8,16,192]{3,2,1,0:T(8,128)(2,1)}, u32[]{:S(2)}, u32[]{:S(2)}) collective-permute-start(bf16[8,8,16,192]{3,2,1,0:T(8,128)(2,1)S(1)} %multiply_convert_fusion.1.refs_0_), channel_id=1, source_target_pairs={{0,3},{1,2},{2,1},{3,0},{4,7},{5,6},{6,5},{7,4},{8,11},{9,10},{10,... | collective-permute-start | bytes 1179656 | tf_op jit(solution)/shard_map/ppermute | solution.py:59
  183.1 21.8 %collective-permute-start.20 = (bf16[1024,192]{1,0:T(8,128)(2,1)}, bf16[1024,192]{1,0:T(8,128)(2,1)}, u32[]{:S(2)}, u32[]{:S(2)}) collective-permute-start(bf16[1024,192]{1,0:T(8,128)(2,1)} %get-tuple-element.115), channel_id=1, source_target_pairs={{0,3},{1,2},{2,1},{3,0},{4,7},{5,6},{6,5},{7,4},{8,11},{9,10},{10,... | collective-permute-start | bytes 1179656 | tf_op jit(solution)/shard_map/ppermute | solution.py:59
  188.5 18.5 %collective-permute-start.19 = (bf16[1024,192]{1,0:T(8,128)(2,1)}, bf16[1024,192]{1,0:T(8,128)(2,1)S(1)}, u32[]{:S(2)}, u32[]{:S(2)}) collective-permute-start(bf16[1024,192]{1,0:T(8,128)(2,1)} %copy-done.46), channel_id=1, source_target_pairs={{0,2},{1,3},{2,0},{3,1},{4,6},{5,7},{6,4},{7,5},{8,10},{9,11},{10,... | collective-permute-start | bytes 1179656 | tf_op jit(solution)/shard_map/ppermute | solution.py:59
  189.8 17.7 %collective-permute-start.18 = (bf16[1024,192]{1,0:T(8,128)(2,1)}, bf16[1024,192]{1,0:T(8,128)(2,1)S(1)}, u32[]{:S(2)}, u32[]{:S(2)}) collective-permute-start(bf16[1024,192]{1,0:T(8,128)(2,1)} %copy-done.45), channel_id=1, source_target_pairs={{0,1},{1,0},{2,3},{3,2},{4,5},{5,4},{6,7},{7,6},{8,9},{9,8},{10,11... | collective-permute-start | bytes 1179656 | tf_op jit(solution)/shard_map/ppermute | solution.py:59
  204.9 18.3 %collective-permute-start.24 = (bf16[4,528,384]{2,1,0:T(8,128)(2,1)}, bf16[4,528,384]{2,1,0:T(8,128)(2,1)}, u32[]{:S(2)}, u32[]{:S(2)}) collective-permute-start(bf16[4,528,384]{2,1,0:T(8,128)(2,1)} %dynamic-slice_bitcast_fusion), channel_id=1, source_target_pairs={{0,16},{16,0},{1,17},{17,1},{2,18},{18,2},{3,19},{19,3},{4,20},{20... | collective-permute-start | bytes 4866056 | tf_op jit(solution)/shard_map/ppermute | solution.py:59
  218.9 17.0 %collective-permute-start.21 = (bf16[8,8,16,192]{3,2,1,0:T(8,128)(2,1)}, bf16[8,8,16,192]{3,2,1,0:T(8,128)(2,1)}, u32[]{:S(2)}, u32[]{:S(2)}) collective-permute-start(bf16[8,8,16,192]{3,2,1,0:T(8,128)(2,1)} %multiply_convert_fusion.refs_0_.g_ref), channel_id=1, source_target_pairs={{0,4},{4,8},{8,12},{12,0},{1,5},{5,9},{9,13},{13,1},{2,6},{6,10},{... | collective-permute-start | bytes 1179656 | tf_op jit(solution)/shard_map/ppermute | solution.py:64
  219.4 38.2 %collective-permute-start.22 = (bf16[8,8,16,192]{3,2,1,0:T(8,128)(2,1)}, bf16[8,8,16,192]{3,2,1,0:T(8,128)(2,1)}, u32[]{:S(2)}, u32[]{:S(2)}) collective-permute-start(bf16[8,8,16,192]{3,2,1,0:T(8,128)(2,1)} %multiply_convert_fusion.refs_0_.g_ref), channel_id=1, source_target_pairs={{0,8},{4,12},{8,0},{12,4},{1,9},{5,13},{9,1},{13,5},{2,10},{6,14},... | collective-permute-start | bytes 1179656 | tf_op jit(solution)/shard_map/ppermute | solution.py:64
  220.0 37.6 %collective-permute-start.23 = (bf16[8,8,16,192]{3,2,1,0:T(8,128)(2,1)}, bf16[8,8,16,192]{3,2,1,0:T(8,128)(2,1)}, u32[]{:S(2)}, u32[]{:S(2)}) collective-permute-start(bf16[8,8,16,192]{3,2,1,0:T(8,128)(2,1)} %multiply_convert_fusion.refs_0_.g_ref), channel_id=1, source_target_pairs={{0,12},{4,0},{8,4},{12,8},{1,13},{5,1},{9,5},{13,9},{2,14},{6,2},{... | collective-permute-start | bytes 1179656 | tf_op jit(solution)/shard_map/ppermute | solution.py:64
  273.8 20.9 %collective-permute-start.32 = (bf16[528,384]{1,0:T(8,128)(2,1)S(1)}, bf16[528,384]{1,0:T(8,128)(2,1)S(1)}, u32[]{:S(2)}, u32[]{:S(2)}) collective-permute-start(bf16[528,384]{1,0:T(8,128)(2,1)S(1)} %get-tuple-element.313), channel_id=1, source_target_pairs={{0,4},{4,8},{8,12},{12,0},{1,5},{5,9},{9,13},{13,1},{2,6},{6,10},{... | collective-permute-start | bytes 1216520 | tf_op jit(solution)/shard_map/ppermute | solution.py:64
  284.8 28.9 %collective-permute-start.29 = (bf16[192,1728]{1,0:T(8,128)(2,1)S(1)}, bf16[192,1728]{1,0:T(8,128)(2,1)S(1)}, u32[]{:S(2)}, u32[]{:S(2)}) collective-permute-start(bf16[192,1728]{1,0:T(8,128)(2,1)S(1)} %get-tuple-element.145.refs_0_), channel_id=1, source_target_pairs={{0,1},{1,0},{2,3},{3,2},{4,5},{5,4},{6,7},{7,6},{8,9},{9,8},{10,11... | collective-permute-start | bytes 1990664 | tf_op jit(solution)/shard_map/ppermute | solution.py:59
  286.4 31.7 %collective-permute-start.30 = (bf16[192,1728]{1,0:T(8,128)(2,1)S(1)}, bf16[192,1728]{1,0:T(8,128)(2,1)S(1)}, u32[]{:S(2)}, u32[]{:S(2)}) collective-permute-start(bf16[192,1728]{1,0:T(8,128)(2,1)S(1)} %get-tuple-element.145.refs_0_), channel_id=1, source_target_pairs={{0,2},{1,3},{2,0},{3,1},{4,6},{5,7},{6,4},{7,5},{8,10},{9,11},{10,... | collective-permute-start | bytes 1990664 | tf_op jit(solution)/shard_map/ppermute | solution.py:59
  287.2 30.9 %collective-permute-start.31 = (bf16[192,1728]{1,0:T(8,128)(2,1)S(1)}, bf16[192,1728]{1,0:T(8,128)(2,1)S(1)}, u32[]{:S(2)}, u32[]{:S(2)}) collective-permute-start(bf16[192,1728]{1,0:T(8,128)(2,1)S(1)} %get-tuple-element.145.refs_0_), channel_id=1, source_target_pairs={{0,3},{1,2},{2,1},{3,0},{4,7},{5,6},{6,5},{7,4},{8,11},{9,10},{10,... | collective-permute-start | bytes 1990664 | tf_op jit(solution)/shard_map/ppermute | solution.py:59
  288.3 23.3 %collective-permute-start.33 = (bf16[528,384]{1,0:T(8,128)(2,1)S(1)}, bf16[528,384]{1,0:T(8,128)(2,1)S(1)}, u32[]{:S(2)}, u32[]{:S(2)}) collective-permute-start(bf16[528,384]{1,0:T(8,128)(2,1)S(1)} %get-tuple-element.312), channel_id=1, source_target_pairs={{0,8},{4,12},{8,0},{12,4},{1,9},{5,13},{9,1},{13,5},{2,10},{6,14},... | collective-permute-start | bytes 1216520 | tf_op jit(solution)/shard_map/ppermute | solution.py:64
  294.7 19.0 %collective-permute-start.34 = (bf16[528,384]{1,0:T(8,128)(2,1)S(1)}, bf16[528,384]{1,0:T(8,128)(2,1)S(1)}, u32[]{:S(2)}, u32[]{:S(2)}) collective-permute-start(bf16[528,384]{1,0:T(8,128)(2,1)S(1)} %get-tuple-element.311), channel_id=1, source_target_pairs={{0,12},{4,0},{8,4},{12,8},{1,13},{5,1},{9,5},{13,9},{2,14},{6,2},{... | collective-permute-start | bytes 1216520 | tf_op jit(solution)/shard_map/ppermute | solution.py:64
  324.6 8.0 %collective-permute-start.38 = (f32[1,24,768]{2,1,0:T(8,128)S(1)}, f32[1,24,768]{2,1,0:T(8,128)S(1)}, u32[]{:S(2)}, u32[]{:S(2)}) collective-permute-start(f32[1,24,768]{2,1,0:T(8,128)S(1)} %get-tuple-element.329), channel_id=1, source_target_pairs={{0,12},{4,0},{8,4},{12,8},{1,13},{5,1},{9,5},{13,9},{2,14},{6,2},{... | collective-permute-start | bytes 221192 | tf_op jit(solution)/shard_map/ppermute | solution.py:64
  337.7 9.9 %collective-permute-start.39 = (f32[1,24,768]{2,1,0:T(8,128)S(1)}, f32[1,24,768]{2,1,0:T(8,128)S(1)}, u32[]{:S(2)}, u32[]{:S(2)}) collective-permute-start(f32[1,24,768]{2,1,0:T(8,128)S(1)} %get-tuple-element.301), channel_id=1, source_target_pairs={{0,12},{4,0},{8,4},{12,8},{1,13},{5,1},{9,5},{13,9},{2,14},{6,2},{... | collective-permute-start | bytes 221192 | tf_op jit(solution)/shard_map/ppermute | solution.py:64
  340.7 40.2 %all-to-all-start.5 = ((bf16[4,192,1056]{2,1,0:T(8,128)(2,1)}), bf16[4,192,1056]{2,1,0:T(8,128)(2,1)}, u32[]{:S(2)}, u32[]{:S(2)}) async-start(bf16[4,192,1056]{2,1,0:T(8,128)(2,1)} %broadcast_in_dim.99), calls=%async_computation.5 | async-start | bytes 3538944 | tf_op jit(solution)/shard_map/all_to_all | solution.py:104
  352.7 21.5 %collective-permute-start.42 = (f32[4,1,24,768]{3,2,1,0:T(8,128)S(1)}, f32[4,1,24,768]{3,2,1,0:T(8,128)S(1)}, u32[]{:S(2)}, u32[]{:S(2)}) collective-permute-start(f32[4,1,24,768]{3,2,1,0:T(8,128)S(1)} %constant_dynamic-slice_fusion.1.refs_0_), channel_id=1, source_target_pairs={{0,1},{1,0},{2,3},{3,2},{4,5},{5,4},{6,7},{7,6},{8,9},{9,8},{10,11... | collective-permute-start | bytes 884744 | tf_op jit(solution)/shard_map/ppermute | solution.py:59
  354.4 19.9 %collective-permute-start.43 = (f32[4,1,24,768]{3,2,1,0:T(8,128)S(1)}, f32[4,1,24,768]{3,2,1,0:T(8,128)S(1)}, u32[]{:S(2)}, u32[]{:S(2)}) collective-permute-start(f32[4,1,24,768]{3,2,1,0:T(8,128)S(1)} %constant_dynamic-slice_fusion.1.refs_0_), channel_id=1, source_target_pairs={{0,2},{1,3},{2,0},{3,1},{4,6},{5,7},{6,4},{7,5},{8,10},{9,11},{10,... | collective-permute-start | bytes 884744 | tf_op jit(solution)/shard_map/ppermute | solution.py:59
  355.9 23.6 %collective-permute-start.44 = (f32[4,1,24,768]{3,2,1,0:T(8,128)S(1)}, f32[4,1,24,768]{3,2,1,0:T(8,128)S(1)}, u32[]{:S(2)}, u32[]{:S(2)}) collective-permute-start(f32[4,1,24,768]{3,2,1,0:T(8,128)S(1)} %constant_dynamic-slice_fusion.1.refs_0_), channel_id=1, source_target_pairs={{0,3},{1,2},{2,1},{3,0},{4,7},{5,6},{6,5},{7,4},{8,11},{9,10},{10,... | collective-permute-start | bytes 884744 | tf_op jit(solution)/shard_map/ppermute | solution.py:59
  380.8 13.6 %all-to-all-start.3 = ((bf16[4,256,384]{2,1,0:T(8,128)(2,1)}), bf16[4,256,384]{2,1,0:T(8,128)(2,1)}, u32[]{:S(2)}, u32[]{:S(2)}) async-start(bf16[4,256,384]{2,1,0:T(8,128)(2,1)} %pad_maximum_fusion.4), calls=%async_computation.3 | async-start | bytes 1572864 | tf_op jit(solution)/shard_map/all_to_all | solution.py:1472
  398.6 12.9 %collective-permute-start.52 = (f32[1,48,768]{2,1,0:T(8,128)}, f32[1,48,768]{2,1,0:T(8,128)}, u32[]{:S(2)}, u32[]{:S(2)}) collective-permute-start(f32[1,48,768]{2,1,0:T(8,128)} %get-tuple-element.325), channel_id=1, source_target_pairs={{0,12},{4,0},{8,4},{12,8},{1,13},{5,1},{9,5},{13,9},{2,14},{6,2},{... | collective-permute-start | bytes 442376 | tf_op jit(solution)/shard_map/ppermute | solution.py:64
  401.3 13.4 %collective-permute-start.51 = (f32[1,48,768]{2,1,0:T(8,128)S(1)}, f32[1,48,768]{2,1,0:T(8,128)}, u32[]{:S(2)}, u32[]{:S(2)}) collective-permute-start(f32[1,48,768]{2,1,0:T(8,128)S(1)} %get-tuple-element.326), channel_id=1, source_target_pairs={{0,8},{4,12},{8,0},{12,4},{1,9},{5,13},{9,1},{13,5},{2,10},{6,14},... | collective-permute-start | bytes 442376 | tf_op jit(solution)/shard_map/ppermute | solution.py:64
  402.2 12.5 %collective-permute-start.50 = (f32[1,48,768]{2,1,0:T(8,128)S(1)}, f32[1,48,768]{2,1,0:T(8,128)}, u32[]{:S(2)}, u32[]{:S(2)}) collective-permute-start(f32[1,48,768]{2,1,0:T(8,128)S(1)} %get-tuple-element.324), channel_id=1, source_target_pairs={{0,4},{4,8},{8,12},{12,0},{1,5},{5,9},{9,13},{13,1},{2,6},{6,10},{... | collective-permute-start | bytes 442376 | tf_op jit(solution)/shard_map/ppermute | solution.py:64
  403.4 8.0 %all-to-all-start.4 = ((f32[4,16,128]{2,1,0:T(8,128)}), f32[4,16,128]{2,1,0:T(8,128)S(1)}, u32[]{:S(2)}, u32[]{:S(2)}) async-start(f32[4,16,128]{2,1,0:T(8,128)} %broadcast_in_dim.96), calls=%async_computation.4 | async-start | bytes 65536 | tf_op jit(solution)/shard_map/all_to_all | solution.py:104
  416.3 13.5 %collective-permute-start.54 = (f32[1,48,768]{2,1,0:T(8,128)S(1)}, f32[1,48,768]{2,1,0:T(8,128)S(1)}, u32[]{:S(2)}, u32[]{:S(2)}) collective-permute-start(f32[1,48,768]{2,1,0:T(8,128)S(1)} %get-tuple-element.299), channel_id=1, source_target_pairs={{0,8},{4,12},{8,0},{12,4},{1,9},{5,13},{9,1},{13,5},{2,10},{6,14},... | collective-permute-start | bytes 442376 | tf_op jit(solution)/shard_map/ppermute | solution.py:64
  417.2 12.6 %collective-permute-start.55 = (f32[1,48,768]{2,1,0:T(8,128)S(1)}, f32[1,48,768]{2,1,0:T(8,128)S(1)}, u32[]{:S(2)}, u32[]{:S(2)}) collective-permute-start(f32[1,48,768]{2,1,0:T(8,128)S(1)} %get-tuple-element.299), channel_id=1, source_target_pairs={{0,4},{4,8},{8,12},{12,0},{1,5},{5,9},{9,13},{13,1},{2,6},{6,10},{... | collective-permute-start | bytes 442376 | tf_op jit(solution)/shard_map/ppermute | solution.py:64
  430.0 38.7 %collective-permute-start.56 = (f32[4,1,48,768]{3,2,1,0:T(8,128)S(1)}, f32[4,1,48,768]{3,2,1,0:T(8,128)}, u32[]{:S(2)}, u32[]{:S(2)}) collective-permute-start(f32[4,1,48,768]{3,2,1,0:T(8,128)S(1)} %constant_dynamic-slice_fusion.refs_0_), channel_id=1, source_target_pairs={{0,1},{1,0},{2,3},{3,2},{4,5},{5,4},{6,7},{7,6},{8,9},{9,8},{10,11... | collective-permute-start | bytes 1769480 | tf_op jit(solution)/shard_map/ppermute | solution.py:59
  430.5 38.1 %collective-permute-start.57 = (f32[4,1,48,768]{3,2,1,0:T(8,128)S(1)}, f32[4,1,48,768]{3,2,1,0:T(8,128)}, u32[]{:S(2)}, u32[]{:S(2)}) collective-permute-start(f32[4,1,48,768]{3,2,1,0:T(8,128)S(1)} %constant_dynamic-slice_fusion.refs_0_), channel_id=1, source_target_pairs={{0,2},{1,3},{2,0},{3,1},{4,6},{5,7},{6,4},{7,5},{8,10},{9,11},{10,... | collective-permute-start | bytes 1769480 | tf_op jit(solution)/shard_map/ppermute | solution.py:59
  430.9 37.7 %collective-permute-start.58 = (f32[4,1,48,768]{3,2,1,0:T(8,128)S(1)}, f32[4,1,48,768]{3,2,1,0:T(8,128)}, u32[]{:S(2)}, u32[]{:S(2)}) collective-permute-start(f32[4,1,48,768]{3,2,1,0:T(8,128)S(1)} %constant_dynamic-slice_fusion.refs_0_), channel_id=1, source_target_pairs={{0,3},{1,2},{2,1},{3,0},{4,7},{5,6},{6,5},{7,4},{8,11},{9,10},{10,... | collective-permute-start | bytes 1769480 | tf_op jit(solution)/shard_map/ppermute | solution.py:59
  434.9 64.9 %all-to-all-start.6 = ((f32[8,32,1536]{2,1,0:T(8,128)}), f32[8,32,1536]{2,1,0:T(8,128)}, u32[]{:S(2)}, u32[]{:S(2)}) async-start(f32[8,32,1536]{2,1,0:T(8,128)} %broadcast_in_dim.100), calls=%async_computation.6 | async-start | bytes 3145728 | tf_op jit(solution)/shard_map/all_to_all | solution.py:104
  (141 other events, 1331.3 us)
Sparse Core Ops, SparseCore 0:
  88.7 39.4 all-gather.4
  155.6 62.4 all-gather.6

commit v5 on v4

--- a/solution.py
+++ b/solution.py
@@ -927,7 +927,13 @@
             if i != j:
                 top[spans[j], spans[i]] = jnp.transpose(value).astype(bf16)
 
-        symmetric(lambda a, b: three(ah[a, :], al[a, :], ah[:, b], al[:, b]), write_map)
+        def square(a, b):
+            if a == b:
+                cross = times(ah[a, :], al[:, a])
+                return times(ah[a, :], ah[:, a]) + (cross + jnp.transpose(cross))
+            return three(ah[a, :], al[a, :], ah[:, b], al[:, b])
+
+        symmetric(square, write_map)
         symmetric(
             lambda a, b: times(ah[a, :], top[:, b]) + times(al[a, :], top[:, b]),
             functools.partial(store, th, tl),
@@ -1390,7 +1396,7 @@
         jnp.transpose(colour_conv, (0, 2, 1)).astype(bf16), ((0, 0), (0, PAD - 3), (0, 0))
     )
     summed, active, picture = conv_two(row, twos, pairs, weight_two, weight_skip, colour)
-    kept_pairs = [after(pair, active) for pair in pairs]
+    kept_pairs = [after(pair, weight_two) for pair in pairs]
     turned = jnp.concatenate([jnp.transpose(pair[0]) for pair in kept_pairs], axis=0)
     ones_all = lax.all_gather(after(turned, others), GROUP, axis=0)
 
@@ -1439,7 +1445,19 @@
     hidden_all = straight(grad_hidden)
     scaled = inverse.reshape(1, 1)
     hidden_all = straight(grad_hidden)
-    *hidden_all, kept, wire = together(*hidden_all, kept, kept.astype(bf16))
+    small = jnp.concatenate(
+        [
+            grad_colour[: 9 * PAD],
+            jnp.broadcast_to(loss_part[:1, :1], (1, c_out)),
+        ],
+        axis=0,
+    )
+
+    wide = 2 * c_in + 2 * c_out + EMB + conds.shape[1] + 1
+    wide = wide + -wide % 128
+    extra = small.reshape(-1)
+    extra = jnp.pad(extra, (0, -extra.shape[0] % (8 * wide))).reshape(-1, wide)
+    *hidden_all, kept, wire, extra = together(*hidden_all, kept, kept.astype(bf16), extra)
     hidden_all = both_cores(hidden_all)
     moment_one, low_one = weight_one_moment(
         where, scaled, hidden_all, ones_all, momentum_first.T
@@ -1490,14 +1508,6 @@
         "bgc,kgc->bk", grad_mods_two, norm_second[:EMB], precision=highest
     )
 
-    small = jnp.concatenate(
-        [
-            grad_colour[: 9 * PAD],
-            jnp.broadcast_to(loss_part[:1, :1], (1, c_out)),
-        ],
-        axis=0,
-    )
-
     grad_cond = jnp.sum(spread(grad_cond, ("row",)), axis=0)
     found = jnp.concatenate(
         [
@@ -1510,9 +1520,6 @@
         axis=1,
     )
     found = jnp.pad(found, ((0, 0), (0, -found.shape[1] % 128)))
-    wide = found.shape[1]
-    extra = small.reshape(-1)
-    extra = jnp.pad(extra, (0, -extra.shape[0] % (8 * wide))).reshape(-1, wide)
     packet = jnp.concatenate([found, extra], axis=0)
     packet = spread(after(packet, total_two), GROUP)
     found = packet[:, :n].reshape(-1, wide)

time: 528 us -> 582 us (1.10)
  waiting for transfers between devices: 166 us -> 218 us
  local copies, waits for them, and re-layouts: 58.5 us -> 66.7 us
  blocking collectives: 8.15 us -> 0 us
    all_gather x1, waiting for transfers between devices: 9.56 us -> 38.9 us  [near_device(): others = lax.all_gather(after(other, below[3], above[3]), GROUP, axis=0)]
    ppermute x36, waiting for transfers between devices: 54.4 us -> 71.6 us  [axis_swap(): return lax.ppermute(value, axis, [(i, i ^ k) for i in range(n)])]
    all_to_all x1 -> x0, blocking collectives: 8.15 us -> none  [spread(): lax.all_to_all(jnp.broadcast_to(value[None], (n,) + value.shape), axis, 0...]
    all_to_all x5 -> x6, waiting for transfers between devices: 19.2 us -> 25.9 us  [spread(): lax.all_to_all(jnp.broadcast_to(value[None], (n,) + value.shape), axis, 0...]
    unnamed x257 -> x255, local copies, waits for them, and re-layouts: 27.3 us -> 33.7 us
    all_to_all x5 -> x6, starting transfers between devices: 21.5 us -> 25 us  [spread(): lax.all_to_all(jnp.broadcast_to(value[None], (n,) + value.shape), axis, 0...]
  transfers between devices with their start and end apart: 68 -> 69, of which waited for: 31 -> 30; matrix products, arithmetic and copies ran while one was open for 12% -> 11% of each run, Pallas kernels for 20% -> 19%
where the time goes in v5:
time: 582 us; the launch traced here: 573 us
  waiting for transfers between devices  218 us (37%)
  Pallas kernels  117 us (20%)
  starting transfers between devices  106 us (18%)
  local copies, waits for them, and re-layouts  66.7 us (11%)
  other arithmetic  40.3 us (7%)
  between operations  17.6 us (3%)
  matrix products  6.94 us (1%)
    ppermute x36, waiting for transfers between devices, axis_swap(): return lax.ppermute(value, axis, [(i, i ^ k) for i in range(n)])  71.6 us
    ppermute x18, waiting for transfers between devices, axis_shift(): return lax.ppermute(value, axis, [(i, (i + k) % n) for i in range(n)])  70.8 us
    pallas_call x2, Pallas kernels, newton(): pl.pallas_call(functools.partial(newton_kernel, count, sides), out_shape=...  47.9 us
    all_gather x1, waiting for transfers between devices, near_device(): others = lax.all_gather(after(other, below[3], above[3]), GROUP, axis=0)  38.9 us
    ppermute x18, starting transfers between devices, axis_shift(): return lax.ppermute(value, axis, [(i, (i + k) % n) for i in range(n)])  34.4 us
    unnamed x255, local copies, waits for them, and re-layouts  33.7 us
    ppermute x36, starting transfers between devices, axis_swap(): return lax.ppermute(value, axis, [(i, i ^ k) for i in range(n)])  29.9 us
    all_to_all x6, waiting for transfers between devices, spread(): lax.all_to_all(jnp.broadcast_to(value[None], (n,) + value.shape), axis, 0...  25.9 us
  transfers between devices with their start and end apart: 69, of which 30 were waited for; matrix products, arithmetic and copies ran while one was open for 11% of the time, Pallas kernels for 19%

profile of v5, /device:TPU:0, one launch (start us, length us, event | category | flops | bytes accessed | tf_op | source)
XLA Modules:
  0.0 573.1 jit_solution(1096634156540641333)
XLA Ops:
  9.6 6.0 %collective-permute-start.3 = (bf16[192,1728]{1,0:T(8,128)(2,1)}, bf16[192,1728]{1,0:T(8,128)(2,1)}, u32[]{:S(2)}, u32[]{:S(2)}) collective-permute-start(bf16[192,1728]{1,0:T(8,128)(2,1)} %bitcast_convert_fusion.2), channel_id=1, source_target_pairs={{0,4},{4,8},{8,12},{1,5},{5,9},{9,13},{2,6},{6,10},{10,14},{3,7},{... | collective-permute-start | bytes 1990664 | tf_op jit(solution)/shard_map/ppermute | solution.py:121
  19.6 5.9 %all-to-all-start = ((f32[8,5,384]{2,1,0:T(8,128)}), f32[8,5,384]{2,1,0:T(8,128)S(1)}, u32[]{:S(2)}, u32[]{:S(2)}) async-start(f32[8,5,384]{2,1,0:T(8,128)} %broadcast_in_dim.37), calls=%async_computation | async-start | bytes 196608 | tf_op jit(solution)/shard_map/all_to_all | solution.py:104
  27.6 9.6 %all-to-all-done = f32[8,5,384]{2,1,0:T(8,128)S(1)} async-done(((f32[8,5,384]{2,1,0:T(8,128)}), f32[8,5,384]{2,1,0:T(8,128)S(1)}, u32[]{:S(2)}, u32[]{:S(2)}) %all-to-all-start) | async-done | bytes 61472 | tf_op jit(solution)/shard_map/all_to_all | solution.py:104
  42.5 2.9 pad_maximum_fusion.mine_ref
  51.9 13.6 %collective-permute-done.1 = bf16[2,256,384]{1,2,0:T(8,128)(2,1)} collective-permute-done((bf16[2,256,384]{1,2,0:T(8,128)(2,1)S(1)}, bf16[2,256,384]{1,2,0:T(8,128)(2,1)}, u32[]{:S(2)}, u32[]{:S(2)}) %collective-permute-start.1) | collective-permute-done | bytes 393248 | tf_op jit(solution)/shard_map/ppermute | solution.py:59
  70.7 5.6 place.4.refs_0_
  78.7 2.9 copy-done.2
  81.6 7.0 %collective-permute-done.10 = bf16[192,1728]{1,0:T(8,128)(2,1)} collective-permute-done((bf16[192,1728]{1,0:T(8,128)(2,1)}, bf16[192,1728]{1,0:T(8,128)(2,1)}, u32[]{:S(2)}, u32[]{:S(2)}) %collective-permute-start.10) | collective-permute-done | bytes 663584 | tf_op jit(solution)/shard_map/ppermute | solution.py:126
  88.6 38.9 %all-gather.5.cloned.1.call-done = bf16[1536,1152]{1,0:T(8,128)(2,1)} async-done(((bf16[192,1152]{1,0:T(8,128)(2,1)}), bf16[1536,1152]{1,0:T(8,128)(2,1)}) %all-gather.5.cloned.1.call-update) | async-done | bytes 3538960 | tf_op jit(solution)/shard_map/all_gather | solution.py:1380
  143.7 3.8 copy-done.3
  149.9 4.4 conv_one.1
  155.0 3.5 all-to-all-start.1
  159.1 6.4 %all-to-all-done.1 = f32[8,4,192]{2,1,0:T(4,128)S(1)} async-done(((f32[8,4,192]{2,1,0:T(4,128)}), f32[8,4,192]{2,1,0:T(4,128)S(1)}, u32[]{:S(2)}, u32[]{:S(2)}) %all-to-all-start.1) | async-done | bytes 24608 | tf_op jit(solution)/shard_map/all_to_all | solution.py:104
  171.7 9.9 %collective-permute-done.12.refs_1_ = bf16[8,8,16,192]{3,2,1,0:T(8,128)(2,1)S(1)} collective-permute-done((bf16[8,8,16,192]{3,2,1,0:T(8,128)(2,1)S(1)}, bf16[8,8,16,192]{3,2,1,0:T(8,128)(2,1)S(1)}, u32[]{:S(2)}, u32[]{:S(2)}) %collective-permute-start.12) | collective-permute-done | bytes 393248 | tf_op jit(solution)/shard_map/ppermute | solution.py:59
  181.6 11.7 %collective-permute-done.13.refs_2_ = bf16[8,8,16,192]{3,2,1,0:T(8,128)(2,1)S(1)} collective-permute-done((bf16[8,8,16,192]{3,2,1,0:T(8,128)(2,1)S(1)}, bf16[8,8,16,192]{3,2,1,0:T(8,128)(2,1)S(1)}, u32[]{:S(2)}, u32[]{:S(2)}) %collective-permute-start.13) | collective-permute-done | bytes 393248 | tf_op jit(solution)/shard_map/ppermute | solution.py:59
  195.7 9.3 %conv_two.1 = (f32[8,8,16,192]{3,2,1,0:T(8,128)S(1)}, bf16[8,8,16,192]{3,2,1,0:T(8,128)(2,1)S(1)}, f32[8,1024]{1,0:T(8,128)}) custom-call(s32[1]{0:T(128)} %bitcast.row_ref, bf16[8,8,16,192]{3,2,1,0:T(8,128)(2,1)S(1)} %multiply_convert_fusion.1.refs_0_, bf16[8,8,16,192]{3,2,1,0:T(8,128)(2,1)S(1)} %collective-permute-done.12.refs_1_, ...), custom_call_target="tpu_custom_call" | custom-call | tf_op jit(solution)/shard_map/conv_two/pallas_call | solution.py:278
  216.1 5.7 critic.1
  225.7 8.5 %back_two.1 = (bf16[10,10,16,192]{3,2,1,0:T(8,128)(2,1)S(1)}, f32[128,192]{1,0:T(8,128)S(1)}, bf16[1024,192]{1,0:T(8,128)(2,1)S(1)}, bf16[1024,192]{1,0:T(8,128)...) custom-call(s32[1]{0:T(128)} %bitcast.row_ref, bf16[1024,128]{1,0:T(8,128)(2,1)S(1)} %get-tuple-element.110.g_ref, ...), custom_call_target="tpu_custom_call" | custom-call | tf_op jit(solution)/shard_map/back_two/pallas_call | solution.py:403
  245.9 7.7 %weight_two.1 = bf16[8,528,384]{2,1,0:T(8,128)(2,1)S(1)} custom-call(s32[1]{0:T(128)} %bitcast.row_ref, bf16[10,10,16,192]{3,2,1,0:T(8,128)(2,1)S(1)} %copy-done.52, bf16[192,1024]{1,0:T(8,128)(2,1)S(1)} %bitcast.294, bf16[192,1024]{1,0:T(8,128)(2,1)S(1)} %bitcast.295, bf16[192,1024]{1,0:T(8,128)(2,1)S(1)} %bitcast.296, bf16[192,1024]{1,0:T(8,128)(2,1)S(1)} %bitcast.297, ...), custom_call_target="tpu_custom_call" | custom-call | flops 8153726976 | tf_op jit(solution)/shard_map/weight_two/pallas_call | solution.py:772
  255.1 5.9 %collective-permute-done.19 = bf16[1024,192]{1,0:T(8,128)(2,1)S(1)} collective-permute-done((bf16[1024,192]{1,0:T(8,128)(2,1)}, bf16[1024,192]{1,0:T(8,128)(2,1)S(1)}, u32[]{:S(2)}, u32[]{:S(2)}) %collective-permute-start.19) | collective-permute-done | bytes 393248 | tf_op jit(solution)/shard_map/ppermute | solution.py:59
  264.0 3.3 all-to-all-start.2
  267.8 5.2 all-to-all-done.2
  275.2 3.2 collective-permute-start.23
  279.9 4.7 fusion.62
  284.6 6.6 %collective-permute-done.21.refs_1_ = bf16[8,8,16,192]{3,2,1,0:T(8,128)(2,1)} collective-permute-done((bf16[8,8,16,192]{3,2,1,0:T(8,128)(2,1)}, bf16[8,8,16,192]{3,2,1,0:T(8,128)(2,1)}, u32[]{:S(2)}, u32[]{:S(2)}) %collective-permute-start.21) | collective-permute-done | bytes 393248 | tf_op jit(solution)/shard_map/ppermute | solution.py:64
  291.2 21.7 %collective-permute-done.22.refs_2_ = bf16[8,8,16,192]{3,2,1,0:T(8,128)(2,1)} collective-permute-done((bf16[8,8,16,192]{3,2,1,0:T(8,128)(2,1)}, bf16[8,8,16,192]{3,2,1,0:T(8,128)(2,1)}, u32[]{:S(2)}, u32[]{:S(2)}) %collective-permute-start.22) | collective-permute-done | bytes 393248 | tf_op jit(solution)/shard_map/ppermute | solution.py:64
  317.3 2.8 copy-done.49
  321.5 7.4 %weight_one.1 = (f32[192,1728]{1,0:T(8,128)}, bf16[192,1728]{1,0:T(8,128)(2,1)S(1)}) custom-call(s32[3]{0:T(128)S(1)} %pad_add_fusion.where_ref, f32[1,1]{1,0:T(1,128)} %bitcast.7.inverse_ref, bf16[8,8,16,192]{3,2,1,0:T(8,128)(2,1)} %multiply_convert_fusion.refs_0_.g_ref, bf16[8,8,16,192]{3,2,1,0:T(8,128)(2,1)} %collective-permute-done.21.refs_1_, ...), custom_call_target="tpu_custom_call" | custom-call | flops 5435817984 | tf_op jit(solution)/shard_map/weight_one/pallas_call | solution.py:710
  329.0 11.0 %collective-permute-start.32 = (bf16[528,384]{1,0:T(8,128)(2,1)S(1)}, bf16[528,384]{1,0:T(8,128)(2,1)S(1)}, u32[]{:S(2)}, u32[]{:S(2)}) collective-permute-start(bf16[528,384]{1,0:T(8,128)(2,1)S(1)} %get-tuple-element.315), channel_id=1, source_target_pairs={{0,4},{4,8},{8,12},{12,0},{1,5},{5,9},{9,13},{13,1},{2,6},{6,10},{... | collective-permute-start | bytes 1216520 | tf_op jit(solution)/shard_map/ppermute | solution.py:64
  343.7 6.2 %collective-permute-done.32.refs_1_ = bf16[528,384]{1,0:T(8,128)(2,1)S(1)} collective-permute-done((bf16[528,384]{1,0:T(8,128)(2,1)S(1)}, bf16[528,384]{1,0:T(8,128)(2,1)S(1)}, u32[]{:S(2)}, u32[]{:S(2)}) %collective-permute-start.32) | collective-permute-done | bytes 405536 | tf_op jit(solution)/shard_map/ppermute | solution.py:64
  351.1 5.5 back_one.1
  357.6 9.2 %collective-permute-done.33.refs_2_ = bf16[528,384]{1,0:T(8,128)(2,1)S(1)} collective-permute-done((bf16[528,384]{1,0:T(8,128)(2,1)S(1)}, bf16[528,384]{1,0:T(8,128)(2,1)S(1)}, u32[]{:S(2)}, u32[]{:S(2)}) %collective-permute-start.33) | collective-permute-done | bytes 405536 | tf_op jit(solution)/shard_map/ppermute | solution.py:64
  368.9 4.1 collective-permute-done.30.refs_2_
  379.5 5.7 collective-permute-start.38
  387.8 5.0 collective-permute-done.37
  395.9 4.5 all-to-all-start.5
  402.8 5.0 collective-permute-done.40
  413.0 16.5 %collective-permute-done.42.refs_1_ = f32[4,1,24,768]{3,2,1,0:T(8,128)S(1)} collective-permute-done((f32[4,1,24,768]{3,2,1,0:T(8,128)S(1)}, f32[4,1,24,768]{3,2,1,0:T(8,128)S(1)}, u32[]{:S(2)}, u32[]{:S(2)}) %collective-permute-start.42) | collective-permute-done | bytes 294944 | tf_op jit(solution)/shard_map/ppermute | solution.py:59
  429.5 5.2 collective-permute-done.44.refs_3_
  436.1 4.2 all-to-all-start.3
  445.9 3.8 all-to-all-done.3
  458.9 3.3 all-to-all-start.4
  462.2 4.7 all-to-all-done.4
  477.0 8.4 %collective-permute-done.54 = f32[1,48,768]{2,1,0:T(8,128)S(1)} collective-permute-done((f32[1,48,768]{2,1,0:T(8,128)S(1)}, f32[1,48,768]{2,1,0:T(8,128)S(1)}, u32[]{:S(2)}, u32[]{:S(2)}) %collective-permute-start.54) | collective-permute-done | bytes 147488 | tf_op jit(solution)/shard_map/ppermute | solution.py:64
  490.4 4.5 all-to-all-start.6
  497.8 23.9 %newton.2.map_ref = bf16[1,4,192,192]{3,2,1,0:T(8,128)(2,1)S(1)} custom-call(s32[3]{0:T(128)S(1)} %pad_add_fusion.where_ref, f32[4,1,24,768]{3,2,1,0:T(8,128)S(1)} %constant_dynamic-slice_fusion.1.refs_0_, f32[4,1,24,768]{3,2,1,0:T(8,128)S(1)} %copy-done.56, f32[4,1,24,768]{3,2,1,0:T(8,128)S(1)} %copy-done.58, f32[4,1,24,768]{3,2,1,0:T(8,128)S(1)} %copy-done.60, ...), custom_call_target="tpu_custom_call" | custom-call | flops 22649241600 | tf_op jit(solution)/shard_map/newton/pallas_call | solution.py:973
  523.9 24.0 %newton.3 = bf16[1,4,192,192]{3,2,1,0:T(8,128)(2,1)S(1)} custom-call(s32[3]{0:T(128)S(1)} %pad_add_fusion.where_ref, f32[4,1,48,768]{3,2,1,0:T(8,128)S(1)} %constant_dynamic-slice_fusion.refs_0_, f32[4,1,48,768]{3,2,1,0:T(8,128)} %collective-permute-done.56.refs_1_, f32[4,1,48,768]{3,2,1,0:T(8,128)} %collective-permute-done.57.refs_2_, ...), custom_call_target="tpu_custom_call" | custom-call | flops 22649241600 | tf_op jit(solution)/shard_map/newton/pallas_call | solution.py:973
  557.5 3.2 multiply_subtract_fusion
  (503 shorter events, 173.5 us)
Async XLA Ops:
  9.6 30.0 %collective-permute-start.3 = (bf16[192,1728]{1,0:T(8,128)(2,1)}, bf16[192,1728]{1,0:T(8,128)(2,1)}, u32[]{:S(2)}, u32[]{:S(2)}) collective-permute-start(bf16[192,1728]{1,0:T(8,128)(2,1)} %bitcast_convert_fusion.2), channel_id=1, source_target_pairs={{0,4},{4,8},{8,12},{1,5},{5,9},{9,13},{2,6},{6,10},{10,14},{3,7},{... | collective-permute-start | bytes 1990664 | tf_op jit(solution)/shard_map/ppermute | solution.py:121
  15.6 25.6 %collective-permute-start.6 = (bf16[192,1728]{1,0:T(8,128)(2,1)}, bf16[192,1728]{1,0:T(8,128)(2,1)}, u32[]{:S(2)}, u32[]{:S(2)}) collective-permute-start(bf16[192,1728]{1,0:T(8,128)(2,1)} %bitcast_convert_fusion.2), channel_id=1, source_target_pairs={{4,0},{8,4},{12,8},{5,1},{9,5},{13,9},{6,2},{10,6},{14,10},{7,3},{... | collective-permute-start | bytes 1990664 | tf_op jit(solution)/shard_map/ppermute | solution.py:126
  19.6 17.6 %all-to-all-start = ((f32[8,5,384]{2,1,0:T(8,128)}), f32[8,5,384]{2,1,0:T(8,128)S(1)}, u32[]{:S(2)}, u32[]{:S(2)}) async-start(f32[8,5,384]{2,1,0:T(8,128)} %broadcast_in_dim.37), calls=%async_computation | async-start | bytes 196608 | tf_op jit(solution)/shard_map/all_to_all | solution.py:104
  25.5 102.1 %all-gather.5.cloned.1.call-start = ((), (), s32[]{:S(2)}) async-start(), calls=%async_computation.7 | async-start | bytes 3981312 | tf_op jit(solution)/shard_map/all_gather | solution.py:1380
  38.1 11.2 %collective-permute-start = (bf16[2,256,384]{1,2,0:T(8,128)(2,1)S(1)}, bf16[2,256,384]{1,2,0:T(8,128)(2,1)S(1)}, u32[]{:S(2)}, u32[]{:S(2)}) collective-permute-start(bf16[2,256,384]{1,2,0:T(8,128)(2,1)S(1)} %pad_maximum_fusion.5), channel_id=1, source_target_pairs={{0,1},{1,0},{2,3},{3,2},{4,5},{5,4},{6,7},{7,6},{8,9},{9,8},{10,11... | collective-permute-start | bytes 1179656 | tf_op jit(solution)/shard_map/ppermute | solution.py:59
  39.6 25.8 %collective-permute-start.4 = (bf16[192,1728]{1,0:T(8,128)(2,1)}, bf16[192,1728]{1,0:T(8,128)(2,1)}, u32[]{:S(2)}, u32[]{:S(2)}) collective-permute-start(bf16[192,1728]{1,0:T(8,128)(2,1)} %collective-permute-done.3), channel_id=1, source_target_pairs={{4,8},{8,12},{5,9},{9,13},{6,10},{10,14},{7,11},{11,15},{20,24},{2... | collective-permute-start | bytes 1990664 | tf_op jit(solution)/shard_map/ppermute | solution.py:121
  41.2 25.8 %collective-permute-start.7 = (bf16[192,1728]{1,0:T(8,128)(2,1)}, bf16[192,1728]{1,0:T(8,128)(2,1)}, u32[]{:S(2)}, u32[]{:S(2)}) collective-permute-start(bf16[192,1728]{1,0:T(8,128)(2,1)} %collective-permute-done.6), channel_id=1, source_target_pairs={{4,0},{8,4},{5,1},{9,5},{6,2},{10,6},{7,3},{11,7},{20,16},{24,20},... | collective-permute-start | bytes 1990664 | tf_op jit(solution)/shard_map/ppermute | solution.py:126
  45.4 25.3 %collective-permute-start.9 = (bf16[3,192,1728]{2,1,0:T(8,128)(2,1)}, bf16[3,192,1728]{2,1,0:T(8,128)(2,1)}, u32[]{:S(2)}, u32[]{:S(2)}) collective-permute-start(bf16[3,192,1728]{2,1,0:T(8,128)(2,1)} %pad_maximum_fusion.mine_ref), channel_id=1, source_target_pairs={{0,16},{16,0},{1,17},{17,1},{2,18},{18,2},{3,19},{19,3},{4,20},{20... | collective-permute-start | bytes 5971976 | tf_op jit(solution)/shard_map/ppermute | solution.py:59
  45.4 20.1 %collective-permute-start.1 = (bf16[2,256,384]{1,2,0:T(8,128)(2,1)S(1)}, bf16[2,256,384]{1,2,0:T(8,128)(2,1)}, u32[]{:S(2)}, u32[]{:S(2)}) collective-permute-start(bf16[2,256,384]{1,2,0:T(8,128)(2,1)S(1)} %pad_maximum_fusion.5), channel_id=1, source_target_pairs={{0,2},{1,3},{2,0},{3,1},{4,6},{5,7},{6,4},{7,5},{8,10},{9,11},{10,... | collective-permute-start | bytes 1179656 | tf_op jit(solution)/shard_map/ppermute | solution.py:59
  49.3 16.2 %collective-permute-start.2 = (bf16[2,256,384]{1,2,0:T(8,128)(2,1)S(1)}, bf16[2,256,384]{1,2,0:T(8,128)(2,1)}, u32[]{:S(2)}, u32[]{:S(2)}) collective-permute-start(bf16[2,256,384]{1,2,0:T(8,128)(2,1)S(1)} %pad_maximum_fusion.5), channel_id=1, source_target_pairs={{0,3},{1,2},{2,1},{3,0},{4,7},{5,6},{6,5},{7,4},{8,11},{9,10},{10,... | collective-permute-start | bytes 1179656 | tf_op jit(solution)/shard_map/ppermute | solution.py:59
  65.5 16.1 %collective-permute-start.5 = (bf16[192,1728]{1,0:T(8,128)(2,1)}, bf16[192,1728]{1,0:T(8,128)(2,1)}, u32[]{:S(2)}, u32[]{:S(2)}) collective-permute-start(bf16[192,1728]{1,0:T(8,128)(2,1)} %collective-permute-done.4), channel_id=1, source_target_pairs={{8,12},{9,13},{10,14},{11,15},{24,28},{25,29},{26,30},{27,31}} | collective-permute-start | bytes 1990664 | tf_op jit(solution)/shard_map/ppermute | solution.py:121
  68.3 20.3 %collective-permute-start.10 = (bf16[192,1728]{1,0:T(8,128)(2,1)}, bf16[192,1728]{1,0:T(8,128)(2,1)}, u32[]{:S(2)}, u32[]{:S(2)}) collective-permute-start(bf16[192,1728]{1,0:T(8,128)(2,1)} %collective-permute-done.7), channel_id=1, source_target_pairs={{4,0},{5,1},{6,2},{7,3},{20,16},{21,17},{22,18},{23,19}} | collective-permute-start | bytes 1990664 | tf_op jit(solution)/shard_map/ppermute | solution.py:126
  88.6 228.7 %all-gather.7.cloned.1.call-start = ((), (), s32[]{:S(2)}) async-start(), calls=%async_computation.8 | async-start | bytes 7077888 | tf_op jit(solution)/shard_map/all_gather | solution.py:1401
  155.0 10.6 %all-to-all-start.1 = ((f32[8,4,192]{2,1,0:T(4,128)}), f32[8,4,192]{2,1,0:T(4,128)S(1)}, u32[]{:S(2)}, u32[]{:S(2)}) async-start(f32[8,4,192]{2,1,0:T(4,128)} %broadcast_in_dim.42), calls=%async_computation.1 | async-start | bytes 65536 | tf_op jit(solution)/shard_map/all_to_all | solution.py:104
  166.7 14.8 %collective-permute-start.12 = (bf16[8,8,16,192]{3,2,1,0:T(8,128)(2,1)S(1)}, bf16[8,8,16,192]{3,2,1,0:T(8,128)(2,1)S(1)}, u32[]{:S(2)}, u32[]{:S(2)}) collective-permute-start(bf16[8,8,16,192]{3,2,1,0:T(8,128)(2,1)S(1)} %multiply_convert_fusion.1.refs_0_), channel_id=1, source_target_pairs={{0,1},{1,0},{2,3},{3,2},{4,5},{5,4},{6,7},{7,6},{8,9},{9,8},{10,11... | collective-permute-start | bytes 1179656 | tf_op jit(solution)/shard_map/ppermute | solution.py:59
  168.3 25.0 %collective-permute-start.13 = (bf16[8,8,16,192]{3,2,1,0:T(8,128)(2,1)S(1)}, bf16[8,8,16,192]{3,2,1,0:T(8,128)(2,1)S(1)}, u32[]{:S(2)}, u32[]{:S(2)}) collective-permute-start(bf16[8,8,16,192]{3,2,1,0:T(8,128)(2,1)S(1)} %multiply_convert_fusion.1.refs_0_), channel_id=1, source_target_pairs={{0,2},{1,3},{2,0},{3,1},{4,6},{5,7},{6,4},{7,5},{8,10},{9,11},{10,... | collective-permute-start | bytes 1179656 | tf_op jit(solution)/shard_map/ppermute | solution.py:59
  169.8 23.6 %collective-permute-start.14 = (bf16[8,8,16,192]{3,2,1,0:T(8,128)(2,1)S(1)}, bf16[8,8,16,192]{3,2,1,0:T(8,128)(2,1)S(1)}, u32[]{:S(2)}, u32[]{:S(2)}) collective-permute-start(bf16[8,8,16,192]{3,2,1,0:T(8,128)(2,1)S(1)} %multiply_convert_fusion.1.refs_0_), channel_id=1, source_target_pairs={{0,3},{1,2},{2,1},{3,0},{4,7},{5,6},{6,5},{7,4},{8,11},{9,10},{10,... | collective-permute-start | bytes 1179656 | tf_op jit(solution)/shard_map/ppermute | solution.py:59
  236.5 18.6 %collective-permute-start.20 = (bf16[1024,192]{1,0:T(8,128)(2,1)}, bf16[1024,192]{1,0:T(8,128)(2,1)}, u32[]{:S(2)}, u32[]{:S(2)}) collective-permute-start(bf16[1024,192]{1,0:T(8,128)(2,1)} %get-tuple-element.116), channel_id=1, source_target_pairs={{0,3},{1,2},{2,1},{3,0},{4,7},{5,6},{6,5},{7,4},{8,11},{9,10},{10,... | collective-permute-start | bytes 1179656 | tf_op jit(solution)/shard_map/ppermute | solution.py:59
  238.9 22.1 %collective-permute-start.19 = (bf16[1024,192]{1,0:T(8,128)(2,1)}, bf16[1024,192]{1,0:T(8,128)(2,1)S(1)}, u32[]{:S(2)}, u32[]{:S(2)}) collective-permute-start(bf16[1024,192]{1,0:T(8,128)(2,1)} %copy-done.54), channel_id=1, source_target_pairs={{0,2},{1,3},{2,0},{3,1},{4,6},{5,7},{6,4},{7,5},{8,10},{9,11},{10,... | collective-permute-start | bytes 1179656 | tf_op jit(solution)/shard_map/ppermute | solution.py:59
  240.0 21.2 %collective-permute-start.18 = (bf16[1024,192]{1,0:T(8,128)(2,1)}, bf16[1024,192]{1,0:T(8,128)(2,1)S(1)}, u32[]{:S(2)}, u32[]{:S(2)}) collective-permute-start(bf16[1024,192]{1,0:T(8,128)(2,1)} %copy-done.53), channel_id=1, source_target_pairs={{0,1},{1,0},{2,3},{3,2},{4,5},{5,4},{6,7},{7,6},{8,9},{9,8},{10,11... | collective-permute-start | bytes 1179656 | tf_op jit(solution)/shard_map/ppermute | solution.py:59
  255.0 24.9 %collective-permute-start.24 = (bf16[4,528,384]{2,1,0:T(8,128)(2,1)}, bf16[4,528,384]{2,1,0:T(8,128)(2,1)}, u32[]{:S(2)}, u32[]{:S(2)}) collective-permute-start(bf16[4,528,384]{2,1,0:T(8,128)(2,1)} %dynamic-slice_bitcast_fusion), channel_id=1, source_target_pairs={{0,16},{16,0},{1,17},{17,1},{2,18},{18,2},{3,19},{19,3},{4,20},{20... | collective-permute-start | bytes 4866056 | tf_op jit(solution)/shard_map/ppermute | solution.py:59
  264.0 9.0 %all-to-all-start.2 = ((f32[8,4,192]{2,1,0:T(4,128)}), f32[8,4,192]{2,1,0:T(4,128)S(1)}, u32[]{:S(2)}, u32[]{:S(2)}) async-start(f32[8,4,192]{2,1,0:T(4,128)} %broadcast_in_dim.46), calls=%async_computation.2 | async-start | bytes 65536 | tf_op jit(solution)/shard_map/all_to_all | solution.py:104
  274.1 17.0 %collective-permute-start.21 = (bf16[8,8,16,192]{3,2,1,0:T(8,128)(2,1)}, bf16[8,8,16,192]{3,2,1,0:T(8,128)(2,1)}, u32[]{:S(2)}, u32[]{:S(2)}) collective-permute-start(bf16[8,8,16,192]{3,2,1,0:T(8,128)(2,1)} %multiply_convert_fusion.refs_0_.g_ref), channel_id=1, source_target_pairs={{0,4},{4,8},{8,12},{12,0},{1,5},{5,9},{9,13},{13,1},{2,6},{6,10},{... | collective-permute-start | bytes 1179656 | tf_op jit(solution)/shard_map/ppermute | solution.py:64
  274.6 38.2 %collective-permute-start.22 = (bf16[8,8,16,192]{3,2,1,0:T(8,128)(2,1)}, bf16[8,8,16,192]{3,2,1,0:T(8,128)(2,1)}, u32[]{:S(2)}, u32[]{:S(2)}) collective-permute-start(bf16[8,8,16,192]{3,2,1,0:T(8,128)(2,1)} %multiply_convert_fusion.refs_0_.g_ref), channel_id=1, source_target_pairs={{0,8},{4,12},{8,0},{12,4},{1,9},{5,13},{9,1},{13,5},{2,10},{6,14},... | collective-permute-start | bytes 1179656 | tf_op jit(solution)/shard_map/ppermute | solution.py:64
  275.2 37.6 %collective-permute-start.23 = (bf16[8,8,16,192]{3,2,1,0:T(8,128)(2,1)}, bf16[8,8,16,192]{3,2,1,0:T(8,128)(2,1)}, u32[]{:S(2)}, u32[]{:S(2)}) collective-permute-start(bf16[8,8,16,192]{3,2,1,0:T(8,128)(2,1)} %multiply_convert_fusion.refs_0_.g_ref), channel_id=1, source_target_pairs={{0,12},{4,0},{8,4},{12,8},{1,13},{5,1},{9,5},{13,9},{2,14},{6,2},{... | collective-permute-start | bytes 1179656 | tf_op jit(solution)/shard_map/ppermute | solution.py:64
  329.0 20.9 %collective-permute-start.32 = (bf16[528,384]{1,0:T(8,128)(2,1)S(1)}, bf16[528,384]{1,0:T(8,128)(2,1)S(1)}, u32[]{:S(2)}, u32[]{:S(2)}) collective-permute-start(bf16[528,384]{1,0:T(8,128)(2,1)S(1)} %get-tuple-element.315), channel_id=1, source_target_pairs={{0,4},{4,8},{8,12},{12,0},{1,5},{5,9},{9,13},{13,1},{2,6},{6,10},{... | collective-permute-start | bytes 1216520 | tf_op jit(solution)/shard_map/ppermute | solution.py:64
  340.1 28.9 %collective-permute-start.29 = (bf16[192,1728]{1,0:T(8,128)(2,1)S(1)}, bf16[192,1728]{1,0:T(8,128)(2,1)S(1)}, u32[]{:S(2)}, u32[]{:S(2)}) collective-permute-start(bf16[192,1728]{1,0:T(8,128)(2,1)S(1)} %get-tuple-element.148.refs_0_), channel_id=1, source_target_pairs={{0,1},{1,0},{2,3},{3,2},{4,5},{5,4},{6,7},{7,6},{8,9},{9,8},{10,11... | collective-permute-start | bytes 1990664 | tf_op jit(solution)/shard_map/ppermute | solution.py:59
  341.3 31.7 %collective-permute-start.30 = (bf16[192,1728]{1,0:T(8,128)(2,1)S(1)}, bf16[192,1728]{1,0:T(8,128)(2,1)S(1)}, u32[]{:S(2)}, u32[]{:S(2)}) collective-permute-start(bf16[192,1728]{1,0:T(8,128)(2,1)S(1)} %get-tuple-element.148.refs_0_), channel_id=1, source_target_pairs={{0,2},{1,3},{2,0},{3,1},{4,6},{5,7},{6,4},{7,5},{8,10},{9,11},{10,... | collective-permute-start | bytes 1990664 | tf_op jit(solution)/shard_map/ppermute | solution.py:59
  342.0 31.0 %collective-permute-start.31 = (bf16[192,1728]{1,0:T(8,128)(2,1)S(1)}, bf16[192,1728]{1,0:T(8,128)(2,1)S(1)}, u32[]{:S(2)}, u32[]{:S(2)}) collective-permute-start(bf16[192,1728]{1,0:T(8,128)(2,1)S(1)} %get-tuple-element.148.refs_0_), channel_id=1, source_target_pairs={{0,3},{1,2},{2,1},{3,0},{4,7},{5,6},{6,5},{7,4},{8,11},{9,10},{10,... | collective-permute-start | bytes 1990664 | tf_op jit(solution)/shard_map/ppermute | solution.py:59
  343.6 23.3 %collective-permute-start.33 = (bf16[528,384]{1,0:T(8,128)(2,1)S(1)}, bf16[528,384]{1,0:T(8,128)(2,1)S(1)}, u32[]{:S(2)}, u32[]{:S(2)}) collective-permute-start(bf16[528,384]{1,0:T(8,128)(2,1)S(1)} %get-tuple-element.314), channel_id=1, source_target_pairs={{0,8},{4,12},{8,0},{12,4},{1,9},{5,13},{9,1},{13,5},{2,10},{6,14},... | collective-permute-start | bytes 1216520 | tf_op jit(solution)/shard_map/ppermute | solution.py:64
  349.9 19.0 %collective-permute-start.34 = (bf16[528,384]{1,0:T(8,128)(2,1)S(1)}, bf16[528,384]{1,0:T(8,128)(2,1)S(1)}, u32[]{:S(2)}, u32[]{:S(2)}) collective-permute-start(bf16[528,384]{1,0:T(8,128)(2,1)S(1)} %get-tuple-element.313), channel_id=1, source_target_pairs={{0,12},{4,0},{8,4},{12,8},{1,13},{5,1},{9,5},{13,9},{2,14},{6,2},{... | collective-permute-start | bytes 1216520 | tf_op jit(solution)/shard_map/ppermute | solution.py:64
  392.9 9.9 %collective-permute-start.39 = (f32[1,24,768]{2,1,0:T(8,128)S(1)}, f32[1,24,768]{2,1,0:T(8,128)S(1)}, u32[]{:S(2)}, u32[]{:S(2)}) collective-permute-start(f32[1,24,768]{2,1,0:T(8,128)S(1)} %get-tuple-element.303), channel_id=1, source_target_pairs={{0,12},{4,0},{8,4},{12,8},{1,13},{5,1},{9,5},{13,9},{2,14},{6,2},{... | collective-permute-start | bytes 221192 | tf_op jit(solution)/shard_map/ppermute | solution.py:64
  395.9 40.2 %all-to-all-start.5 = ((bf16[4,192,1056]{2,1,0:T(8,128)(2,1)}), bf16[4,192,1056]{2,1,0:T(8,128)(2,1)}, u32[]{:S(2)}, u32[]{:S(2)}) async-start(bf16[4,192,1056]{2,1,0:T(8,128)(2,1)} %broadcast_in_dim.99), calls=%async_computation.5 | async-start | bytes 3538944 | tf_op jit(solution)/shard_map/all_to_all | solution.py:104
  407.9 21.5 %collective-permute-start.42 = (f32[4,1,24,768]{3,2,1,0:T(8,128)S(1)}, f32[4,1,24,768]{3,2,1,0:T(8,128)S(1)}, u32[]{:S(2)}, u32[]{:S(2)}) collective-permute-start(f32[4,1,24,768]{3,2,1,0:T(8,128)S(1)} %constant_dynamic-slice_fusion.1.refs_0_), channel_id=1, source_target_pairs={{0,1},{1,0},{2,3},{3,2},{4,5},{5,4},{6,7},{7,6},{8,9},{9,8},{10,11... | collective-permute-start | bytes 884744 | tf_op jit(solution)/shard_map/ppermute | solution.py:59
  409.6 19.9 %collective-permute-start.43 = (f32[4,1,24,768]{3,2,1,0:T(8,128)S(1)}, f32[4,1,24,768]{3,2,1,0:T(8,128)S(1)}, u32[]{:S(2)}, u32[]{:S(2)}) collective-permute-start(f32[4,1,24,768]{3,2,1,0:T(8,128)S(1)} %constant_dynamic-slice_fusion.1.refs_0_), channel_id=1, source_target_pairs={{0,2},{1,3},{2,0},{3,1},{4,6},{5,7},{6,4},{7,5},{8,10},{9,11},{10,... | collective-permute-start | bytes 884744 | tf_op jit(solution)/shard_map/ppermute | solution.py:59
  411.1 23.6 %collective-permute-start.44 = (f32[4,1,24,768]{3,2,1,0:T(8,128)S(1)}, f32[4,1,24,768]{3,2,1,0:T(8,128)S(1)}, u32[]{:S(2)}, u32[]{:S(2)}) collective-permute-start(f32[4,1,24,768]{3,2,1,0:T(8,128)S(1)} %constant_dynamic-slice_fusion.1.refs_0_), channel_id=1, source_target_pairs={{0,3},{1,2},{2,1},{3,0},{4,7},{5,6},{6,5},{7,4},{8,11},{9,10},{10,... | collective-permute-start | bytes 884744 | tf_op jit(solution)/shard_map/ppermute | solution.py:59
  436.1 13.7 %all-to-all-start.3 = ((bf16[4,256,384]{2,1,0:T(8,128)(2,1)}), bf16[4,256,384]{2,1,0:T(8,128)(2,1)}, u32[]{:S(2)}, u32[]{:S(2)}) async-start(bf16[4,256,384]{2,1,0:T(8,128)(2,1)} %pad_maximum_fusion.4), calls=%async_computation.3 | async-start | bytes 1572864 | tf_op jit(solution)/shard_map/all_to_all | solution.py:1490
  444.8 9.2 %collective-permute-start.45 = (f32[4,1,24,768]{3,2,1,0:T(8,128)S(1)}, f32[4,1,24,768]{3,2,1,0:T(8,128)}, u32[]{:S(2)}, u32[]{:S(2)}) collective-permute-start(f32[4,1,24,768]{3,2,1,0:T(8,128)S(1)} %constant_dynamic-slice_fusion.1.refs_0_), channel_id=1, source_target_pairs={{0,16},{16,0},{1,17},{17,1},{2,18},{18,2},{3,19},{19,3},{4,20},{20... | collective-permute-start | bytes 884744 | tf_op jit(solution)/shard_map/ppermute | solution.py:59
  445.3 8.7 %collective-permute-start.46 = (f32[4,1,24,768]{3,2,1,0:T(8,128)S(1)}, f32[4,1,24,768]{3,2,1,0:T(8,128)}, u32[]{:S(2)}, u32[]{:S(2)}) collective-permute-start(f32[4,1,24,768]{3,2,1,0:T(8,128)S(1)} %collective-permute-done.42.refs_1_), channel_id=1, source_target_pairs={{0,16},{16,0},{1,17},{17,1},{2,18},{18,2},{3,19},{19,3},{4,20},{20... | collective-permute-start | bytes 884744 | tf_op jit(solution)/shard_map/ppermute | solution.py:59
  454.0 13.7 %collective-permute-start.52 = (f32[1,48,768]{2,1,0:T(8,128)S(1)}, f32[1,48,768]{2,1,0:T(8,128)S(1)}, u32[]{:S(2)}, u32[]{:S(2)}) collective-permute-start(f32[1,48,768]{2,1,0:T(8,128)S(1)} %get-tuple-element.327), channel_id=1, source_target_pairs={{0,12},{4,0},{8,4},{12,8},{1,13},{5,1},{9,5},{13,9},{2,14},{6,2},{... | collective-permute-start | bytes 442376 | tf_op jit(solution)/shard_map/ppermute | solution.py:64
  456.8 13.2 %collective-permute-start.51 = (f32[1,48,768]{2,1,0:T(8,128)S(1)}, f32[1,48,768]{2,1,0:T(8,128)}, u32[]{:S(2)}, u32[]{:S(2)}) collective-permute-start(f32[1,48,768]{2,1,0:T(8,128)S(1)} %get-tuple-element.328), channel_id=1, source_target_pairs={{0,8},{4,12},{8,0},{12,4},{1,9},{5,13},{9,1},{13,5},{2,10},{6,14},... | collective-permute-start | bytes 442376 | tf_op jit(solution)/shard_map/ppermute | solution.py:64
  457.6 12.3 %collective-permute-start.50 = (f32[1,48,768]{2,1,0:T(8,128)S(1)}, f32[1,48,768]{2,1,0:T(8,128)}, u32[]{:S(2)}, u32[]{:S(2)}) collective-permute-start(f32[1,48,768]{2,1,0:T(8,128)S(1)} %get-tuple-element.326), channel_id=1, source_target_pairs={{0,4},{4,8},{8,12},{12,0},{1,5},{5,9},{9,13},{13,1},{2,6},{6,10},{... | collective-permute-start | bytes 442376 | tf_op jit(solution)/shard_map/ppermute | solution.py:64
  472.3 13.0 %collective-permute-start.54 = (f32[1,48,768]{2,1,0:T(8,128)S(1)}, f32[1,48,768]{2,1,0:T(8,128)S(1)}, u32[]{:S(2)}, u32[]{:S(2)}) collective-permute-start(f32[1,48,768]{2,1,0:T(8,128)S(1)} %get-tuple-element.301), channel_id=1, source_target_pairs={{0,8},{4,12},{8,0},{12,4},{1,9},{5,13},{9,1},{13,5},{2,10},{6,14},... | collective-permute-start | bytes 442376 | tf_op jit(solution)/shard_map/ppermute | solution.py:64
  472.6 12.7 %collective-permute-start.55 = (f32[1,48,768]{2,1,0:T(8,128)S(1)}, f32[1,48,768]{2,1,0:T(8,128)S(1)}, u32[]{:S(2)}, u32[]{:S(2)}) collective-permute-start(f32[1,48,768]{2,1,0:T(8,128)S(1)} %get-tuple-element.301), channel_id=1, source_target_pairs={{0,4},{4,8},{8,12},{12,0},{1,5},{5,9},{9,13},{13,1},{2,6},{6,10},{... | collective-permute-start | bytes 442376 | tf_op jit(solution)/shard_map/ppermute | solution.py:64
  485.5 38.3 %collective-permute-start.56 = (f32[4,1,48,768]{3,2,1,0:T(8,128)S(1)}, f32[4,1,48,768]{3,2,1,0:T(8,128)}, u32[]{:S(2)}, u32[]{:S(2)}) collective-permute-start(f32[4,1,48,768]{3,2,1,0:T(8,128)S(1)} %constant_dynamic-slice_fusion.refs_0_), channel_id=1, source_target_pairs={{0,1},{1,0},{2,3},{3,2},{4,5},{5,4},{6,7},{7,6},{8,9},{9,8},{10,11... | collective-permute-start | bytes 1769480 | tf_op jit(solution)/shard_map/ppermute | solution.py:59
  486.0 37.9 %collective-permute-start.57 = (f32[4,1,48,768]{3,2,1,0:T(8,128)S(1)}, f32[4,1,48,768]{3,2,1,0:T(8,128)}, u32[]{:S(2)}, u32[]{:S(2)}) collective-permute-start(f32[4,1,48,768]{3,2,1,0:T(8,128)S(1)} %constant_dynamic-slice_fusion.refs_0_), channel_id=1, source_target_pairs={{0,2},{1,3},{2,0},{3,1},{4,6},{5,7},{6,4},{7,5},{8,10},{9,11},{10,... | collective-permute-start | bytes 1769480 | tf_op jit(solution)/shard_map/ppermute | solution.py:59
  487.0 36.8 %collective-permute-start.58 = (f32[4,1,48,768]{3,2,1,0:T(8,128)S(1)}, f32[4,1,48,768]{3,2,1,0:T(8,128)}, u32[]{:S(2)}, u32[]{:S(2)}) collective-permute-start(f32[4,1,48,768]{3,2,1,0:T(8,128)S(1)} %constant_dynamic-slice_fusion.refs_0_), channel_id=1, source_target_pairs={{0,3},{1,2},{2,1},{3,0},{4,7},{5,6},{6,5},{7,4},{8,11},{9,10},{10,... | collective-permute-start | bytes 1769480 | tf_op jit(solution)/shard_map/ppermute | solution.py:59
  490.4 63.2 %all-to-all-start.6 = ((f32[8,32,1536]{2,1,0:T(8,128)}), f32[8,32,1536]{2,1,0:T(8,128)}, u32[]{:S(2)}, u32[]{:S(2)}) async-start(f32[8,32,1536]{2,1,0:T(8,128)} %broadcast_in_dim.100), calls=%async_computation.6 | async-start | bytes 3145728 | tf_op jit(solution)/shard_map/all_to_all | solution.py:104
  (141 other events, 1596.0 us)
Sparse Core Ops, SparseCore 0:
  88.7 38.7 all-gather.4
  138.2 64.3 all-gather.6
